TPU v7x, 32 devices: a whole 2x2x4 slice. The times are simulated.
32 devices in a mesh: grp: 2 (over y), gy: 4 (over z), gz: 2 (over x), wa: 2 (over core).
Axes of the slice: x: 2, y: 2, z: 4, core: 2. Of those that a mesh axis runs over, the one named last changes fastest.
Arguments:
- start: float32 [2, 96, 96, 256], P('grp', 'gy', 'gz', 'wa'), may hold values from 0 to 1
- rates: float32 [8, 2, 96, 96, 256], P(None, 'grp', 'gy', 'gz', 'wa'), may hold values from 0.05 to 1
- labels: int32 [2, 96, 96, 256], P('grp', 'gy', 'gz', 'wa'), may hold values from 0 to 2, as said below
- cotangent: float32 [2, 96, 96, 256], P('grp', 'gy', 'gz', 'wa'), may hold values from -24 to 24
Outputs:
- committor: float32 [2, 96, 96, 256], P('grp', 'gy', 'gz', 'wa')
- grad_start: float32 [2, 96, 96, 256], P('grp', 'gy', 'gz', 'wa')
- grad_rates: float32 [8, 2, 96, 96, 256], P(None, 'grp', 'gy', 'gz', 'wa')
Inputs may be any that keep to these rules, and one draw needn't show every extreme that they name: `labels`: 0 marks an interior cell, 1 a reactant milestone cell, 2 a product milestone cell.
All inputs are finite; a program needn't handle non-finite values.
Results may differ from a plain program's by a relative error of at most 0.00002.
Values sent between devices are 32-bit elements; how exact they have to be, the bound alone decides.
No kernel may reach another device: no remote copies, remote signals or barrier semaphores. Data moves between devices by JAX's collectives and lax.ppermute only.
A program may use at most 192 MiB of HBM per device.

v0:
```python
import jax
import jax.numpy as jnp
from jax import lax
from jax.sharding import PartitionSpec as P


def extended(x, sides, width):
    for axis, dim in sides:
        size, length = (lax.axis_size(axis), x.shape[dim])
        up = [(i, (i + 1) % size) for i in range(size)]
        down = [(j, i) for i, j in up]
        last = lax.slice_in_dim(x, length - width, length, axis=dim)
        leading = lax.slice_in_dim(x, 0, width, axis=dim)
        before = lax.ppermute(last, axis, up)
        after = lax.ppermute(leading, axis, down)
        x = jnp.concatenate([before, x, after], axis=dim)
    return x


def passed_along(block, axis, distance):
    devices = range(lax.axis_size(axis))
    route = [((i - distance) % len(devices), i) for i in devices]
    return lax.ppermute(block, axis, route)


def extend(field):
    return extended(field, (("grp", 0), ("gy", 1), ("gz", 2), ("wa", 3)), 1)


def neighbour(padded, d, offset):
    sizes = padded.shape
    index = []
    for axis in range(4):
        if axis == d:
            index.append(slice(1 + offset, sizes[axis] - 1 + offset))
        else:
            index.append(slice(1, sizes[axis] - 1))
    return padded[tuple(index)]


def last_layer(term, d):
    count = term.shape[d]
    return lax.slice_in_dim(term, count - 1, count, axis=d)


def first_layer(term, d):
    return lax.slice_in_dim(term, 0, 1, axis=d)


def from_below(term, came, d):
    count = term.shape[d]
    return jnp.concatenate([came, lax.slice_in_dim(term, 0, count - 1, axis=d)], axis=d)


def from_above(term, came, d):
    count = term.shape[d]
    return jnp.concatenate([lax.slice_in_dim(term, 1, count, axis=d), came], axis=d)


def forward(field, weight, interior, product):
    padded = extend(field)
    average = jnp.zeros_like(field)
    for d in range(4):
        average = average + weight[2 * d] * neighbour(padded, d, 1)
        average = average + weight[2 * d + 1] * neighbour(padded, d, -1)
    return (interior * ((1.0 - 0.8) * field + 0.8 * average) + product, average, padded)


def on_device(start, rates, labels, cotangent):
    interior = (labels == 0).astype(jnp.float32)
    product = (labels == 2).astype(jnp.float32)
    total = jnp.sum(rates, axis=0)
    weight = rates / total
    first, avg_zero, padded_zero = forward(start, weight, interior, product)
    committor, avg_one, padded_one = forward(first, weight, interior, product)
    coeff = 0.8 * interior * weight

    def adjoint(grad):
        result = (1.0 - 0.8) * interior * grad
        plus = [coeff[2 * d] * grad for d in range(4)]
        minus = [coeff[2 * d + 1] * grad for d in range(4)]
        came_plus = [
            passed_along(last_layer(plus[0], 0), "grp", 1),
            passed_along(last_layer(plus[1], 1), "gy", 1),
            passed_along(last_layer(plus[2], 2), "gz", 1),
            passed_along(last_layer(plus[3], 3), "wa", 1),
        ]
        came_minus = [
            passed_along(first_layer(minus[0], 0), "grp", -1),
            passed_along(first_layer(minus[1], 1), "gy", -1),
            passed_along(first_layer(minus[2], 2), "gz", -1),
            passed_along(first_layer(minus[3], 3), "wa", -1),
        ]
        for d in range(4):
            result = result + from_below(plus[d], came_plus[d], d)
            result = result + from_above(minus[d], came_minus[d], d)
        return result

    back = adjoint(cotangent)
    grad_start = adjoint(back)
    factor = 0.8 * interior / total
    pieces = []
    for d in range(4):
        for offset in (1, -1):
            term = cotangent * (neighbour(padded_one, d, offset) - avg_one)
            term = term + back * (neighbour(padded_zero, d, offset) - avg_zero)
            pieces.append(term * factor)
    return (committor, grad_start, jnp.stack(pieces))


def solution(mesh):
    placed = (
        P("grp", "gy", "gz", "wa"),
        P(None, "grp", "gy", "gz", "wa"),
        P("grp", "gy", "gz", "wa"),
        P("grp", "gy", "gz", "wa"),
    )
    return jax.shard_map(
        on_device,
        mesh=mesh,
        in_specs=placed,
        out_specs=(
            P("grp", "gy", "gz", "wa"),
            P("grp", "gy", "gz", "wa"),
            P(None, "grp", "gy", "gz", "wa"),
        ),
        check_vma=False,
    )
```

profile of v0, /device:TPU:0, one launch (start us, length us, event | category | flops | bytes accessed | tf_op | source)
XLA Modules:
  0.0 204.8 jit_solution(17230781331203733108)
XLA Ops:
  0.6 3.0 %collective-permute-start.1 = (f32[1,24,48,128]{3,2,1,0:T(8,128)}, f32[1,24,48,128]{3,2,1,0:T(8,128)S(1)}, u32[]{:S(2)}, u32[]{:S(2)}) collective-permute-start(f32[1,24,48,128]{3,2,1,0:T(8,128)} %param.4), channel_id=1, source_target_pairs={{0,16},{16,0},{1,17},{17,1},{2,18},{18,2},{3,19},{19,3},{4,20},{20... | collective-permute-start | bytes 1769480 | tf_op jit(solution)/shard_map/ppermute | solution.py:14
  3.7 14.3 %collective-permute-done.1 = f32[1,24,48,128]{3,2,1,0:T(8,128)S(1)} collective-permute-done((f32[1,24,48,128]{3,2,1,0:T(8,128)}, f32[1,24,48,128]{3,2,1,0:T(8,128)S(1)}, u32[]{:S(2)}, u32[]{:S(2)}) %collective-permute-start.1) | collective-permute-done | bytes 589856 | tf_op jit(solution)/shard_map/ppermute | solution.py:14
  18.1 1.3 constant_dynamic-update-slice_fusion.1
  19.4 10.5 %collective-permute-done = f32[1,24,48,128]{3,2,1,0:T(8,128)S(1)} collective-permute-done((f32[1,24,48,128]{3,2,1,0:T(8,128)}, f32[1,24,48,128]{3,2,1,0:T(8,128)S(1)}, u32[]{:S(2)}, u32[]{:S(2)}) %collective-permute-start) | collective-permute-done | bytes 589856 | tf_op jit(solution)/shard_map/ppermute | solution.py:15
  29.9 1.8 collective-permute-start.3
  31.8 2.1 %collective-permute-start.2 = (f32[3,1,48,128]{3,2,1,0:T(8,128)S(1)}, f32[3,1,48,128]{3,2,1,0:T(8,128)S(1)}, u32[]{:S(2)}, u32[]{:S(2)}) collective-permute-start(f32[3,1,48,128]{3,2,1,0:T(8,128)S(1)} %get-tuple-element.51), channel_id=1, source_target_pairs={{4,0},{8,4},{12,8},{0,12},{5,1},{9,5},{13,9},{1,13},{6,2},{10,6},{... | collective-permute-start | bytes 221192 | tf_op jit(solution)/shard_map/ppermute | solution.py:15
  33.9 2.9 %collective-permute-done.3 = f32[3,1,48,128]{3,2,1,0:T(8,128)S(1)} collective-permute-done((f32[3,1,48,128]{3,2,1,0:T(8,128)S(1)}, f32[3,1,48,128]{3,2,1,0:T(8,128)S(1)}, u32[]{:S(2)}, u32[]{:S(2)}) %collective-permute-start.3) | collective-permute-done | bytes 73760 | tf_op jit(solution)/shard_map/ppermute | solution.py:14
  37.0 1.6 collective-permute-start.5
  39.1 0.9 select_bitcast_fusion
  40.0 2.7 %reduce_sum.11 = f32[24,48,128]{2,1,0:T(8,128)S(1)} reduce(f32[8,1,24,48,128]{4,3,2,1,0:T(8,128)} %param.5, f32[]{:T(128)} %constant.11.clone.1), dimensions={0,1}, to_apply=%region_0.0 | reduce | flops 1032192 | bytes 5308420 | tf_op jit(solution)/shard_map/reduce_sum | solution.py:72
  43.0 2.8 %fusion.50 = (f32[3,26,50,1]{3,2,1,0:T(8,128)}, f32[3,26,50,1]{3,2,1,0:T(8,128)}) fusion(f32[3,26,50,128]{3,2,1,0:T(8,128)S(1)} %pad_maximum_fusion), kind=kLoop, calls=%fused_computation.137 | loop fusion | bytes 62400 | tf_op jit(solution)/shard_map/slice | solution.py:12
  45.8 2.5 %copy.67 = f32[3,26,50,1]{2,3,1,0:T(1,128)S(1)} copy(f32[3,26,50,1]{3,2,1,0:T(8,128)} %get-tuple-element.42) | data formatting | bytes 31200
  48.3 2.4 %copy.66 = f32[3,26,50,1]{2,3,1,0:T(1,128)S(1)} copy(f32[3,26,50,1]{3,2,1,0:T(8,128)} %get-tuple-element.43) | data formatting | bytes 31200
  51.3 7.1 %broadcast_multiply_fusion = (f32[8,1,24,48,128]{4,3,2,1,0:T(8,128)}, f32[8,1,24,48,128]{4,3,2,1,0:T(8,128)}) fusion(f32[24,48,128]{2,1,0:T(8,128)S(1)} %copy-done.34, f32[8,1,24,48,128]{4,3,2,1,0:T(8,128)} %param.5, f32[24,48,128]{2,1,0:T(8,128)S(1)} %reduce_sum.11), kind=kLoop, calls=%fused_computation.4 | loop fusion | flops 2359296 | bytes 15335424 | tf_op jit(solution)/shard_map/mul | solution.py:76
  58.4 2.2 %copy.45 = f32[3,26,50,1]{3,2,1,0:T(8,128)} copy(f32[3,26,50,1]{2,3,1,0:T(1,128)S(1)} %collective-permute-done.7) | data formatting | bytes 31200 | tf_op jit(solution)/shard_map/ppermute | solution.py:14
  60.7 2.2 %copy.43 = f32[3,26,50,1]{3,2,1,0:T(8,128)} copy(f32[3,26,50,1]{2,3,1,0:T(1,128)S(1)} %collective-permute-done.6) | data formatting | bytes 31200 | tf_op jit(solution)/shard_map/ppermute | solution.py:15
  62.9 6.9 %convert_add_fusion.1 = (f32[1,24,48,128]{3,2,1,0:T(8,128)S(1)}, f32[1,24,48,128]{3,2,1,0:T(8,128)S(1)}, f32[1,24,48,128]{3,2,1,0:T(8,128)}, f32[1,24,48,128]{3,...) fusion(pred[1,24,48,128]{3,2,1,0:T(8,128)(4,1)S(1)} %get-tuple-, ...), kind=kLoop, calls=%fused_computation.9 | loop fusion | flops 5898240 | bytes 14119392 | tf_op jit(solution)/shard_map/add | solution.py:66
  69.7 1.6 collective-permute-start.9
  71.8 14.2 %collective-permute-done.9 = f32[1,24,48,128]{3,2,1,0:T(8,128)S(1)} collective-permute-done((f32[1,24,48,128]{3,2,1,0:T(8,128)S(1)}, f32[1,24,48,128]{3,2,1,0:T(8,128)S(1)}, u32[]{:S(2)}, u32[]{:S(2)}) %collective-permute-start.9) | collective-permute-done | bytes 589856 | tf_op jit(solution)/shard_map/ppermute | solution.py:14
  86.0 11.8 %collective-permute-done.8 = f32[1,24,48,128]{3,2,1,0:T(8,128)S(1)} collective-permute-done((f32[1,24,48,128]{3,2,1,0:T(8,128)S(1)}, f32[1,24,48,128]{3,2,1,0:T(8,128)S(1)}, u32[]{:S(2)}, u32[]{:S(2)}) %collective-permute-start.8) | collective-permute-done | bytes 589856 | tf_op jit(solution)/shard_map/ppermute | solution.py:15
  97.8 1.1 collective-permute-start.11
  98.9 2.8 %collective-permute-start.10 = (f32[3,1,48,128]{3,2,1,0:T(8,128)S(1)}, f32[3,1,48,128]{3,2,1,0:T(8,128)S(1)}, u32[]{:S(2)}, u32[]{:S(2)}) collective-permute-start(f32[3,1,48,128]{3,2,1,0:T(8,128)S(1)} %get-tuple-element.49), channel_id=1, source_target_pairs={{4,0},{8,4},{12,8},{0,12},{5,1},{9,5},{13,9},{1,13},{6,2},{10,6},{... | collective-permute-start | bytes 221192 | tf_op jit(solution)/shard_map/ppermute | solution.py:15
  101.6 2.5 %collective-permute-done.11 = f32[3,1,48,128]{3,2,1,0:T(8,128)S(1)} collective-permute-done((f32[3,1,48,128]{3,2,1,0:T(8,128)S(1)}, f32[3,1,48,128]{3,2,1,0:T(8,128)S(1)}, u32[]{:S(2)}, u32[]{:S(2)}) %collective-permute-start.11) | collective-permute-done | bytes 73760 | tf_op jit(solution)/shard_map/ppermute | solution.py:14
  104.2 1.7 collective-permute-start.12
  106.3 2.1 %fusion.31 = (f32[1,24,48,128]{3,2,1,0:T(8,128)}, f32[1,24,48,128]{3,2,1,0:T(8,128)}, f32[1,24,48,128]{3,2,1,0:T(8,128)S(1)}, f32[1,24,48,128]{3,2,1,0:T(8,128)}...) fusion(f32[1,24,48,128]{3,2,1,0:T(8,128)S(1)} %copy-done, ...), kind=kLoop, calls=%fused_computation.105 | loop fusion | flops 1179648 | bytes 10027008 | tf_op jit(solution)/shard_map/mul | solution.py:80
  108.4 1.7 collective-permute-start.16
  110.7 2.8 %fusion.49 = (f32[3,26,50,1]{3,2,1,0:T(8,128)}, f32[3,26,50,1]{3,2,1,0:T(8,128)}) fusion(f32[3,26,50,128]{3,2,1,0:T(8,128)S(1)} %pad_maximum_fusion.1), kind=kLoop, calls=%fused_computation.136 | loop fusion | bytes 62400 | tf_op jit(solution)/shard_map/slice | solution.py:12
  113.6 3.0 %copy.68 = f32[3,26,50,1]{2,3,1,0:T(1,128)} copy(f32[3,26,50,1]{3,2,1,0:T(8,128)} %get-tuple-element.41) | data formatting | bytes 31200
  116.6 1.9 copy.56
  119.0 1.5 slice.323
  120.5 1.6 collective-permute-start.20
  122.2 1.1 slice.329
  123.2 2.0 copy.54
  125.2 3.0 %copy.69 = f32[3,26,50,1]{2,3,1,0:T(1,128)} copy(f32[3,26,50,1]{3,2,1,0:T(8,128)} %get-tuple-element.40) | data formatting | bytes 31200
  128.8 1.3 slice.321
  130.2 1.3 slice.317
  131.5 1.1 collective-permute-start.18
  132.6 2.8 %collective-permute-start.19 = (f32[1,1,48,128]{3,2,1,0:T(8,128)}, f32[1,1,48,128]{3,2,1,0:T(8,128)}, u32[]{:S(2)}, u32[]{:S(2)}) collective-permute-start(f32[1,1,48,128]{3,2,1,0:T(8,128)} %slice.321), channel_id=1, source_target_pairs={{4,0},{8,4},{12,8},{0,12},{5,1},{9,5},{13,9},{1,13},{6,2},{10,6},{... | collective-permute-start | bytes 73736 | tf_op jit(solution)/shard_map/ppermute | solution.py:23
  137.3 1.9 slice.320
  140.1 1.0 slice.332
  141.2 1.8 copy.57
  143.0 1.8 copy.55
  144.8 3.0 %copy.49 = f32[3,26,50,1]{3,2,1,0:T(8,128)} copy(f32[3,26,50,1]{2,3,1,0:T(1,128)} %collective-permute-done.15) | data formatting | bytes 31200 | tf_op jit(solution)/shard_map/ppermute | solution.py:14
  147.8 3.0 %copy.47 = f32[3,26,50,1]{3,2,1,0:T(8,128)} copy(f32[3,26,50,1]{2,3,1,0:T(1,128)} %collective-permute-done.14) | data formatting | bytes 31200 | tf_op jit(solution)/shard_map/ppermute | solution.py:15
  150.8 8.3 %bitcast_dynamic-update-slice_fusion.7 = (f32[8,1,24,48,128]{4,3,2,1,0:T(8,128)}, f32[1,24,48,128]{3,2,1,0:T(8,128)S(1)}, f32[1,24,48,128]{3,2,1,0:T(8,128)}, f32[1,24,48,128]{3,2,1,0:T(8,128)}, f32[1,24,48,128]{3,2,1,0:T(8,128)}) fusion(f32[1,24,48,128]{3,2,1,0:T(8,128)} %copy-done.10, f32[1,24,48,128]{3,2,1,0:T(8,128)S(1)} %get-tuple-element.16, ...), kind=kLoop, calls=%fused_computation.101 | loop fusion | flops 10174463 | bytes 16921056
  159.1 4.6 %fusion.44 = (f32[1,24,48,128]{3,2,1,0:T(8,128)}, f32[1,24,48,128]{3,2,1,0:T(8,128)}, f32[1,24,48,128]{3,2,1,0:T(8,128)}, f32[1,24,48,128]{3,2,1,0:T(8,128)}, f3...) fusion(f32[1,24,48,128]{3,2,1,0:T(8,128)S(1)} %get-tuple-elemen, ...), kind=kLoop, calls=%fused_computation.118 | loop fusion | flops 1179648 | bytes 10027008 | tf_op jit(solution)/shard_map/mul | solution.py:81
  163.7 1.9 copy.64
  166.5 1.6 collective-permute-start.28
  168.1 2.1 %slice.342 = f32[1,24,48,1]{3,2,1,0:T(8,128)} slice(f32[1,24,48,128]{3,2,1,0:T(8,128)} %get-tuple-element.25), slice={[0:1], [0:24], [0:48], [127:128]} | slice | bytes 9216 | tf_op jit(solution)/shard_map/slice | solution.py:43
  170.3 1.9 copy.62
  172.7 1.5 collective-permute-start.25
  174.7 2.5 %bitcast_dynamic-update-slice_fusion.6 = f32[8,1,24,48,128]{4,3,2,1,0:T(8,128)} fusion(f32[8,1,24,48,128]{4,3,2,1,0:T(8,128)} %get-tuple-element.6, f32[1,24,48,128]{3,2,1,0:T(8,128)S(1)} %get-tuple-element.7, f32[1,24,48,128]{3,2,1,0:T(8,128)} %copy-done.9, f32[1,24,48,128]{3,2,1,0:T(8,128)S(1)} %get-tuple-element.16, f32[1,24,48,128]{3,2,1,0:T(8,128)S(1)} %copy-done, ...), kind=kLoop, calls=%fused_computation.100 | loop fusion | flops 1179648 | bytes 4866048
  177.3 1.2 bitcast_dynamic-update-slice_fusion.5
  178.4 1.2 bitcast_dynamic-update-slice_fusion.4
  179.6 1.2 bitcast_dynamic-update-slice_fusion.3
  180.8 1.2 bitcast_dynamic-update-slice_fusion.2
  182.1 1.1 bitcast_dynamic-update-slice_fusion.1
  185.5 3.8 %collective-permute-start.27 = (f32[1,1,48,128]{3,2,1,0:T(8,128)}, f32[1,1,48,128]{3,2,1,0:T(8,128)}, u32[]{:S(2)}, u32[]{:S(2)}) collective-permute-start(f32[1,1,48,128]{3,2,1,0:T(8,128)} %slice.337), channel_id=1, source_target_pairs={{4,0},{8,4},{12,8},{0,12},{5,1},{9,5},{13,9},{1,13},{6,2},{10,6},{... | collective-permute-start | bytes 73736 | tf_op jit(solution)/shard_map/ppermute | solution.py:23
  189.3 1.2 bitcast_dynamic-update-slice_fusion
  193.1 1.0 slice.344
  194.1 1.0 copy.65
  195.1 1.1 copy.63
  196.2 4.6 %collective-permute-done.24 = f32[1,24,48,128]{3,2,1,0:T(8,128)} collective-permute-done((f32[1,24,48,128]{3,2,1,0:T(8,128)}, f32[1,24,48,128]{3,2,1,0:T(8,128)}, u32[]{:S(2)}, u32[]{:S(2)}) %collective-permute-start.24) | collective-permute-done | bytes 589856 | tf_op jit(solution)/shard_map/ppermute | solution.py:23
  200.9 4.0 %fusion.15 = (f32[1,24,48,128]{3,2,1,0:T(8,128)}, f32[1,24,48,128]{3,2,1,0:T(8,128)}) fusion(f32[1,24,48,128]{3,2,1,0:T(8,128)} %collective-permute-done.25, f32[1,24,48,128]{3,2,1,0:T(8,128)} %collective-permute-done.24, f32[1,24,48,128]{3,2,1,0:T(8,128)S(1)} %get-tuple-element.7, pred[1,24,48,128]{3,2,1,0:T(8,128)(4,1)S(1)} %copy-done.8, ...), kind=kLoop, calls=%fused_computation.29 | loop fusion | flops 3244032 | bytes 7962624 | tf_op jit(solution)/shard_map/add | solution.py:96
  (149 shorter events, 14.3 us)
Async XLA Ops:
  0.6 17.4 %collective-permute-start.1 = (f32[1,24,48,128]{3,2,1,0:T(8,128)}, f32[1,24,48,128]{3,2,1,0:T(8,128)S(1)}, u32[]{:S(2)}, u32[]{:S(2)}) collective-permute-start(f32[1,24,48,128]{3,2,1,0:T(8,128)} %param.4), channel_id=1, source_target_pairs={{0,16},{16,0},{1,17},{17,1},{2,18},{18,2},{3,19},{19,3},{4,20},{20... | collective-permute-start | bytes 1769480 | tf_op jit(solution)/shard_map/ppermute | solution.py:14
  3.7 26.2 %collective-permute-start = (f32[1,24,48,128]{3,2,1,0:T(8,128)}, f32[1,24,48,128]{3,2,1,0:T(8,128)S(1)}, u32[]{:S(2)}, u32[]{:S(2)}) collective-permute-start(f32[1,24,48,128]{3,2,1,0:T(8,128)} %param.4), channel_id=1, source_target_pairs={{16,0},{0,16},{17,1},{1,17},{18,2},{2,18},{19,3},{3,19},{20,4},{4,... | collective-permute-start | bytes 1769480 | tf_op jit(solution)/shard_map/ppermute | solution.py:15
  18.0 44.8 %copy-start.9 = (f32[1,24,48,128]{3,2,1,0:T(8,128)}, f32[1,24,48,128]{3,2,1,0:T(8,128)S(1)}, u32[]{:S(2)}) copy-start(f32[1,24,48,128]{3,2,1,0:T(8,128)S(1)} %collective-permute-done.1) | copy-start | bytes 1769476
  18.1 21.0 %copy-start.31 = (s32[1,24,48,128]{3,2,1,0:T(8,128)S(1)}, s32[1,24,48,128]{3,2,1,0:T(8,128)}, u32[]{:S(2)}) copy-start(s32[1,24,48,128]{3,2,1,0:T(8,128)} %param.6) | copy-start | bytes 1769476
  29.8 9.2 %copy-start.10 = (f32[1,24,48,128]{3,2,1,0:T(8,128)}, f32[1,24,48,128]{3,2,1,0:T(8,128)S(1)}, u32[]{:S(2)}) copy-start(f32[1,24,48,128]{3,2,1,0:T(8,128)S(1)} %collective-permute-done) | copy-start | bytes 1769476
  29.9 12.8 %copy-start.5 = (f32[3,24,48,128]{3,2,1,0:T(8,128)}, f32[3,24,48,128]{3,2,1,0:T(8,128)S(1)}, u32[]{:S(2)}) copy-start(f32[3,24,48,128]{3,2,1,0:T(8,128)S(1)} %constant_dynamic-update-slice_fusion) | copy-start | bytes 5308420
  29.9 6.9 %collective-permute-start.3 = (f32[3,1,48,128]{3,2,1,0:T(8,128)S(1)}, f32[3,1,48,128]{3,2,1,0:T(8,128)S(1)}, u32[]{:S(2)}, u32[]{:S(2)}) collective-permute-start(f32[3,1,48,128]{3,2,1,0:T(8,128)S(1)} %get-tuple-element.50), channel_id=1, source_target_pairs={{0,4},{4,8},{8,12},{12,0},{1,5},{5,9},{9,13},{13,1},{2,6},{6,10},{... | collective-permute-start | bytes 221192 | tf_op jit(solution)/shard_map/ppermute | solution.py:14
  31.8 5.1 %collective-permute-start.2 = (f32[3,1,48,128]{3,2,1,0:T(8,128)S(1)}, f32[3,1,48,128]{3,2,1,0:T(8,128)S(1)}, u32[]{:S(2)}, u32[]{:S(2)}) collective-permute-start(f32[3,1,48,128]{3,2,1,0:T(8,128)S(1)} %get-tuple-element.51), channel_id=1, source_target_pairs={{4,0},{8,4},{12,8},{0,12},{5,1},{9,5},{13,9},{1,13},{6,2},{10,6},{... | collective-permute-start | bytes 221192 | tf_op jit(solution)/shard_map/ppermute | solution.py:15
  37.0 5.7 %collective-permute-start.5 = (f32[3,26,1,128]{3,2,1,0:T(1,128)S(1)}, f32[3,26,1,128]{3,2,1,0:T(1,128)S(1)}, u32[]{:S(2)}, u32[]{:S(2)}) collective-permute-start(f32[3,26,1,128]{3,2,1,0:T(1,128)S(1)} %get-tuple-element.46), channel_id=1, source_target_pairs={{0,2},{2,0},{1,3},{3,1},{4,6},{6,4},{5,7},{7,5},{8,10},{10,8},{9,1... | collective-permute-start | bytes 119816 | tf_op jit(solution)/shard_map/ppermute | solution.py:14
  38.5 4.2 %collective-permute-start.4 = (f32[3,26,1,128]{3,2,1,0:T(1,128)S(1)}, f32[3,26,1,128]{3,2,1,0:T(1,128)S(1)}, u32[]{:S(2)}, u32[]{:S(2)}) collective-permute-start(f32[3,26,1,128]{3,2,1,0:T(1,128)S(1)} %get-tuple-element.47), channel_id=1, source_target_pairs={{2,0},{0,2},{3,1},{1,3},{6,4},{4,6},{7,5},{5,7},{10,8},{8,10},{11,... | collective-permute-start | bytes 119816 | tf_op jit(solution)/shard_map/ppermute | solution.py:15
  40.0 22.9 %copy-start.6 = (pred[1,24,48,128]{3,2,1,0:T(8,128)(4,1)}, pred[1,24,48,128]{3,2,1,0:T(8,128)(4,1)S(1)}, u32[]{:S(2)}) copy-start(pred[1,24,48,128]{3,2,1,0:T(8,128)(4,1)S(1)} %get-tuple-element.14) | copy-start | bytes 442372
  45.8 5.5 %copy-start.34 = (f32[24,48,128]{2,1,0:T(8,128)S(1)}, f32[24,48,128]{2,1,0:T(8,128)}, u32[]{:S(2)}) copy-start(f32[24,48,128]{2,1,0:T(8,128)} %get-tuple-element.13) | copy-start | bytes 1769476
  50.7 9.9 %collective-permute-start.6 = (f32[3,26,50,1]{2,3,1,0:T(1,128)S(1)}, f32[3,26,50,1]{2,3,1,0:T(1,128)S(1)}, u32[]{:S(2)}, u32[]{:S(2)}) collective-permute-start(f32[3,26,50,1]{2,3,1,0:T(1,128)S(1)} %copy.66), channel_id=1, source_target_pairs={{1,0},{0,1},{3,2},{2,3},{5,4},{4,5},{7,6},{6,7},{9,8},{8,9},{11,10... | collective-permute-start | bytes 46808 | tf_op jit(solution)/shard_map/ppermute | solution.py:15
  50.8 7.6 %collective-permute-start.7 = (f32[3,26,50,1]{2,3,1,0:T(1,128)S(1)}, f32[3,26,50,1]{2,3,1,0:T(1,128)S(1)}, u32[]{:S(2)}, u32[]{:S(2)}) collective-permute-start(f32[3,26,50,1]{2,3,1,0:T(1,128)S(1)} %copy.67), channel_id=1, source_target_pairs={{0,1},{1,0},{2,3},{3,2},{4,5},{5,4},{6,7},{7,6},{8,9},{9,8},{10,11... | collective-permute-start | bytes 46808 | tf_op jit(solution)/shard_map/ppermute | solution.py:14
  58.4 4.5 %copy-start.11 = (f32[1,24,48,128]{3,2,1,0:T(8,128)S(1)}, f32[1,24,48,128]{3,2,1,0:T(8,128)}, u32[]{:S(2)}) copy-start(f32[1,24,48,128]{3,2,1,0:T(8,128)} %copy-done.10) | copy-start | bytes 1769476
  62.8 43.4 %slice-start = ((s8[4718592]{0:T(1024)(128)(4,1)}), s8[4194304]{0:T(1024)(128)(4,1)S(1)}, s32[]{:S(2)}) async-start(s8[4718592]{0:T(1024)(128)(4,1)} %bitcast.162), calls=%async_computation | async-start | bytes 8388608
  62.9 43.4 %slice-start.1 = ((s8[4718592]{0:T(1024)(128)(4,1)}), s8[524288]{0:T(1024)(128)(4,1)S(1)}, s32[]{:S(2)}) async-start(s8[4718592]{0:T(1024)(128)(4,1)} %bitcast.162), calls=%async_computation.1 | async-start | bytes 1048576
  69.7 36.6 %copy-start = (f32[1,24,48,128]{3,2,1,0:T(8,128)S(1)}, f32[1,24,48,128]{3,2,1,0:T(8,128)}, u32[]{:S(2)}) copy-start(f32[1,24,48,128]{3,2,1,0:T(8,128)} %param.7) | copy-start | bytes 1769476
  69.7 16.2 %collective-permute-start.9 = (f32[1,24,48,128]{3,2,1,0:T(8,128)S(1)}, f32[1,24,48,128]{3,2,1,0:T(8,128)S(1)}, u32[]{:S(2)}, u32[]{:S(2)}) collective-permute-start(f32[1,24,48,128]{3,2,1,0:T(8,128)S(1)} %get-tuple-element.15), channel_id=1, source_target_pairs={{0,16},{16,0},{1,17},{17,1},{2,18},{18,2},{3,19},{19,3},{4,20},{20... | collective-permute-start | bytes 1769480 | tf_op jit(solution)/shard_map/ppermute | solution.py:14
  71.3 26.4 %collective-permute-start.8 = (f32[1,24,48,128]{3,2,1,0:T(8,128)S(1)}, f32[1,24,48,128]{3,2,1,0:T(8,128)S(1)}, u32[]{:S(2)}, u32[]{:S(2)}) collective-permute-start(f32[1,24,48,128]{3,2,1,0:T(8,128)S(1)} %get-tuple-element.15), channel_id=1, source_target_pairs={{16,0},{0,16},{17,1},{1,17},{18,2},{2,18},{19,3},{3,19},{20,4},{4,... | collective-permute-start | bytes 1769480 | tf_op jit(solution)/shard_map/ppermute | solution.py:15
  97.8 12.7 %copy-start.3 = (f32[1,24,48,128]{3,2,1,0:T(8,128)}, f32[1,24,48,128]{3,2,1,0:T(8,128)S(1)}, u32[]{:S(2)}) copy-start(f32[1,24,48,128]{3,2,1,0:T(8,128)S(1)} %collective-permute-done.8) | copy-start | bytes 1769476
  97.8 6.3 %collective-permute-start.11 = (f32[3,1,48,128]{3,2,1,0:T(8,128)S(1)}, f32[3,1,48,128]{3,2,1,0:T(8,128)S(1)}, u32[]{:S(2)}, u32[]{:S(2)}) collective-permute-start(f32[3,1,48,128]{3,2,1,0:T(8,128)S(1)} %get-tuple-element.48), channel_id=1, source_target_pairs={{0,4},{4,8},{8,12},{12,0},{1,5},{5,9},{9,13},{13,1},{2,6},{6,10},{... | collective-permute-start | bytes 221192 | tf_op jit(solution)/shard_map/ppermute | solution.py:14
  98.9 5.2 %collective-permute-start.10 = (f32[3,1,48,128]{3,2,1,0:T(8,128)S(1)}, f32[3,1,48,128]{3,2,1,0:T(8,128)S(1)}, u32[]{:S(2)}, u32[]{:S(2)}) collective-permute-start(f32[3,1,48,128]{3,2,1,0:T(8,128)S(1)} %get-tuple-element.49), channel_id=1, source_target_pairs={{4,0},{8,4},{12,8},{0,12},{5,1},{9,5},{13,9},{1,13},{6,2},{10,6},{... | collective-permute-start | bytes 221192 | tf_op jit(solution)/shard_map/ppermute | solution.py:15
  104.1 6.3 %copy-start.16 = (f32[3,1,48,128]{3,2,1,0:T(8,128)}, f32[3,1,48,128]{3,2,1,0:T(8,128)S(1)}, u32[]{:S(2)}) copy-start(f32[3,1,48,128]{3,2,1,0:T(8,128)S(1)} %collective-permute-done.11) | copy-start | bytes 221188
  104.1 6.3 %copy-start.18 = (f32[3,1,48,128]{3,2,1,0:T(8,128)}, f32[3,1,48,128]{3,2,1,0:T(8,128)S(1)}, u32[]{:S(2)}) copy-start(f32[3,1,48,128]{3,2,1,0:T(8,128)S(1)} %collective-permute-done.10) | copy-start | bytes 221188
  104.2 6.2 %collective-permute-start.12 = (f32[3,26,1,128]{3,2,1,0:T(1,128)S(1)}, f32[3,26,1,128]{3,2,1,0:T(1,128)S(1)}, u32[]{:S(2)}, u32[]{:S(2)}) collective-permute-start(f32[3,26,1,128]{3,2,1,0:T(1,128)S(1)} %get-tuple-element.44), channel_id=1, source_target_pairs={{2,0},{0,2},{3,1},{1,3},{6,4},{4,6},{7,5},{5,7},{10,8},{8,10},{11,... | collective-permute-start | bytes 119816 | tf_op jit(solution)/shard_map/ppermute | solution.py:15
  105.9 4.5 %collective-permute-start.13 = (f32[3,26,1,128]{3,2,1,0:T(1,128)S(1)}, f32[3,26,1,128]{3,2,1,0:T(1,128)S(1)}, u32[]{:S(2)}, u32[]{:S(2)}) collective-permute-start(f32[3,26,1,128]{3,2,1,0:T(1,128)S(1)} %get-tuple-element.45), channel_id=1, source_target_pairs={{0,2},{2,0},{1,3},{3,1},{4,6},{6,4},{5,7},{7,5},{8,10},{10,8},{9,1... | collective-permute-start | bytes 119816 | tf_op jit(solution)/shard_map/ppermute | solution.py:14
  108.4 13.8 %copy-start.12 = (f32[1,24,48,128]{3,2,1,0:T(8,128)}, f32[1,24,48,128]{3,2,1,0:T(8,128)S(1)}, u32[]{:S(2)}) copy-start(f32[1,24,48,128]{3,2,1,0:T(8,128)S(1)} %get-tuple-element.34) | copy-start | bytes 1769476
  108.4 42.4 %collective-permute-start.16 = (f32[1,24,48,128]{3,2,1,0:T(8,128)}, f32[1,24,48,128]{3,2,1,0:T(8,128)}, u32[]{:S(2)}, u32[]{:S(2)}) collective-permute-start(f32[1,24,48,128]{3,2,1,0:T(8,128)} %get-tuple-element.32), channel_id=1, source_target_pairs={{16,0},{0,16},{17,1},{1,17},{18,2},{2,18},{19,3},{3,19},{20,4},{4,... | collective-permute-start | bytes 1769480 | tf_op jit(solution)/shard_map/ppermute | solution.py:23
  110.0 40.8 %collective-permute-start.17 = (f32[1,24,48,128]{3,2,1,0:T(8,128)}, f32[1,24,48,128]{3,2,1,0:T(8,128)}, u32[]{:S(2)}, u32[]{:S(2)}) collective-permute-start(f32[1,24,48,128]{3,2,1,0:T(8,128)} %get-tuple-element.39), channel_id=1, source_target_pairs={{16,0},{0,16},{17,1},{1,17},{18,2},{2,18},{19,3},{3,19},{20,4},{4,... | collective-permute-start | bytes 1769480 | tf_op jit(solution)/shard_map/ppermute | solution.py:23
  110.4 3.2 %copy-start.38 = (f32[3,26,1,128]{3,2,1,0:T(1,128)}, f32[3,26,1,128]{3,2,1,0:T(1,128)S(1)}, u32[]{:S(2)}) copy-start(f32[3,26,1,128]{3,2,1,0:T(1,128)S(1)} %collective-permute-done.12) | copy-start | bytes 119812
  110.4 3.1 %copy-start.36 = (f32[3,26,1,128]{3,2,1,0:T(1,128)}, f32[3,26,1,128]{3,2,1,0:T(1,128)S(1)}, u32[]{:S(2)}) copy-start(f32[3,26,1,128]{3,2,1,0:T(1,128)S(1)} %collective-permute-done.13) | copy-start | bytes 119812
  116.6 16.0 %collective-permute-start.14 = (f32[3,26,50,1]{2,3,1,0:T(1,128)}, f32[3,26,50,1]{2,3,1,0:T(1,128)}, u32[]{:S(2)}, u32[]{:S(2)}) collective-permute-start(f32[3,26,50,1]{2,3,1,0:T(1,128)} %copy.68), channel_id=1, source_target_pairs={{1,0},{0,1},{3,2},{2,3},{5,4},{4,5},{7,6},{6,7},{9,8},{8,9},{11,10... | collective-permute-start | bytes 46808 | tf_op jit(solution)/shard_map/ppermute | solution.py:15
  118.5 6.7 %collective-permute-start.23 = (f32[1,24,48,1]{2,1,3,0:T(8,128)}, f32[1,24,48,1]{2,1,3,0:T(8,128)}, u32[]{:S(2)}, u32[]{:S(2)}) collective-permute-start(f32[1,24,48,1]{2,1,3,0:T(8,128)} %copy.56), channel_id=1, source_target_pairs={{1,0},{0,1},{3,2},{2,3},{5,4},{4,5},{7,6},{6,7},{9,8},{8,9},{11,10... | collective-permute-start | bytes 13832 | tf_op jit(solution)/shard_map/ppermute | solution.py:23
  120.5 11.0 %collective-permute-start.20 = (f32[1,24,1,128]{3,1,2,0:T(8,128)}, f32[1,24,1,128]{3,1,2,0:T(8,128)S(1)}, u32[]{:S(2)}, u32[]{:S(2)}) collective-permute-start(f32[1,24,1,128]{3,1,2,0:T(8,128)} %bitcast.14), channel_id=1, source_target_pairs={{2,0},{0,2},{3,1},{1,3},{6,4},{4,6},{7,5},{5,7},{10,8},{8,10},{11,... | collective-permute-start | bytes 36872 | tf_op jit(solution)/shard_map/ppermute | solution.py:23
  123.2 12.1 %copy-start.20 = (f32[1,24,48,128]{3,2,1,0:T(8,128)S(1)}, f32[1,24,48,128]{3,2,1,0:T(8,128)}, u32[]{:S(2)}) copy-start(f32[1,24,48,128]{3,2,1,0:T(8,128)} %get-tuple-element.35) | copy-start | bytes 1769476
  125.2 3.1 %collective-permute-start.22 = (f32[1,24,48,1]{2,1,3,0:T(8,128)}, f32[1,24,48,1]{2,1,3,0:T(8,128)}, u32[]{:S(2)}, u32[]{:S(2)}) collective-permute-start(f32[1,24,48,1]{2,1,3,0:T(8,128)} %copy.54), channel_id=1, source_target_pairs={{1,0},{0,1},{3,2},{2,3},{5,4},{4,5},{7,6},{6,7},{9,8},{8,9},{11,10... | collective-permute-start | bytes 13832 | tf_op jit(solution)/shard_map/ppermute | solution.py:23
  128.2 11.0 %copy-start.28 = (f32[1,24,48,128]{3,2,1,0:T(8,128)S(1)}, f32[1,24,48,128]{3,2,1,0:T(8,128)}, u32[]{:S(2)}) copy-start(f32[1,24,48,128]{3,2,1,0:T(8,128)} %get-tuple-element.38) | copy-start | bytes 1769476
  128.2 11.9 %copy-start.13 = (f32[1,24,48,128]{3,2,1,0:T(8,128)S(1)}, f32[1,24,48,128]{3,2,1,0:T(8,128)}, u32[]{:S(2)}) copy-start(f32[1,24,48,128]{3,2,1,0:T(8,128)} %get-tuple-element.33) | copy-start | bytes 1769476
  128.3 7.7 %collective-permute-start.15 = (f32[3,26,50,1]{2,3,1,0:T(1,128)}, f32[3,26,50,1]{2,3,1,0:T(1,128)}, u32[]{:S(2)}, u32[]{:S(2)}) collective-permute-start(f32[3,26,50,1]{2,3,1,0:T(1,128)} %copy.69), channel_id=1, source_target_pairs={{0,1},{1,0},{2,3},{3,2},{4,5},{5,4},{6,7},{7,6},{8,9},{9,8},{10,11... | collective-permute-start | bytes 46808 | tf_op jit(solution)/shard_map/ppermute | solution.py:14
  131.5 19.3 %collective-permute-start.18 = (f32[1,1,48,128]{3,2,1,0:T(8,128)}, f32[1,1,48,128]{3,2,1,0:T(8,128)}, u32[]{:S(2)}, u32[]{:S(2)}) collective-permute-start(f32[1,1,48,128]{3,2,1,0:T(8,128)} %slice.317), channel_id=1, source_target_pairs={{12,0},{0,4},{4,8},{8,12},{13,1},{1,5},{5,9},{9,13},{14,2},{2,6},{... | collective-permute-start | bytes 73736 | tf_op jit(solution)/shard_map/ppermute | solution.py:23
  132.6 18.2 %collective-permute-start.19 = (f32[1,1,48,128]{3,2,1,0:T(8,128)}, f32[1,1,48,128]{3,2,1,0:T(8,128)}, u32[]{:S(2)}, u32[]{:S(2)}) collective-permute-start(f32[1,1,48,128]{3,2,1,0:T(8,128)} %slice.321), channel_id=1, source_target_pairs={{4,0},{8,4},{12,8},{0,12},{5,1},{9,5},{13,9},{1,13},{6,2},{10,6},{... | collective-permute-start | bytes 73736 | tf_op jit(solution)/shard_map/ppermute | solution.py:23
  135.9 14.8 %collective-permute-start.21 = (f32[1,24,1,128]{3,1,2,0:T(8,128)}, f32[1,24,1,128]{3,1,2,0:T(8,128)}, u32[]{:S(2)}, u32[]{:S(2)}) collective-permute-start(f32[1,24,1,128]{3,1,2,0:T(8,128)} %bitcast.17), channel_id=1, source_target_pairs={{2,0},{0,2},{3,1},{1,3},{6,4},{4,6},{7,5},{5,7},{10,8},{8,10},{11,... | collective-permute-start | bytes 36872 | tf_op jit(solution)/shard_map/ppermute | solution.py:23
  166.5 19.0 %collective-permute-start.28 = (f32[1,24,1,128]{3,1,2,0:T(8,128)S(1)}, f32[1,24,1,128]{3,1,2,0:T(8,128)}, u32[]{:S(2)}, u32[]{:S(2)}) collective-permute-start(f32[1,24,1,128]{3,1,2,0:T(8,128)S(1)} %bitcast.171), channel_id=1, source_target_pairs={{2,0},{0,2},{3,1},{1,3},{6,4},{4,6},{7,5},{5,7},{10,8},{8,10},{11,... | collective-permute-start | bytes 36872 | tf_op jit(solution)/shard_map/ppermute | solution.py:23
  168.1 16.9 %collective-permute-start.31 = (f32[1,24,48,1]{2,1,3,0:T(8,128)}, f32[1,24,48,1]{2,1,3,0:T(8,128)}, u32[]{:S(2)}, u32[]{:S(2)}) collective-permute-start(f32[1,24,48,1]{2,1,3,0:T(8,128)} %copy.64), channel_id=1, source_target_pairs={{1,0},{0,1},{3,2},{2,3},{5,4},{4,5},{7,6},{6,7},{9,8},{8,9},{11,10... | collective-permute-start | bytes 13832 | tf_op jit(solution)/shard_map/ppermute | solution.py:23
  172.2 13.3 %collective-permute-start.30 = (f32[1,24,48,1]{2,1,3,0:T(8,128)}, f32[1,24,48,1]{2,1,3,0:T(8,128)S(1)}, u32[]{:S(2)}, u32[]{:S(2)}) collective-permute-start(f32[1,24,48,1]{2,1,3,0:T(8,128)} %copy.62), channel_id=1, source_target_pairs={{1,0},{0,1},{3,2},{2,3},{5,4},{4,5},{7,6},{6,7},{9,8},{8,9},{11,10... | collective-permute-start | bytes 13832 | tf_op jit(solution)/shard_map/ppermute | solution.py:23
  172.7 23.6 %collective-permute-start.25 = (f32[1,24,48,128]{3,2,1,0:T(8,128)}, f32[1,24,48,128]{3,2,1,0:T(8,128)}, u32[]{:S(2)}, u32[]{:S(2)}) collective-permute-start(f32[1,24,48,128]{3,2,1,0:T(8,128)} %get-tuple-element.30), channel_id=1, source_target_pairs={{16,0},{0,16},{17,1},{1,17},{18,2},{2,18},{19,3},{3,19},{20,4},{4,... | collective-permute-start | bytes 1769480 | tf_op jit(solution)/shard_map/ppermute | solution.py:23
  174.2 26.7 %collective-permute-start.24 = (f32[1,24,48,128]{3,2,1,0:T(8,128)}, f32[1,24,48,128]{3,2,1,0:T(8,128)}, u32[]{:S(2)}, u32[]{:S(2)}) collective-permute-start(f32[1,24,48,128]{3,2,1,0:T(8,128)} %get-tuple-element.31), channel_id=1, source_target_pairs={{16,0},{0,16},{17,1},{1,17},{18,2},{2,18},{19,3},{3,19},{20,4},{4,... | collective-permute-start | bytes 1769480 | tf_op jit(solution)/shard_map/ppermute | solution.py:23
  174.7 2.5 %copy-start.4 = (f32[1,24,48,128]{3,2,1,0:T(8,128)S(1)}, f32[1,24,48,128]{3,2,1,0:T(8,128)}, u32[]{:S(2)}) copy-start(f32[1,24,48,128]{3,2,1,0:T(8,128)} %copy-done.3) | copy-start | bytes 1769476
  174.7 2.5 %copy-start.7 = (pred[1,24,48,128]{3,2,1,0:T(8,128)(4,1)S(1)}, pred[1,24,48,128]{3,2,1,0:T(8,128)(4,1)}, u32[]{:S(2)}) copy-start(pred[1,24,48,128]{3,2,1,0:T(8,128)(4,1)} %copy-done.6) | copy-start | bytes 442372
  174.7 2.5 %copy-start.19 = (f32[3,1,48,128]{3,2,1,0:T(8,128)S(1)}, f32[3,1,48,128]{3,2,1,0:T(8,128)}, u32[]{:S(2)}) copy-start(f32[3,1,48,128]{3,2,1,0:T(8,128)} %copy-done.18) | copy-start | bytes 221188
  174.7 2.5 %copy-start.25 = (f32[1,24,48,128]{3,2,1,0:T(8,128)S(1)}, f32[1,24,48,128]{3,2,1,0:T(8,128)}, u32[]{:S(2)}) copy-start(f32[1,24,48,128]{3,2,1,0:T(8,128)} %get-tuple-element.17) | copy-start | bytes 1769476
  182.1 7.3 %copy-start.22 = (f32[1,24,48,128]{3,2,1,0:T(8,128)S(1)}, f32[1,24,48,128]{3,2,1,0:T(8,128)}, u32[]{:S(2)}) copy-start(f32[1,24,48,128]{3,2,1,0:T(8,128)} %get-tuple-element.22) | copy-start | bytes 1769476
  182.1 7.3 %copy-start.26 = (f32[1,24,48,128]{3,2,1,0:T(8,128)S(1)}, f32[1,24,48,128]{3,2,1,0:T(8,128)}, u32[]{:S(2)}) copy-start(f32[1,24,48,128]{3,2,1,0:T(8,128)} %get-tuple-element.10) | copy-start | bytes 1769476
  185.0 11.2 %collective-permute-start.29 = (f32[1,24,1,128]{3,1,2,0:T(8,128)}, f32[1,24,1,128]{3,1,2,0:T(8,128)}, u32[]{:S(2)}, u32[]{:S(2)}) collective-permute-start(f32[1,24,1,128]{3,1,2,0:T(8,128)} %bitcast.23), channel_id=1, source_target_pairs={{2,0},{0,2},{3,1},{1,3},{6,4},{4,6},{7,5},{5,7},{10,8},{8,10},{11,... | collective-permute-start | bytes 36872 | tf_op jit(solution)/shard_map/ppermute | solution.py:23
  185.5 5.0 %copy-start.40 = (f32[1,24,48,1]{2,1,3,0:T(8,128)}, f32[1,24,48,1]{2,1,3,0:T(8,128)S(1)}, u32[]{:S(2)}) copy-start(f32[1,24,48,1]{2,1,3,0:T(8,128)S(1)} %collective-permute-done.30) | copy-start | bytes 13828
  185.5 10.7 %collective-permute-start.26 = (f32[1,1,48,128]{3,2,1,0:T(8,128)}, f32[1,1,48,128]{3,2,1,0:T(8,128)}, u32[]{:S(2)}, u32[]{:S(2)}) collective-permute-start(f32[1,1,48,128]{3,2,1,0:T(8,128)} %slice.334), channel_id=1, source_target_pairs={{12,0},{0,4},{4,8},{8,12},{13,1},{1,5},{5,9},{9,13},{14,2},{2,6},{... | collective-permute-start | bytes 73736 | tf_op jit(solution)/shard_map/ppermute | solution.py:23
  185.5 10.7 %collective-permute-start.27 = (f32[1,1,48,128]{3,2,1,0:T(8,128)}, f32[1,1,48,128]{3,2,1,0:T(8,128)}, u32[]{:S(2)}, u32[]{:S(2)}) collective-permute-start(f32[1,1,48,128]{3,2,1,0:T(8,128)} %slice.337), channel_id=1, source_target_pairs={{4,0},{8,4},{12,8},{0,12},{5,1},{9,5},{13,9},{1,13},{6,2},{10,6},{... | collective-permute-start | bytes 73736 | tf_op jit(solution)/shard_map/ppermute | solution.py:23
  190.5 2.6 %copy-start.14 = (f32[1,24,48,128]{3,2,1,0:T(8,128)S(1)}, f32[1,24,48,128]{3,2,1,0:T(8,128)}, u32[]{:S(2)}) copy-start(f32[1,24,48,128]{3,2,1,0:T(8,128)} %get-tuple-element.24) | copy-start | bytes 1769476
  191.4 3.7 %copy-start.41 = (f32[1,24,48,1]{2,1,3,0:T(8,128)S(1)}, f32[1,24,48,1]{2,1,3,0:T(8,128)}, u32[]{:S(2)}) copy-start(f32[1,24,48,1]{2,1,3,0:T(8,128)} %copy-done.40) | copy-start | bytes 13828
  191.4 9.5 %copy-start.2 = (f32[1,24,48,128]{3,2,1,0:T(8,128)S(1)}, f32[1,24,48,128]{3,2,1,0:T(8,128)}, u32[]{:S(2)}) copy-start(f32[1,24,48,128]{3,2,1,0:T(8,128)} %get-tuple-element.8) | copy-start | bytes 1769476
  191.4 9.5 %copy-start.8 = (pred[1,24,48,128]{3,2,1,0:T(8,128)(4,1)S(1)}, pred[1,24,48,128]{3,2,1,0:T(8,128)(4,1)}, u32[]{:S(2)}) copy-start(pred[1,24,48,128]{3,2,1,0:T(8,128)(4,1)} %copy-done.6) | copy-start | bytes 442372
  191.4 9.5 %copy-start.15 = (f32[1,24,48,128]{3,2,1,0:T(8,128)S(1)}, f32[1,24,48,128]{3,2,1,0:T(8,128)}, u32[]{:S(2)}) copy-start(f32[1,24,48,128]{3,2,1,0:T(8,128)} %get-tuple-element.25) | copy-start | bytes 1769476
  191.4 9.5 %copy-start.35 = (pred[1,24,48,128]{3,2,1,0:T(8,128)(4,1)S(1)}, pred[1,24,48,128]{3,2,1,0:T(8,128)(4,1)}, u32[]{:S(2)}) copy-start(pred[1,24,48,128]{3,2,1,0:T(8,128)(4,1)} %get-tuple-element.23) | copy-start | bytes 442372
  (12 other events, 17.3 us)
where the time goes:
time: 206 us; the launch traced here: 205 us
  local copies, waits for them, and re-layouts  61 us (30%)
  waiting for transfers between devices  60.9 us (30%)
  other arithmetic  46.7 us (23%)
  starting transfers between devices  35.3 us (17%)
    ppermute x8, waiting for transfers between devices, extended(): before = lax.ppermute(last, axis, up)  33.8 us
    ppermute x8, waiting for transfers between devices, extended(): after = lax.ppermute(leading, axis, down)  22.4 us
    ppermute x16, starting transfers between devices, passed_along(): return lax.ppermute(block, axis, route)  16.9 us
    unnamed x8, other arithmetic  16.6 us
    unnamed x94, local copies, waits for them, and re-layouts  12.6 us
    slice x8, local copies, waits for them, and re-layouts, last_layer(): return lax.slice_in_dim(term, count - 1, count, axis=d)  11.4 us
    ppermute x8, starting transfers between devices, extended(): before = lax.ppermute(last, axis, up)  10.6 us
    mul x2, other arithmetic, on_device(): coeff = 0.8 * interior * weight  8.03 us
  transfers between devices with their start and end apart: 32, of which 8 were waited for; matrix products, arithmetic and copies ran while one was open for 34% of the time, Pallas kernels for 0%

commit v1 on v0

v1 whole, which is shorter than its diff:
```python
import functools

import jax
import jax.numpy as jnp
from jax import lax
from jax.experimental import pallas as pl
from jax.experimental.pallas import tpu as pltpu
from jax.sharding import PartitionSpec as P

DAMP = 0.8
KEEP = 1.0 - 0.8


def ring(axis, distance):
    size = lax.axis_size(axis)
    return [(i, (i + distance) % size) for i in range(size)]


def both_ways(up, down, axis):
    if lax.axis_size(axis) == 2 and up is down:
        other = lax.ppermute(up, axis, ring(axis, 1))
        return other, other
    return lax.ppermute(up, axis, ring(axis, 1)), lax.ppermute(down, axis, ring(axis, -1))


def call(body, name, operands, shapes, flops):
    unique, places = [], []
    for x in operands:
        for i, y in enumerate(unique):
            if x is y:
                places.append(i)
                break
        else:
            places.append(len(unique))
            unique.append(x)

    def kernel(*refs):
        ins = [refs[i] for i in places]
        body(*ins, *refs[len(unique):])

    moved = sum(4 * x.size for x in unique) + sum(4 * functools.reduce(lambda a, b: a * b, s) for s in shapes)
    return pl.pallas_call(
        kernel,
        out_shape=[jax.ShapeDtypeStruct(s, jnp.float32) for s in shapes],
        in_specs=[pl.BlockSpec(memory_space=pltpu.VMEM)] * len(unique),
        out_specs=[pl.BlockSpec(memory_space=pltpu.VMEM)] * len(shapes),
        compiler_params=pltpu.CompilerParams(vmem_limit_bytes=40 * 1024 * 1024),
        cost_estimate=pl.CostEstimate(flops=flops, bytes_accessed=moved, transcendentals=0),
        name=name,
    )(*unique)


def iotas(c, d):
    return lax.broadcasted_iota(jnp.int32, (c, d), 0), lax.broadcasted_iota(jnp.int32, (c, d), 1)


def next_c(x, halo, row):
    c = x.shape[0]
    return jnp.where(row == c - 1, halo, pltpu.roll(x, c - 1, 0))


def prev_c(x, halo, row):
    return jnp.where(row == 0, halo, pltpu.roll(x, 1, 0))


def next_d(x, other, lane):
    d = x.shape[1]
    return pltpu.roll(jnp.where(lane == 0, other, x), d - 1, 1)


def prev_d(x, other, lane):
    d = x.shape[1]
    return pltpu.roll(jnp.where(lane == d - 1, other, x), 1, 1)


def prev_b(ref, halo, b):
    return jnp.where(b == 0, halo, ref[0, jnp.maximum(b - 1, 0)])


def next_b(ref, halo, b, count):
    return jnp.where(b == count - 1, halo, ref[0, jnp.minimum(b + 1, count - 1)])


def neighbours(ref, before_b, after_b, gz_before, gz_after, wa_before, wa_after, b, row, lane):
    count = ref.shape[1]
    x = ref[0, b]
    return [
        next_b(ref, after_b[0], b, count),
        prev_b(ref, before_b[0], b),
        next_c(x, gz_after[1, pl.ds(b, 1), :], row),
        prev_c(x, gz_before[0, pl.ds(b, 1), :], row),
        next_d(x, wa_after[0, b], lane),
        prev_d(x, wa_before[0, b], lane),
    ]


def prepare_body(pair, rates, labels, cot, start, f_ref, g_ref, w_ref, up_ref, down_ref, gz_ref, *u_refs):
    count, c, d = g_ref.shape[1:]
    row, lane = iotas(c, d)

    def step(b, _):
        r = [rates[j, 0, b] for j in range(8)]
        total = ((r[0] + r[1]) + (r[2] + r[3])) + ((r[4] + r[5]) + (r[6] + r[7]))
        f = jnp.where(labels[0, b] == 0, DAMP / total, 0.0)
        g = f * cot[0, b]
        f_ref[0, b] = f
        g_ref[0, b] = g
        if pair:
            u_refs[0][0, b] = (r[0] + r[1]) * g
        else:
            u_refs[0][0, b] = r[0] * g
            u_refs[1][0, b] = r[1] * g
        w_ref[0, b] = jnp.where(lane == 0, r[7] * g, r[6] * g)
        gz_ref[0, pl.ds(b, 1), :] = start[0, b, c - 1 :, :]
        gz_ref[1, pl.ds(b, 1), :] = start[0, b, :1, :]
        gz_ref[2, pl.ds(b, 1), :] = (r[4] * g)[c - 1 :]
        gz_ref[3, pl.ds(b, 1), :] = (r[5] * g)[:1]
        return 0

    lax.fori_loop(0, count, step, 0)
    up_ref[0] = start[0, count - 1]
    up_ref[1] = rates[2, 0, count - 1] * g_ref[0, count - 1]
    down_ref[0] = start[0, 0]
    down_ref[1] = rates[3, 0, 0] * g_ref[0, 0]


def forward_body(pair, rates, f_ref, labels, q, q_before, q_after, up, down, gz_before, gz_after, wa_before, wa_after, first, s_ref):
    count, c, d = q.shape[1:]
    row, lane = iotas(c, d)

    def step(b, _):
        f = f_ref[0, b]
        near = neighbours(q, up, down, gz_before, gz_after, wa_before, wa_after, b, row, lane)
        total = sum(rates[2 + k, 0, b] * near[k] for k in range(6))
        if pair:
            total = total + (rates[0, 0, b] + rates[1, 0, b]) * q_after[0, b]
        else:
            total = total + rates[0, 0, b] * q_after[0, b] + rates[1, 0, b] * q_before[0, b]
        s = f * total
        label = labels[0, b]
        s_ref[0, b] = s
        first[0, b] = jnp.where(label == 0, KEEP * q[0, b] + s, jnp.where(label == 2, 1.0, 0.0))
        return 0

    lax.fori_loop(0, count, step, 0)


def spread(rates, f_ref, x, g, up, down, gz_before, gz_after, wa_before, wa_after, at, b, row, lane):
    count, c, d = g.shape[1:]
    f, own = f_ref[0, b], g[0, b]
    below, above = jnp.maximum(b - 1, 0), jnp.minimum(b + 1, count - 1)
    out = jnp.where(f > 0.0, KEEP * x, 0.0)
    out = out + jnp.where(b == 0, up[at], rates[2, 0, below] * g[0, below])
    out = out + jnp.where(b == count - 1, down[at], rates[3, 0, above] * g[0, above])
    out = out + prev_c(rates[4, 0, b] * own, gz_before[2 * at, pl.ds(b, 1), :], row)
    out = out + next_c(rates[5, 0, b] * own, gz_after[2 * at + 1, pl.ds(b, 1), :], row)
    out = out + prev_d(rates[6, 0, b] * own, wa_before[0, b], lane)
    out = out + next_d(rates[7, 0, b] * own, wa_after[0, b], lane)
    return out


def back_body(pair, rates, f_ref, cot, g, u_before, u_after, up, down, gz_before, gz_after, wa_before, wa_after, first,
              back, h_ref, w_ref, up_ref, down_ref, gz_ref, *v_refs):
    count, c, d = g.shape[1:]
    row, lane = iotas(c, d)

    def step(b, _):
        out = spread(rates, f_ref, cot[0, b], g, up, down, gz_before, gz_after, wa_before, wa_after, 1, b, row, lane)
        if pair:
            out = out + u_before[0, b]
        else:
            out = out + u_before[0, b] + u_after[0, b]
        h = f_ref[0, b] * out
        back[0, b] = out
        h_ref[0, b] = h
        if pair:
            v_refs[0][0, b] = (rates[0, 0, b] + rates[1, 0, b]) * h
        else:
            v_refs[0][0, b] = rates[0, 0, b] * h
            v_refs[1][0, b] = rates[1, 0, b] * h
        w_ref[0, b] = jnp.where(lane == 0, rates[7, 0, b] * h, rates[6, 0, b] * h)
        gz_ref[0, pl.ds(b, 1), :] = first[0, b, c - 1 :, :]
        gz_ref[1, pl.ds(b, 1), :] = first[0, b, :1, :]
        gz_ref[2, pl.ds(b, 1), :] = (rates[4, 0, b] * h)[c - 1 :]
        gz_ref[3, pl.ds(b, 1), :] = (rates[5, 0, b] * h)[:1]
        return 0

    lax.fori_loop(0, count, step, 0)
    up_ref[0] = first[0, count - 1]
    up_ref[1] = rates[2, 0, count - 1] * h_ref[0, count - 1]
    down_ref[0] = first[0, 0]
    down_ref[1] = rates[3, 0, 0] * h_ref[0, 0]


def partial_body(rates, f_ref, back, h, up, down, gz_before, gz_after, wa_before, wa_after, out):
    count, c, d = h.shape[1:]
    row, lane = iotas(c, d)

    def step(b, _):
        out[0, b] = spread(rates, f_ref, back[0, b], h, up, down, gz_before, gz_after, wa_before, wa_after, 1, b, row, lane)
        return 0

    lax.fori_loop(0, count, step, 0)


def last_body(rates, f_ref, labels, g, h, s_ref, start, start_before, start_after, up0, down0, gz_before0, gz_after0, wa_before0,
              wa_after0, first, first_before, first_after, up1, down1, gz_before1, gz_after1, wa_before1, wa_after1, committor, out):
    count, c, d = first.shape[1:]
    row, lane = iotas(c, d)

    def step(b, _):
        f = f_ref[0, b]
        near1 = [first_after[0, b], first_before[0, b]]
        near1 += neighbours(first, up1, down1, gz_before1, gz_after1, wa_before1, wa_after1, b, row, lane)
        s1 = f * sum(rates[k, 0, b] * near1[k] for k in range(8))
        label = labels[0, b]
        committor[0, b] = jnp.where(label == 0, KEEP * first[0, b] + s1, jnp.where(label == 2, 1.0, 0.0))
        near0 = [start_after[0, b], start_before[0, b]]
        near0 += neighbours(start, up0, down0, gz_before0, gz_after0, wa_before0, wa_after0, b, row, lane)
        avg1, avg0 = s1 * (1.0 / DAMP), s_ref[0, b] * (1.0 / DAMP)
        gb, hb = g[0, b], h[0, b]
        for k in range(8):
            out[k, 0, b] = gb * (near1[k] - avg1) + hb * (near0[k] - avg0)
        return 0

    lax.fori_loop(0, count, step, 0)


def on_device(start, rates, labels, cotangent):
    _, b, c, d = start.shape
    block = (1, b, c, d)
    cells = b * c * d
    pair = lax.axis_size("grp") == 2
    blocks = [block] * (1 if pair else 2)
    faces = [(2, c, d), (2, c, d), (4, b, d)]

    start_before, start_after = both_ways(start, start, "grp")
    f, g, w0, up, down, gz, *u = call(
        functools.partial(prepare_body, pair), "prepare", [rates, labels, cotangent, start], [block] * 3 + faces + blocks, 20 * cells
    )
    u_before, u_after = both_ways(u[0], u[-1], "grp")
    up0, down0 = both_ways(up, down, "gy")
    gz_before0, gz_after0 = both_ways(gz, gz, "gz")
    wa0 = both_ways(start, start, "wa")
    waw0 = both_ways(w0, w0, "wa")

    first, s0 = call(
        functools.partial(forward_body, pair),
        "forward",
        [rates, f, labels, start, start_before, start_after, up0, down0, gz_before0, gz_after0, *wa0],
        [block] * 2,
        30 * cells,
    )
    first_before, first_after = both_ways(first, first, "grp")
    wa1 = both_ways(first, first, "wa")

    back, h, w1, up, down, gz, *v = call(
        functools.partial(back_body, pair),
        "backward",
        [rates, f, cotangent, g, u_before, u_after, up0, down0, gz_before0, gz_after0, *waw0, first],
        [block] * 3 + faces + blocks,
        30 * cells,
    )
    v_before, v_after = both_ways(v[0], v[-1], "grp")
    up1, down1 = both_ways(up, down, "gy")
    gz_before1, gz_after1 = both_ways(gz, gz, "gz")
    waw1 = both_ways(w1, w1, "wa")

    (grad,) = call(partial_body, "partial", [rates, f, back, h, up1, down1, gz_before1, gz_after1, *waw1], [block], 30 * cells)
    committor, grad_rates = call(
        last_body,
        "last",
        [rates, f, labels, g, h, s0, start, start_before, start_after, up0, down0, gz_before0, gz_after0, *wa0,
         first, first_before, first_after, up1, down1, gz_before1, gz_after1, *wa1],
        [block, (8, 1, b, c, d)],
        90 * cells,
    )
    grad_start = grad + v_before if pair else grad + v_before + v_after
    return committor, grad_start, grad_rates


def solution(mesh):
    placed = (
        P("grp", "gy", "gz", "wa"),
        P(None, "grp", "gy", "gz", "wa"),
        P("grp", "gy", "gz", "wa"),
        P("grp", "gy", "gz", "wa"),
    )
    return jax.shard_map(
        on_device,
        mesh=mesh,
        in_specs=placed,
        out_specs=(
            P("grp", "gy", "gz", "wa"),
            P("grp", "gy", "gz", "wa"),
            P(None, "grp", "gy", "gz", "wa"),
        ),
        check_vma=False,
    )
```

time: 206 us -> 66 us (0.32)
  local copies, waits for them, and re-layouts: 61 us -> 5.54 us
  other arithmetic: 46.7 us -> 0.88 us
  waiting for transfers between devices: 60.9 us -> 29.6 us
  starting transfers between devices: 35.3 us -> 16.8 us
  Pallas kernels: 0 us -> 12.3 us
    slice x25 -> x0, local copies, waits for them, and re-layouts: 32.3 us -> none  [the longest x8 11.4 us: last_layer(): return lax.slice_in_dim(term, count - 1, count, axis=d)]
    ppermute x32 -> x14, waiting for transfers between devices: 60.9 us -> 29.6 us  [the longest x10 17 us: both_ways(): other = lax.ppermute(up, axis, ring(axis, 1))]
    ppermute x32 -> x14, starting transfers between devices: 35.3 us -> 16.8 us  [the longest x10 9.31 us: both_ways(): other = lax.ppermute(up, axis, ring(axis, 1))]
    unnamed x8 -> x0, other arithmetic: 16.6 us -> none
    ppermute x8 -> x0, local copies, waits for them, and re-layouts: 16.1 us -> none  [the longest x4 5.72 us: passed_along(): return lax.ppermute(block, axis, route)]
    mul x4 -> x0, other arithmetic: 14.7 us -> none  [the longest x2 8.03 us: on_device(): coeff = 0.8 * interior * weight]
    pallas_call x0 -> x5, Pallas kernels: none -> 12.3 us  [call(): pl.pallas_call(kernel, out_shape=[jax.ShapeDtypeStruct(s, jnp.float32) fo...]
    add x2 -> x1, other arithmetic: 10.8 us -> 0.88 us  [on_device(): grad_start = grad + v_before if pair else grad + v_before + v_after]
  transfers between devices with their start and end apart: 32 -> 14, of which waited for: 8 -> 8; matrix products, arithmetic and copies ran while one was open for 34% -> 1% of each run, Pallas kernels for 0% -> 7%
where the time goes in v1:
time: 66 us; the launch traced here: 65.7 us
  waiting for transfers between devices  29.6 us (45%)
  starting transfers between devices  16.8 us (25%)
  Pallas kernels  12.3 us (19%)
  local copies, waits for them, and re-layouts  5.54 us (8%)
  other arithmetic  0.88 us (1%)
  between operations  0.68 us (1%)
    ppermute x10, waiting for transfers between devices, both_ways(): other = lax.ppermute(up, axis, ring(axis, 1))  17 us
    pallas_call x5, Pallas kernels, call(): pl.pallas_call(kernel, out_shape=[jax.ShapeDtypeStruct(s, jnp.float32) fo...  12.3 us
    ppermute x10, starting transfers between devices, both_ways(): other = lax.ppermute(up, axis, ring(axis, 1))  9.31 us
    ppermute x2, waiting for transfers between devices, both_ways(): lax.ppermute(up, axis, ring(axis, 1))  8.3 us
    unnamed x12, local copies, waits for them, and re-layouts  5.54 us
    ppermute x2, waiting for transfers between devices, both_ways(): lax.ppermute(down, axis, ring(axis, -1))  4.25 us
    ppermute x2, starting transfers between devices, both_ways(): lax.ppermute(down, axis, ring(axis, -1))  3.93 us
    ppermute x2, starting transfers between devices, both_ways(): lax.ppermute(up, axis, ring(axis, 1))  3.52 us
  transfers between devices with their start and end apart: 14, of which 8 were waited for; matrix products, arithmetic and copies ran while one was open for 1% of the time, Pallas kernels for 7%

profile of v1, /device:TPU:0, one launch (start us, length us, event | category | flops | bytes accessed | tf_op | source)
XLA Modules:
  0.0 65.7 jit_solution(5807386778938383278)
XLA Ops:
  0.6 3.0 %collective-permute-start.5 = (f32[1,24,48,128]{3,2,1,0:T(8,128)}, f32[1,24,48,128]{3,2,1,0:T(8,128)S(1)}, u32[]{:S(2)}, u32[]{:S(2)}) collective-permute-start(f32[1,24,48,128]{3,2,1,0:T(8,128)} %refs_6_.1), channel_id=1, source_target_pairs={{0,16},{16,0},{1,17},{17,1},{2,18},{18,2},{3,19},{19,3},{4,20},{20... | collective-permute-start | bytes 1769480 | tf_op jit(solution)/shard_map/ppermute | solution.py:21
  3.7 0.0 collective-permute-start.6
  3.7 0.0 copy-start
  3.7 2.3 %copy-done = f32[8,1,24,48,128]{4,3,2,1,0:T(8,128)S(1)} copy-done((f32[8,1,24,48,128]{4,3,2,1,0:T(8,128)S(1)}, f32[8,1,24,48,128]{4,3,2,1,0:T(8,128)}, u32[]{:S(2)}) %copy-start) | copy-done | bytes 4718616
  6.0 0.0 copy-start.1
  6.0 1.1 %copy-done.1 = s32[1,24,48,128]{3,2,1,0:T(8,128)S(1)} copy-done((s32[1,24,48,128]{3,2,1,0:T(8,128)S(1)}, s32[1,24,48,128]{3,2,1,0:T(8,128)}, u32[]{:S(2)}) %copy-start.1) | copy-done | bytes 589848
  7.1 0.0 copy-start.3
  7.1 1.1 %copy-done.3 = f32[1,24,48,128]{3,2,1,0:T(8,128)S(1)} copy-done((f32[1,24,48,128]{3,2,1,0:T(8,128)S(1)}, f32[1,24,48,128]{3,2,1,0:T(8,128)}, u32[]{:S(2)}) %copy-start.3) | copy-done | bytes 589848
  8.1 0.0 copy-start.5
  8.1 1.1 %copy-done.5 = f32[1,24,48,128]{3,2,1,0:T(8,128)S(1)} copy-done((f32[1,24,48,128]{3,2,1,0:T(8,128)S(1)}, f32[1,24,48,128]{3,2,1,0:T(8,128)}, u32[]{:S(2)}) %copy-start.5) | copy-done | bytes 589848
  9.2 0.6 prepare.1
  9.8 0.2 collective-permute-start
  10.0 0.5 collective-permute-start.4
  10.5 1.7 %collective-permute-start.1 = (f32[2,48,128]{2,1,0:T(8,128)S(1)}, f32[2,48,128]{2,1,0:T(8,128)S(1)}, u32[]{:S(2)}, u32[]{:S(2)}) collective-permute-start(f32[2,48,128]{2,1,0:T(8,128)S(1)} %get-tuple-element.24), channel_id=1, source_target_pairs={{0,4},{4,8},{8,12},{12,0},{1,5},{5,9},{9,13},{13,1},{2,6},{6,10},{... | collective-permute-start | bytes 147464 | tf_op jit(solution)/shard_map/ppermute | solution.py:23
  12.2 4.2 %collective-permute-done.1.refs_5_.refs_8_ = f32[2,48,128]{2,1,0:T(8,128)S(1)} collective-permute-done((f32[2,48,128]{2,1,0:T(8,128)S(1)}, f32[2,48,128]{2,1,0:T(8,128)S(1)}, u32[]{:S(2)}, u32[]{:S(2)}) %collective-permute-start.1) | collective-permute-done | bytes 49184 | tf_op jit(solution)/shard_map/ppermute | solution.py:23
  16.4 1.9 %collective-permute-start.2 = (f32[2,48,128]{2,1,0:T(8,128)S(1)}, f32[2,48,128]{2,1,0:T(8,128)S(1)}, u32[]{:S(2)}, u32[]{:S(2)}) collective-permute-start(f32[2,48,128]{2,1,0:T(8,128)S(1)} %get-tuple-element.25), channel_id=1, source_target_pairs={{0,12},{4,0},{8,4},{12,8},{1,13},{5,1},{9,5},{13,9},{2,14},{6,2},{... | collective-permute-start | bytes 147464 | tf_op jit(solution)/shard_map/ppermute | solution.py:23
  18.3 2.2 %collective-permute-done.2.refs_6_.refs_9_ = f32[2,48,128]{2,1,0:T(8,128)S(1)} collective-permute-done((f32[2,48,128]{2,1,0:T(8,128)S(1)}, f32[2,48,128]{2,1,0:T(8,128)S(1)}, u32[]{:S(2)}, u32[]{:S(2)}) %collective-permute-start.2) | collective-permute-done | bytes 49184 | tf_op jit(solution)/shard_map/ppermute | solution.py:23
  20.5 1.6 %collective-permute-start.3 = (f32[4,24,128]{2,1,0:T(8,128)S(1)}, f32[4,24,128]{2,1,0:T(8,128)S(1)}, u32[]{:S(2)}, u32[]{:S(2)}) collective-permute-start(f32[4,24,128]{2,1,0:T(8,128)S(1)} %get-tuple-element.26), channel_id=1, source_target_pairs={{0,2},{2,0},{1,3},{3,1},{4,6},{6,4},{5,7},{7,5},{8,10},{10,8},{9,1... | collective-permute-start | bytes 147464 | tf_op jit(solution)/shard_map/ppermute | solution.py:21
  22.1 2.5 %collective-permute-done.3.refs_7_.refs_10_ = f32[4,24,128]{2,1,0:T(8,128)S(1)} collective-permute-done((f32[4,24,128]{2,1,0:T(8,128)S(1)}, f32[4,24,128]{2,1,0:T(8,128)S(1)}, u32[]{:S(2)}, u32[]{:S(2)}) %collective-permute-start.3) | collective-permute-done | bytes 49184 | tf_op jit(solution)/shard_map/ppermute | solution.py:21
  24.6 0.0 collective-permute-done.5.refs_4_.refs_7_
  24.6 0.0 collective-permute-done.6.refs_8_.refs_11_
  24.6 2.1 %forward.1 = (f32[1,24,48,128]{3,2,1,0:T(8,128)S(1)}, f32[1,24,48,128]{3,2,1,0:T(8,128)S(1)}) custom-call(f32[8,1,24,48,128]{4,3,2,1,0:T(8,128)S(1)} %copy-done, f32[1,24,48,128]{3,2,1,0:T(8,128)S(1)} %get-tuple-element.21.refs_1_, s32[1,24,48,128]{3,2,1,0:T(8,128)S(1)} %copy-done.1, f32[1,24,48,128]{3,2,1,0:T(8,128)S(1)} %copy-done.3, ...), custom_call_target="tpu_custom_call" | custom-call | flops 4423680 | bytes 8994816 | tf_op jit(solution)/shard_map/forward/pallas_call | solution.py:42
  26.7 3.1 %collective-permute-done.refs_4_ = f32[1,24,48,128]{3,2,1,0:T(8,128)S(1)} collective-permute-done((f32[1,24,48,128]{3,2,1,0:T(8,128)S(1)}, f32[1,24,48,128]{3,2,1,0:T(8,128)S(1)}, u32[]{:S(2)}, u32[]{:S(2)}) %collective-permute-start) | collective-permute-done | bytes 589856 | tf_op jit(solution)/shard_map/ppermute | solution.py:21
  29.8 0.0 collective-permute-done.4.refs_8_
  29.8 2.3 %backward.1 = (f32[1,24,48,128]{3,2,1,0:T(8,128)S(1)}, f32[1,24,48,128]{3,2,1,0:T(8,128)S(1)}, f32[1,24,48,128]{3,2,1,0:T(8,128)S(1)}, f32[2,48,128]{2,1,0:T(8,1...) custom-call(f32[8,1,24,48,128]{4,3,2,1,0:T(8,128)S(1)} %copy-done, ...), custom_call_target="tpu_custom_call" | custom-call | flops 4423680 | bytes 10911744 | tf_op jit(solution)/shard_map/backward/pallas_call | solution.py:42
  32.1 0.1 collective-permute-start.12
  32.2 1.8 %collective-permute-start.13 = (f32[1,24,48,128]{3,2,1,0:T(8,128)S(1)}, f32[1,24,48,128]{3,2,1,0:T(8,128)S(1)}, u32[]{:S(2)}, u32[]{:S(2)}) collective-permute-start(f32[1,24,48,128]{3,2,1,0:T(8,128)S(1)} %get-tuple-element.37), channel_id=1, source_target_pairs={{0,16},{16,0},{1,17},{17,1},{2,18},{18,2},{3,19},{19,3},{4,20},{20... | collective-permute-start | bytes 1769480 | tf_op jit(solution)/shard_map/ppermute | solution.py:21
  34.0 0.2 collective-permute-start.11
  34.2 0.3 collective-permute-start.7
  34.5 1.7 %collective-permute-start.10 = (f32[4,24,128]{2,1,0:T(8,128)S(1)}, f32[4,24,128]{2,1,0:T(8,128)S(1)}, u32[]{:S(2)}, u32[]{:S(2)}) collective-permute-start(f32[4,24,128]{2,1,0:T(8,128)S(1)} %get-tuple-element.33), channel_id=1, source_target_pairs={{0,2},{2,0},{1,3},{3,1},{4,6},{6,4},{5,7},{7,5},{8,10},{10,8},{9,1... | collective-permute-start | bytes 147464 | tf_op jit(solution)/shard_map/ppermute | solution.py:21
  36.2 2.4 %collective-permute-done.10.refs_16_.refs_6_ = f32[4,24,128]{2,1,0:T(8,128)S(1)} collective-permute-done((f32[4,24,128]{2,1,0:T(8,128)S(1)}, f32[4,24,128]{2,1,0:T(8,128)S(1)}, u32[]{:S(2)}, u32[]{:S(2)}) %collective-permute-start.10) | collective-permute-done | bytes 49184 | tf_op jit(solution)/shard_map/ppermute | solution.py:21
  38.5 1.8 %collective-permute-start.8 = (f32[2,48,128]{2,1,0:T(8,128)S(1)}, f32[2,48,128]{2,1,0:T(8,128)S(1)}, u32[]{:S(2)}, u32[]{:S(2)}) collective-permute-start(f32[2,48,128]{2,1,0:T(8,128)S(1)} %get-tuple-element.31), channel_id=1, source_target_pairs={{0,4},{4,8},{8,12},{12,0},{1,5},{5,9},{9,13},{13,1},{2,6},{6,10},{... | collective-permute-start | bytes 147464 | tf_op jit(solution)/shard_map/ppermute | solution.py:23
  40.3 4.1 %collective-permute-done.8.refs_14_.refs_4_ = f32[2,48,128]{2,1,0:T(8,128)S(1)} collective-permute-done((f32[2,48,128]{2,1,0:T(8,128)S(1)}, f32[2,48,128]{2,1,0:T(8,128)S(1)}, u32[]{:S(2)}, u32[]{:S(2)}) %collective-permute-start.8) | collective-permute-done | bytes 49184 | tf_op jit(solution)/shard_map/ppermute | solution.py:23
  44.4 2.0 %collective-permute-start.9 = (f32[2,48,128]{2,1,0:T(8,128)S(1)}, f32[2,48,128]{2,1,0:T(8,128)S(1)}, u32[]{:S(2)}, u32[]{:S(2)}) collective-permute-start(f32[2,48,128]{2,1,0:T(8,128)S(1)} %get-tuple-element.32), channel_id=1, source_target_pairs={{0,12},{4,0},{8,4},{12,8},{1,13},{5,1},{9,5},{13,9},{2,14},{6,2},{... | collective-permute-start | bytes 147464 | tf_op jit(solution)/shard_map/ppermute | solution.py:23
  46.5 2.1 %collective-permute-done.9.refs_15_.refs_5_ = f32[2,48,128]{2,1,0:T(8,128)S(1)} collective-permute-done((f32[2,48,128]{2,1,0:T(8,128)S(1)}, f32[2,48,128]{2,1,0:T(8,128)S(1)}, u32[]{:S(2)}, u32[]{:S(2)}) %collective-permute-start.9) | collective-permute-done | bytes 49184 | tf_op jit(solution)/shard_map/ppermute | solution.py:23
  48.5 0.0 collective-permute-done.12.refs_7_
  48.5 0.0 copy-start.2
  48.5 0.0 copy-start.4
  48.5 2.2 %partial.1 = f32[1,24,48,128]{3,2,1,0:T(8,128)S(1)} custom-call(f32[8,1,24,48,128]{4,3,2,1,0:T(8,128)S(1)} %copy-done, f32[1,24,48,128]{3,2,1,0:T(8,128)S(1)} %get-tuple-element.21.refs_1_, f32[1,24,48,128]{3,2,1,0:T(8,128)S(1)} %get-tuple-element.35.refs_2_, f32[1,24,48,128]{3,2,1,0:T(8,128)S(1)} %get-tuple-element.29.refs_4_.refs_3_, ...), custom_call_target="tpu_custom_call" | custom-call | flops 4423680 | bytes 7815168 | tf_op jit(solution)/shard_map/partial/pallas_call | solution.py:42
  50.7 0.0 collective-permute-done.13
  50.7 0.9 %add.3 = f32[1,24,48,128]{3,2,1,0:T(8,128)} add(f32[1,24,48,128]{3,2,1,0:T(8,128)S(1)} %partial.1, f32[1,24,48,128]{3,2,1,0:T(8,128)S(1)} %collective-permute-done.13) | non-fusion elementwise | flops 147456 | bytes 1769472 | tf_op jit(solution)/shard_map/add | solution.py:278
  51.6 0.0 collective-permute-done.11.refs_17_
  51.6 9.0 %collective-permute-done.7.refs_13_ = f32[1,24,48,128]{3,2,1,0:T(8,128)S(1)} collective-permute-done((f32[1,24,48,128]{3,2,1,0:T(8,128)S(1)}, f32[1,24,48,128]{3,2,1,0:T(8,128)S(1)}, u32[]{:S(2)}, u32[]{:S(2)}) %collective-permute-start.7) | collective-permute-done | bytes 589856 | tf_op jit(solution)/shard_map/ppermute | solution.py:21
  60.6 0.0 copy-done.2
  60.6 0.0 copy-done.4
  60.6 5.1 %last.1 = (f32[1,24,48,128]{3,2,1,0:T(8,128)}, f32[8,1,24,48,128]{4,3,2,1,0:T(8,128)}) custom-call(f32[8,1,24,48,128]{4,3,2,1,0:T(8,128)S(1)} %copy-done, f32[1,24,48,128]{3,2,1,0:T(8,128)S(1)} %get-tuple-element.21.refs_1_, s32[1,24,48,128]{3,2,1,0:T(8,128)S(1)} %copy-done.2, f32[1,24,48,128]{3,2,1,0:T(8,128)S(1)} %get-tuple-element.22.refs_3_, ...), custom_call_target="tpu_custom_call" | custom-call | flops 13271040 | bytes 16809984 | tf_op jit(solution)/shard_map/last/pallas_call | solution.py:42
Async XLA Ops:
  0.6 24.0 %collective-permute-start.5 = (f32[1,24,48,128]{3,2,1,0:T(8,128)}, f32[1,24,48,128]{3,2,1,0:T(8,128)S(1)}, u32[]{:S(2)}, u32[]{:S(2)}) collective-permute-start(f32[1,24,48,128]{3,2,1,0:T(8,128)} %refs_6_.1), channel_id=1, source_target_pairs={{0,16},{16,0},{1,17},{17,1},{2,18},{18,2},{3,19},{19,3},{4,20},{20... | collective-permute-start | bytes 1769480 | tf_op jit(solution)/shard_map/ppermute | solution.py:21
  3.7 20.9 %collective-permute-start.6 = (f32[1,24,48,128]{3,2,1,0:T(8,128)}, f32[1,24,48,128]{3,2,1,0:T(8,128)S(1)}, u32[]{:S(2)}, u32[]{:S(2)}) collective-permute-start(f32[1,24,48,128]{3,2,1,0:T(8,128)} %refs_6_.1), channel_id=1, source_target_pairs={{0,1},{1,0},{2,3},{3,2},{4,5},{5,4},{6,7},{7,6},{8,9},{9,8},{10,11... | collective-permute-start | bytes 1769480 | tf_op jit(solution)/shard_map/ppermute | solution.py:21
  3.7 2.3 %copy-start = (f32[8,1,24,48,128]{4,3,2,1,0:T(8,128)S(1)}, f32[8,1,24,48,128]{4,3,2,1,0:T(8,128)}, u32[]{:S(2)}) copy-start(f32[8,1,24,48,128]{4,3,2,1,0:T(8,128)} %refs_0_.9) | copy-start | bytes 14155780
  6.0 1.1 %copy-start.1 = (s32[1,24,48,128]{3,2,1,0:T(8,128)S(1)}, s32[1,24,48,128]{3,2,1,0:T(8,128)}, u32[]{:S(2)}) copy-start(s32[1,24,48,128]{3,2,1,0:T(8,128)} %refs_2_.7) | copy-start | bytes 1769476
  7.1 1.1 %copy-start.3 = (f32[1,24,48,128]{3,2,1,0:T(8,128)S(1)}, f32[1,24,48,128]{3,2,1,0:T(8,128)}, u32[]{:S(2)}) copy-start(f32[1,24,48,128]{3,2,1,0:T(8,128)} %refs_6_.1) | copy-start | bytes 1769476
  8.1 1.1 %copy-start.5 = (f32[1,24,48,128]{3,2,1,0:T(8,128)S(1)}, f32[1,24,48,128]{3,2,1,0:T(8,128)}, u32[]{:S(2)}) copy-start(f32[1,24,48,128]{3,2,1,0:T(8,128)} %refs_2_.6) | copy-start | bytes 1769476
  9.8 20.0 %collective-permute-start = (f32[1,24,48,128]{3,2,1,0:T(8,128)S(1)}, f32[1,24,48,128]{3,2,1,0:T(8,128)S(1)}, u32[]{:S(2)}, u32[]{:S(2)}) collective-permute-start(f32[1,24,48,128]{3,2,1,0:T(8,128)S(1)} %get-tuple-element.23), channel_id=1, source_target_pairs={{0,16},{16,0},{1,17},{17,1},{2,18},{18,2},{3,19},{19,3},{4,20},{20... | collective-permute-start | bytes 1769480 | tf_op jit(solution)/shard_map/ppermute | solution.py:21
  10.0 19.9 %collective-permute-start.4 = (f32[1,24,48,128]{3,2,1,0:T(8,128)S(1)}, f32[1,24,48,128]{3,2,1,0:T(8,128)S(1)}, u32[]{:S(2)}, u32[]{:S(2)}) collective-permute-start(f32[1,24,48,128]{3,2,1,0:T(8,128)S(1)} %get-tuple-element.27), channel_id=1, source_target_pairs={{0,1},{1,0},{2,3},{3,2},{4,5},{5,4},{6,7},{7,6},{8,9},{9,8},{10,11... | collective-permute-start | bytes 1769480 | tf_op jit(solution)/shard_map/ppermute | solution.py:21
  10.5 5.9 %collective-permute-start.1 = (f32[2,48,128]{2,1,0:T(8,128)S(1)}, f32[2,48,128]{2,1,0:T(8,128)S(1)}, u32[]{:S(2)}, u32[]{:S(2)}) collective-permute-start(f32[2,48,128]{2,1,0:T(8,128)S(1)} %get-tuple-element.24), channel_id=1, source_target_pairs={{0,4},{4,8},{8,12},{12,0},{1,5},{5,9},{9,13},{13,1},{2,6},{6,10},{... | collective-permute-start | bytes 147464 | tf_op jit(solution)/shard_map/ppermute | solution.py:23
  16.4 4.1 %collective-permute-start.2 = (f32[2,48,128]{2,1,0:T(8,128)S(1)}, f32[2,48,128]{2,1,0:T(8,128)S(1)}, u32[]{:S(2)}, u32[]{:S(2)}) collective-permute-start(f32[2,48,128]{2,1,0:T(8,128)S(1)} %get-tuple-element.25), channel_id=1, source_target_pairs={{0,12},{4,0},{8,4},{12,8},{1,13},{5,1},{9,5},{13,9},{2,14},{6,2},{... | collective-permute-start | bytes 147464 | tf_op jit(solution)/shard_map/ppermute | solution.py:23
  20.5 4.1 %collective-permute-start.3 = (f32[4,24,128]{2,1,0:T(8,128)S(1)}, f32[4,24,128]{2,1,0:T(8,128)S(1)}, u32[]{:S(2)}, u32[]{:S(2)}) collective-permute-start(f32[4,24,128]{2,1,0:T(8,128)S(1)} %get-tuple-element.26), channel_id=1, source_target_pairs={{0,2},{2,0},{1,3},{3,1},{4,6},{6,4},{5,7},{7,5},{8,10},{10,8},{9,1... | collective-permute-start | bytes 147464 | tf_op jit(solution)/shard_map/ppermute | solution.py:21
  32.1 16.4 %collective-permute-start.12 = (f32[1,24,48,128]{3,2,1,0:T(8,128)S(1)}, f32[1,24,48,128]{3,2,1,0:T(8,128)S(1)}, u32[]{:S(2)}, u32[]{:S(2)}) collective-permute-start(f32[1,24,48,128]{3,2,1,0:T(8,128)S(1)} %get-tuple-element.36), channel_id=1, source_target_pairs={{0,1},{1,0},{2,3},{3,2},{4,5},{5,4},{6,7},{7,6},{8,9},{9,8},{10,11... | collective-permute-start | bytes 1769480 | tf_op jit(solution)/shard_map/ppermute | solution.py:21
  32.2 18.5 %collective-permute-start.13 = (f32[1,24,48,128]{3,2,1,0:T(8,128)S(1)}, f32[1,24,48,128]{3,2,1,0:T(8,128)S(1)}, u32[]{:S(2)}, u32[]{:S(2)}) collective-permute-start(f32[1,24,48,128]{3,2,1,0:T(8,128)S(1)} %get-tuple-element.37), channel_id=1, source_target_pairs={{0,16},{16,0},{1,17},{17,1},{2,18},{18,2},{3,19},{19,3},{4,20},{20... | collective-permute-start | bytes 1769480 | tf_op jit(solution)/shard_map/ppermute | solution.py:21
  34.0 17.6 %collective-permute-start.11 = (f32[1,24,48,128]{3,2,1,0:T(8,128)S(1)}, f32[1,24,48,128]{3,2,1,0:T(8,128)S(1)}, u32[]{:S(2)}, u32[]{:S(2)}) collective-permute-start(f32[1,24,48,128]{3,2,1,0:T(8,128)S(1)} %get-tuple-element.28.refs_9_.refs_12_), channel_id=1, source_target_pairs={{0,1},{1,0},{2,3},{3,2},{4,5},{5,4},{6,7},{7,6},{8,9},{9,8},{10,11... | collective-permute-start | bytes 1769480 | tf_op jit(solution)/shard_map/ppermute | solution.py:21
  34.2 26.4 %collective-permute-start.7 = (f32[1,24,48,128]{3,2,1,0:T(8,128)S(1)}, f32[1,24,48,128]{3,2,1,0:T(8,128)S(1)}, u32[]{:S(2)}, u32[]{:S(2)}) collective-permute-start(f32[1,24,48,128]{3,2,1,0:T(8,128)S(1)} %get-tuple-element.28.refs_9_.refs_12_), channel_id=1, source_target_pairs={{0,16},{16,0},{1,17},{17,1},{2,18},{18,2},{3,19},{19,3},{4,20},{20... | collective-permute-start | bytes 1769480 | tf_op jit(solution)/shard_map/ppermute | solution.py:21
  34.5 4.1 %collective-permute-start.10 = (f32[4,24,128]{2,1,0:T(8,128)S(1)}, f32[4,24,128]{2,1,0:T(8,128)S(1)}, u32[]{:S(2)}, u32[]{:S(2)}) collective-permute-start(f32[4,24,128]{2,1,0:T(8,128)S(1)} %get-tuple-element.33), channel_id=1, source_target_pairs={{0,2},{2,0},{1,3},{3,1},{4,6},{6,4},{5,7},{7,5},{8,10},{10,8},{9,1... | collective-permute-start | bytes 147464 | tf_op jit(solution)/shard_map/ppermute | solution.py:21
  38.5 5.9 %collective-permute-start.8 = (f32[2,48,128]{2,1,0:T(8,128)S(1)}, f32[2,48,128]{2,1,0:T(8,128)S(1)}, u32[]{:S(2)}, u32[]{:S(2)}) collective-permute-start(f32[2,48,128]{2,1,0:T(8,128)S(1)} %get-tuple-element.31), channel_id=1, source_target_pairs={{0,4},{4,8},{8,12},{12,0},{1,5},{5,9},{9,13},{13,1},{2,6},{6,10},{... | collective-permute-start | bytes 147464 | tf_op jit(solution)/shard_map/ppermute | solution.py:23
  44.4 4.1 %collective-permute-start.9 = (f32[2,48,128]{2,1,0:T(8,128)S(1)}, f32[2,48,128]{2,1,0:T(8,128)S(1)}, u32[]{:S(2)}, u32[]{:S(2)}) collective-permute-start(f32[2,48,128]{2,1,0:T(8,128)S(1)} %get-tuple-element.32), channel_id=1, source_target_pairs={{0,12},{4,0},{8,4},{12,8},{1,13},{5,1},{9,5},{13,9},{2,14},{6,2},{... | collective-permute-start | bytes 147464 | tf_op jit(solution)/shard_map/ppermute | solution.py:23
  48.5 12.1 %copy-start.2 = (s32[1,24,48,128]{3,2,1,0:T(8,128)S(1)}, s32[1,24,48,128]{3,2,1,0:T(8,128)}, u32[]{:S(2)}) copy-start(s32[1,24,48,128]{3,2,1,0:T(8,128)} %refs_2_.7) | copy-start | bytes 1769476
  48.5 12.1 %copy-start.4 = (f32[1,24,48,128]{3,2,1,0:T(8,128)S(1)}, f32[1,24,48,128]{3,2,1,0:T(8,128)}, u32[]{:S(2)}) copy-start(f32[1,24,48,128]{3,2,1,0:T(8,128)} %refs_6_.1) | copy-start | bytes 1769476

commit v2 on v1

--- a/solution.py
+++ b/solution.py
@@ -79,6 +79,15 @@
 
 def next_b(ref, halo, b, count):
     return jnp.where(b == count - 1, halo, ref[0, jnp.minimum(b + 1, count - 1)])
+
+
+def pack_d(field, low, high, lane):
+    d = field.shape[1]
+    return jnp.where((lane == 0) | (lane == d - 1), field, pltpu.roll(jnp.where(lane == 0, low, high), d // 2, 1))
+
+
+def unpack_d(packed):
+    return pltpu.roll(packed, packed.shape[1] // 2, 1)
 
 
 def neighbours(ref, before_b, after_b, gz_before, gz_after, wa_before, wa_after, b, row, lane):
@@ -110,7 +119,7 @@
         else:
             u_refs[0][0, b] = r[0] * g
             u_refs[1][0, b] = r[1] * g
-        w_ref[0, b] = jnp.where(lane == 0, r[7] * g, r[6] * g)
+        w_ref[0, b] = pack_d(start[0, b], r[7] * g, r[6] * g, lane)
         gz_ref[0, pl.ds(b, 1), :] = start[0, b, c - 1 :, :]
         gz_ref[1, pl.ds(b, 1), :] = start[0, b, :1, :]
         gz_ref[2, pl.ds(b, 1), :] = (r[4] * g)[c - 1 :]
@@ -154,8 +163,8 @@
     out = out + jnp.where(b == count - 1, down[at], rates[3, 0, above] * g[0, above])
     out = out + prev_c(rates[4, 0, b] * own, gz_before[2 * at, pl.ds(b, 1), :], row)
     out = out + next_c(rates[5, 0, b] * own, gz_after[2 * at + 1, pl.ds(b, 1), :], row)
-    out = out + prev_d(rates[6, 0, b] * own, wa_before[0, b], lane)
-    out = out + next_d(rates[7, 0, b] * own, wa_after[0, b], lane)
+    out = out + prev_d(rates[6, 0, b] * own, unpack_d(wa_before[0, b]), lane)
+    out = out + next_d(rates[7, 0, b] * own, unpack_d(wa_after[0, b]), lane)
     return out
 
 
@@ -178,7 +187,7 @@
         else:
             v_refs[0][0, b] = rates[0, 0, b] * h
             v_refs[1][0, b] = rates[1, 0, b] * h
-        w_ref[0, b] = jnp.where(lane == 0, rates[7, 0, b] * h, rates[6, 0, b] * h)
+        w_ref[0, b] = pack_d(first[0, b], rates[7, 0, b] * h, rates[6, 0, b] * h, lane)
         gz_ref[0, pl.ds(b, 1), :] = first[0, b, c - 1 :, :]
         gz_ref[1, pl.ds(b, 1), :] = first[0, b, :1, :]
         gz_ref[2, pl.ds(b, 1), :] = (rates[4, 0, b] * h)[c - 1 :]
@@ -192,19 +201,8 @@
     down_ref[1] = rates[3, 0, 0] * h_ref[0, 0]
 
 
-def partial_body(rates, f_ref, back, h, up, down, gz_before, gz_after, wa_before, wa_after, out):
-    count, c, d = h.shape[1:]
-    row, lane = iotas(c, d)
-
-    def step(b, _):
-        out[0, b] = spread(rates, f_ref, back[0, b], h, up, down, gz_before, gz_after, wa_before, wa_after, 1, b, row, lane)
-        return 0
-
-    lax.fori_loop(0, count, step, 0)
-
-
 def last_body(rates, f_ref, labels, g, h, s_ref, start, start_before, start_after, up0, down0, gz_before0, gz_after0, wa_before0,
-              wa_after0, first, first_before, first_after, up1, down1, gz_before1, gz_after1, wa_before1, wa_after1, committor, out):
+              wa_after0, first, first_before, first_after, up1, down1, gz_before1, gz_after1, wa_before1, wa_after1, back, committor, out, partial):
     count, c, d = first.shape[1:]
     row, lane = iotas(c, d)
 
@@ -221,6 +219,7 @@
         gb, hb = g[0, b], h[0, b]
         for k in range(8):
             out[k, 0, b] = gb * (near1[k] - avg1) + hb * (near0[k] - avg0)
+        partial[0, b] = spread(rates, f_ref, back[0, b], h, up1, down1, gz_before1, gz_after1, wa_before1, wa_after1, 1, b, row, lane)
         return 0
 
     lax.fori_loop(0, count, step, 0)
@@ -241,8 +240,7 @@
     u_before, u_after = both_ways(u[0], u[-1], "grp")
     up0, down0 = both_ways(up, down, "gy")
     gz_before0, gz_after0 = both_ways(gz, gz, "gz")
-    wa0 = both_ways(start, start, "wa")
-    waw0 = both_ways(w0, w0, "wa")
+    wa0 = both_ways(w0, w0, "wa")
 
     first, s0 = call(
         functools.partial(forward_body, pair),
@@ -252,28 +250,26 @@
         30 * cells,
     )
     first_before, first_after = both_ways(first, first, "grp")
-    wa1 = both_ways(first, first, "wa")
 
     back, h, w1, up, down, gz, *v = call(
         functools.partial(back_body, pair),
         "backward",
-        [rates, f, cotangent, g, u_before, u_after, up0, down0, gz_before0, gz_after0, *waw0, first],
+        [rates, f, cotangent, g, u_before, u_after, up0, down0, gz_before0, gz_after0, *wa0, first],
         [block] * 3 + faces + blocks,
         30 * cells,
     )
     v_before, v_after = both_ways(v[0], v[-1], "grp")
     up1, down1 = both_ways(up, down, "gy")
     gz_before1, gz_after1 = both_ways(gz, gz, "gz")
-    waw1 = both_ways(w1, w1, "wa")
-
-    (grad,) = call(partial_body, "partial", [rates, f, back, h, up1, down1, gz_before1, gz_after1, *waw1], [block], 30 * cells)
-    committor, grad_rates = call(
+    wa1 = both_ways(w1, w1, "wa")
+
+    committor, grad_rates, grad = call(
         last_body,
         "last",
         [rates, f, labels, g, h, s0, start, start_before, start_after, up0, down0, gz_before0, gz_after0, *wa0,
-         first, first_before, first_after, up1, down1, gz_before1, gz_after1, *wa1],
-        [block, (8, 1, b, c, d)],
-        90 * cells,
+         first, first_before, first_after, up1, down1, gz_before1, gz_after1, *wa1, back],
+        [block, (8, 1, b, c, d), block],
+        120 * cells,
     )
     grad_start = grad + v_before if pair else grad + v_before + v_after
     return committor, grad_start, grad_rates

time: 66 us -> 56.3 us (0.85)
  waiting for transfers between devices: 29.6 us -> 14.7 us
  Pallas kernels: 12.3 us -> 15.9 us
  starting transfers between devices: 16.8 us -> 18.4 us
    ppermute x10 -> x8, waiting for transfers between devices: 17 us -> 10.4 us  [both_ways(): other = lax.ppermute(up, axis, ring(axis, 1))]
    ppermute x2, waiting for transfers between devices: 4.25 us -> 0.01 us  [both_ways(): lax.ppermute(down, axis, ring(axis, -1))]
    ppermute x2, waiting for transfers between devices: 8.3 us -> 4.3 us  [both_ways(): lax.ppermute(up, axis, ring(axis, 1))]
    pallas_call x5 -> x4, Pallas kernels: 12.3 us -> 15.9 us  [call(): pl.pallas_call(kernel, out_shape=[jax.ShapeDtypeStruct(s, jnp.float32) fo...]
    ppermute x10 -> x8, starting transfers between devices: 9.31 us -> 10.4 us  [both_ways(): other = lax.ppermute(up, axis, ring(axis, 1))]
    unnamed x12 -> x14, local copies, waits for them, and re-layouts: 5.54 us -> 5.54 us
  transfers between devices with their start and end apart: 14 -> 12, of which waited for: 8 -> 6; matrix products, arithmetic and copies ran while one was open for 1% -> 0% of each run, Pallas kernels for 7% -> 28%
where the time goes in v2:
time: 56.3 us; the launch traced here: 56 us
  starting transfers between devices  18.4 us (33%)
  Pallas kernels  15.9 us (28%)
  waiting for transfers between devices  14.7 us (26%)
  local copies, waits for them, and re-layouts  5.54 us (10%)
  other arithmetic  0.88 us (2%)
  between operations  0.68 us (1%)
    pallas_call x4, Pallas kernels, call(): pl.pallas_call(kernel, out_shape=[jax.ShapeDtypeStruct(s, jnp.float32) fo...  15.9 us
    ppermute x8, starting transfers between devices, both_ways(): other = lax.ppermute(up, axis, ring(axis, 1))  10.4 us
    ppermute x8, waiting for transfers between devices, both_ways(): other = lax.ppermute(up, axis, ring(axis, 1))  10.4 us
    unnamed x14, local copies, waits for them, and re-layouts  5.54 us
    ppermute x2, waiting for transfers between devices, both_ways(): lax.ppermute(up, axis, ring(axis, 1))  4.3 us
    ppermute x2, starting transfers between devices, both_ways(): lax.ppermute(down, axis, ring(axis, -1))  4.28 us
    ppermute x2, starting transfers between devices, both_ways(): lax.ppermute(up, axis, ring(axis, 1))  3.65 us
  transfers between devices with their start and end apart: 12, of which 6 were waited for; matrix products, arithmetic and copies ran while one was open for 0% of the time, Pallas kernels for 28%

profile of v2, /device:TPU:0, one launch (start us, length us, event | category | flops | bytes accessed | tf_op | source)
XLA Modules:
  0.0 56.0 jit_solution(3552271315876385419)
XLA Ops:
  0.6 3.0 %collective-permute-start.5 = (f32[1,24,48,128]{3,2,1,0:T(8,128)}, f32[1,24,48,128]{3,2,1,0:T(8,128)S(1)}, u32[]{:S(2)}, u32[]{:S(2)}) collective-permute-start(f32[1,24,48,128]{3,2,1,0:T(8,128)} %refs_6_.1), channel_id=1, source_target_pairs={{0,16},{16,0},{1,17},{17,1},{2,18},{18,2},{3,19},{19,3},{4,20},{20... | collective-permute-start | bytes 1769480 | tf_op jit(solution)/shard_map/ppermute | solution.py:21
  3.7 0.0 copy-start
  3.7 2.3 %copy-done = f32[8,1,24,48,128]{4,3,2,1,0:T(8,128)S(1)} copy-done((f32[8,1,24,48,128]{4,3,2,1,0:T(8,128)S(1)}, f32[8,1,24,48,128]{4,3,2,1,0:T(8,128)}, u32[]{:S(2)}) %copy-start) | copy-done | bytes 4718616
  6.0 0.0 copy-start.1
  6.0 1.1 %copy-done.1 = s32[1,24,48,128]{3,2,1,0:T(8,128)S(1)} copy-done((s32[1,24,48,128]{3,2,1,0:T(8,128)S(1)}, s32[1,24,48,128]{3,2,1,0:T(8,128)}, u32[]{:S(2)}) %copy-start.1) | copy-done | bytes 589848
  7.1 0.0 copy-start.3
  7.1 1.1 %copy-done.3 = f32[1,24,48,128]{3,2,1,0:T(8,128)S(1)} copy-done((f32[1,24,48,128]{3,2,1,0:T(8,128)S(1)}, f32[1,24,48,128]{3,2,1,0:T(8,128)}, u32[]{:S(2)}) %copy-start.3) | copy-done | bytes 589848
  8.1 0.0 copy-start.5
  8.1 1.1 %copy-done.5 = f32[1,24,48,128]{3,2,1,0:T(8,128)S(1)} copy-done((f32[1,24,48,128]{3,2,1,0:T(8,128)S(1)}, f32[1,24,48,128]{3,2,1,0:T(8,128)}, u32[]{:S(2)}) %copy-start.5) | copy-done | bytes 589848
  9.2 0.0 copy-start.4
  9.2 2.3 %prepare.1 = (f32[1,24,48,128]{3,2,1,0:T(8,128)S(1)}, f32[1,24,48,128]{3,2,1,0:T(8,128)S(1)}, f32[1,24,48,128]{3,2,1,0:T(8,128)S(1)}, f32[2,48,128]{2,1,0:T(8,12...) custom-call(f32[8,1,24,48,128]{4,3,2,1,0:T(8,128)S(1)} %copy-done, ...), custom_call_target="tpu_custom_call" | custom-call | flops 2949120 | bytes 8994816 | tf_op jit(solution)/shard_map/prepare/pallas_call | solution.py:42
  11.5 0.0 copy-start.6
  11.5 0.1 collective-permute-start.4
  11.6 0.1 collective-permute-start
  11.7 2.1 %collective-permute-start.1 = (f32[2,48,128]{2,1,0:T(8,128)S(1)}, f32[2,48,128]{2,1,0:T(8,128)S(1)}, u32[]{:S(2)}, u32[]{:S(2)}) collective-permute-start(f32[2,48,128]{2,1,0:T(8,128)S(1)} %get-tuple-element.25), channel_id=1, source_target_pairs={{0,4},{4,8},{8,12},{12,0},{1,5},{5,9},{9,13},{13,1},{2,6},{6,10},{... | collective-permute-start | bytes 147464 | tf_op jit(solution)/shard_map/ppermute | solution.py:23
  13.7 2.0 %collective-permute-start.2 = (f32[2,48,128]{2,1,0:T(8,128)S(1)}, f32[2,48,128]{2,1,0:T(8,128)S(1)}, u32[]{:S(2)}, u32[]{:S(2)}) collective-permute-start(f32[2,48,128]{2,1,0:T(8,128)S(1)} %get-tuple-element.26), channel_id=1, source_target_pairs={{0,12},{4,0},{8,4},{12,8},{1,13},{5,1},{9,5},{13,9},{2,14},{6,2},{... | collective-permute-start | bytes 147464 | tf_op jit(solution)/shard_map/ppermute | solution.py:23
  15.8 2.1 %collective-permute-done.1.refs_5_.refs_8_ = f32[2,48,128]{2,1,0:T(8,128)S(1)} collective-permute-done((f32[2,48,128]{2,1,0:T(8,128)S(1)}, f32[2,48,128]{2,1,0:T(8,128)S(1)}, u32[]{:S(2)}, u32[]{:S(2)}) %collective-permute-start.1) | collective-permute-done | bytes 49184 | tf_op jit(solution)/shard_map/ppermute | solution.py:23
  17.9 1.8 %collective-permute-start.3 = (f32[4,24,128]{2,1,0:T(8,128)S(1)}, f32[4,24,128]{2,1,0:T(8,128)S(1)}, u32[]{:S(2)}, u32[]{:S(2)}) collective-permute-start(f32[4,24,128]{2,1,0:T(8,128)S(1)} %get-tuple-element.27), channel_id=1, source_target_pairs={{0,2},{2,0},{1,3},{3,1},{4,6},{6,4},{5,7},{7,5},{8,10},{10,8},{9,1... | collective-permute-start | bytes 147464 | tf_op jit(solution)/shard_map/ppermute | solution.py:21
  19.6 0.0 collective-permute-done.2.refs_6_.refs_9_
  19.6 2.3 %collective-permute-done.3.refs_7_.refs_10_ = f32[4,24,128]{2,1,0:T(8,128)S(1)} collective-permute-done((f32[4,24,128]{2,1,0:T(8,128)S(1)}, f32[4,24,128]{2,1,0:T(8,128)S(1)}, u32[]{:S(2)}, u32[]{:S(2)}) %collective-permute-start.3) | collective-permute-done | bytes 49184 | tf_op jit(solution)/shard_map/ppermute | solution.py:21
  22.0 0.0 collective-permute-done.5.refs_4_.refs_7_
  22.0 0.0 collective-permute-done.4.refs_8_.refs_11_
  22.0 0.0 copy-done.4
  22.0 2.1 %forward.1 = (f32[1,24,48,128]{3,2,1,0:T(8,128)S(1)}, f32[1,24,48,128]{3,2,1,0:T(8,128)S(1)}) custom-call(f32[8,1,24,48,128]{4,3,2,1,0:T(8,128)S(1)} %copy-done, f32[1,24,48,128]{3,2,1,0:T(8,128)S(1)} %get-tuple-element.22.refs_1_, s32[1,24,48,128]{3,2,1,0:T(8,128)S(1)} %copy-done.1, f32[1,24,48,128]{3,2,1,0:T(8,128)S(1)} %copy-done.4, ...), custom_call_target="tpu_custom_call" | custom-call | flops 4423680 | bytes 8994816 | tf_op jit(solution)/shard_map/forward/pallas_call | solution.py:42
  24.1 0.0 copy-start.2
  24.1 1.9 %collective-permute-start.6 = (f32[1,24,48,128]{3,2,1,0:T(8,128)S(1)}, f32[1,24,48,128]{3,2,1,0:T(8,128)S(1)}, u32[]{:S(2)}, u32[]{:S(2)}) collective-permute-start(f32[1,24,48,128]{3,2,1,0:T(8,128)S(1)} %get-tuple-element.29.refs_9_.refs_12_), channel_id=1, source_target_pairs={{0,16},{16,0},{1,17},{17,1},{2,18},{18,2},{3,19},{19,3},{4,20},{20... | collective-permute-start | bytes 1769480 | tf_op jit(solution)/shard_map/ppermute | solution.py:21
  26.0 4.7 %collective-permute-done.refs_4_ = f32[1,24,48,128]{3,2,1,0:T(8,128)S(1)} collective-permute-done((f32[1,24,48,128]{3,2,1,0:T(8,128)S(1)}, f32[1,24,48,128]{3,2,1,0:T(8,128)S(1)}, u32[]{:S(2)}, u32[]{:S(2)}) %collective-permute-start) | collective-permute-done | bytes 589856 | tf_op jit(solution)/shard_map/ppermute | solution.py:21
  30.7 0.0 copy-done.6
  30.7 5.4 %backward.1 = (f32[1,24,48,128]{3,2,1,0:T(8,128)S(1)}, f32[1,24,48,128]{3,2,1,0:T(8,128)S(1)}, f32[1,24,48,128]{3,2,1,0:T(8,128)S(1)}, f32[2,48,128]{2,1,0:T(8,1...) custom-call(f32[8,1,24,48,128]{4,3,2,1,0:T(8,128)S(1)} %copy-done, ...), custom_call_target="tpu_custom_call" | custom-call | flops 4423680 | bytes 10911744 | tf_op jit(solution)/shard_map/backward/pallas_call | solution.py:42
  36.1 0.0 collective-permute-start.10
  36.1 2.1 %collective-permute-start.11 = (f32[1,24,48,128]{3,2,1,0:T(8,128)S(1)}, f32[1,24,48,128]{3,2,1,0:T(8,128)S(1)}, u32[]{:S(2)}, u32[]{:S(2)}) collective-permute-start(f32[1,24,48,128]{3,2,1,0:T(8,128)S(1)} %get-tuple-element.39), channel_id=1, source_target_pairs={{0,16},{16,0},{1,17},{17,1},{2,18},{18,2},{3,19},{19,3},{4,20},{20... | collective-permute-start | bytes 1769480 | tf_op jit(solution)/shard_map/ppermute | solution.py:21
  38.2 1.6 %collective-permute-start.7 = (f32[2,48,128]{2,1,0:T(8,128)S(1)}, f32[2,48,128]{2,1,0:T(8,128)S(1)}, u32[]{:S(2)}, u32[]{:S(2)}) collective-permute-start(f32[2,48,128]{2,1,0:T(8,128)S(1)} %get-tuple-element.32), channel_id=1, source_target_pairs={{0,4},{4,8},{8,12},{12,0},{1,5},{5,9},{9,13},{13,1},{2,6},{6,10},{... | collective-permute-start | bytes 147464 | tf_op jit(solution)/shard_map/ppermute | solution.py:23
  39.8 2.2 %collective-permute-start.8 = (f32[2,48,128]{2,1,0:T(8,128)S(1)}, f32[2,48,128]{2,1,0:T(8,128)S(1)}, u32[]{:S(2)}, u32[]{:S(2)}) collective-permute-start(f32[2,48,128]{2,1,0:T(8,128)S(1)} %get-tuple-element.33), channel_id=1, source_target_pairs={{0,12},{4,0},{8,4},{12,8},{1,13},{5,1},{9,5},{13,9},{2,14},{6,2},{... | collective-permute-start | bytes 147464 | tf_op jit(solution)/shard_map/ppermute | solution.py:23
  42.1 2.2 %collective-permute-done.7.refs_14_ = f32[2,48,128]{2,1,0:T(8,128)S(1)} collective-permute-done((f32[2,48,128]{2,1,0:T(8,128)S(1)}, f32[2,48,128]{2,1,0:T(8,128)S(1)}, u32[]{:S(2)}, u32[]{:S(2)}) %collective-permute-start.7) | collective-permute-done | bytes 49184 | tf_op jit(solution)/shard_map/ppermute | solution.py:23
  44.2 1.5 %collective-permute-start.9 = (f32[4,24,128]{2,1,0:T(8,128)S(1)}, f32[4,24,128]{2,1,0:T(8,128)S(1)}, u32[]{:S(2)}, u32[]{:S(2)}) collective-permute-start(f32[4,24,128]{2,1,0:T(8,128)S(1)} %get-tuple-element.34), channel_id=1, source_target_pairs={{0,2},{2,0},{1,3},{3,1},{4,6},{6,4},{5,7},{7,5},{8,10},{10,8},{9,1... | collective-permute-start | bytes 147464 | tf_op jit(solution)/shard_map/ppermute | solution.py:21
  45.7 0.0 collective-permute-done.8.refs_15_
  45.7 2.6 %collective-permute-done.9.refs_16_ = f32[4,24,128]{2,1,0:T(8,128)S(1)} collective-permute-done((f32[4,24,128]{2,1,0:T(8,128)S(1)}, f32[4,24,128]{2,1,0:T(8,128)S(1)}, u32[]{:S(2)}, u32[]{:S(2)}) %collective-permute-start.9) | collective-permute-done | bytes 49184 | tf_op jit(solution)/shard_map/ppermute | solution.py:21
  48.3 0.0 collective-permute-done.6.refs_13_
  48.3 0.0 collective-permute-done.10.refs_17_
  48.3 0.0 copy-done.2
  48.3 6.0 %last.1 = (f32[1,24,48,128]{3,2,1,0:T(8,128)}, f32[8,1,24,48,128]{4,3,2,1,0:T(8,128)}, f32[1,24,48,128]{3,2,1,0:T(8,128)S(1)}) custom-call(f32[8,1,24,48,128]{4,3,2,1,0:T(8,128)S(1)} %copy-done, f32[1,24,48,128]{3,2,1,0:T(8,128)S(1)} %get-tuple-element.22.refs_1_, s32[1,24,48,128]{3,2,1,0:T(8,128)S(1)} %copy-done.2, ...), custom_call_target="tpu_custom_call" | custom-call | flops 17694720 | bytes 17989632 | tf_op jit(solution)/shard_map/last/pallas_call | solution.py:42
  54.3 0.8 %collective-permute-done.11 = f32[1,24,48,128]{3,2,1,0:T(8,128)S(1)} collective-permute-done((f32[1,24,48,128]{3,2,1,0:T(8,128)S(1)}, f32[1,24,48,128]{3,2,1,0:T(8,128)S(1)}, u32[]{:S(2)}, u32[]{:S(2)}) %collective-permute-start.11) | collective-permute-done | bytes 589856 | tf_op jit(solution)/shard_map/ppermute | solution.py:21
  55.1 0.9 %add.3 = f32[1,24,48,128]{3,2,1,0:T(8,128)} add(f32[1,24,48,128]{3,2,1,0:T(8,128)S(1)} %get-tuple-element.38, f32[1,24,48,128]{3,2,1,0:T(8,128)S(1)} %collective-permute-done.11) | non-fusion elementwise | flops 147456 | bytes 1769472 | tf_op jit(solution)/shard_map/add | solution.py:274
Async XLA Ops:
  0.6 21.3 %collective-permute-start.5 = (f32[1,24,48,128]{3,2,1,0:T(8,128)}, f32[1,24,48,128]{3,2,1,0:T(8,128)S(1)}, u32[]{:S(2)}, u32[]{:S(2)}) collective-permute-start(f32[1,24,48,128]{3,2,1,0:T(8,128)} %refs_6_.1), channel_id=1, source_target_pairs={{0,16},{16,0},{1,17},{17,1},{2,18},{18,2},{3,19},{19,3},{4,20},{20... | collective-permute-start | bytes 1769480 | tf_op jit(solution)/shard_map/ppermute | solution.py:21
  3.7 2.3 %copy-start = (f32[8,1,24,48,128]{4,3,2,1,0:T(8,128)S(1)}, f32[8,1,24,48,128]{4,3,2,1,0:T(8,128)}, u32[]{:S(2)}) copy-start(f32[8,1,24,48,128]{4,3,2,1,0:T(8,128)} %refs_0_.7) | copy-start | bytes 14155780
  6.0 1.1 %copy-start.1 = (s32[1,24,48,128]{3,2,1,0:T(8,128)S(1)}, s32[1,24,48,128]{3,2,1,0:T(8,128)}, u32[]{:S(2)}) copy-start(s32[1,24,48,128]{3,2,1,0:T(8,128)} %refs_2_.7) | copy-start | bytes 1769476
  7.1 1.1 %copy-start.3 = (f32[1,24,48,128]{3,2,1,0:T(8,128)S(1)}, f32[1,24,48,128]{3,2,1,0:T(8,128)}, u32[]{:S(2)}) copy-start(f32[1,24,48,128]{3,2,1,0:T(8,128)} %refs_6_.1) | copy-start | bytes 1769476
  8.1 1.1 %copy-start.5 = (f32[1,24,48,128]{3,2,1,0:T(8,128)S(1)}, f32[1,24,48,128]{3,2,1,0:T(8,128)}, u32[]{:S(2)}) copy-start(f32[1,24,48,128]{3,2,1,0:T(8,128)} %refs_2_.6) | copy-start | bytes 1769476
  9.2 12.8 %copy-start.4 = (f32[1,24,48,128]{3,2,1,0:T(8,128)S(1)}, f32[1,24,48,128]{3,2,1,0:T(8,128)}, u32[]{:S(2)}) copy-start(f32[1,24,48,128]{3,2,1,0:T(8,128)} %refs_6_.1) | copy-start | bytes 1769476
  11.5 19.2 %copy-start.6 = (f32[1,24,48,128]{3,2,1,0:T(8,128)S(1)}, f32[1,24,48,128]{3,2,1,0:T(8,128)}, u32[]{:S(2)}) copy-start(f32[1,24,48,128]{3,2,1,0:T(8,128)} %refs_2_.6) | copy-start | bytes 1769476
  11.5 10.5 %collective-permute-start.4 = (f32[1,24,48,128]{3,2,1,0:T(8,128)S(1)}, f32[1,24,48,128]{3,2,1,0:T(8,128)S(1)}, u32[]{:S(2)}, u32[]{:S(2)}) collective-permute-start(f32[1,24,48,128]{3,2,1,0:T(8,128)S(1)} %get-tuple-element.28), channel_id=1, source_target_pairs={{0,1},{1,0},{2,3},{3,2},{4,5},{5,4},{6,7},{7,6},{8,9},{9,8},{10,11... | collective-permute-start | bytes 1769480 | tf_op jit(solution)/shard_map/ppermute | solution.py:21
  11.6 19.1 %collective-permute-start = (f32[1,24,48,128]{3,2,1,0:T(8,128)S(1)}, f32[1,24,48,128]{3,2,1,0:T(8,128)S(1)}, u32[]{:S(2)}, u32[]{:S(2)}) collective-permute-start(f32[1,24,48,128]{3,2,1,0:T(8,128)S(1)} %get-tuple-element.24), channel_id=1, source_target_pairs={{0,16},{16,0},{1,17},{17,1},{2,18},{18,2},{3,19},{19,3},{4,20},{20... | collective-permute-start | bytes 1769480 | tf_op jit(solution)/shard_map/ppermute | solution.py:21
  11.7 6.2 %collective-permute-start.1 = (f32[2,48,128]{2,1,0:T(8,128)S(1)}, f32[2,48,128]{2,1,0:T(8,128)S(1)}, u32[]{:S(2)}, u32[]{:S(2)}) collective-permute-start(f32[2,48,128]{2,1,0:T(8,128)S(1)} %get-tuple-element.25), channel_id=1, source_target_pairs={{0,4},{4,8},{8,12},{12,0},{1,5},{5,9},{9,13},{13,1},{2,6},{6,10},{... | collective-permute-start | bytes 147464 | tf_op jit(solution)/shard_map/ppermute | solution.py:23
  13.7 5.9 %collective-permute-start.2 = (f32[2,48,128]{2,1,0:T(8,128)S(1)}, f32[2,48,128]{2,1,0:T(8,128)S(1)}, u32[]{:S(2)}, u32[]{:S(2)}) collective-permute-start(f32[2,48,128]{2,1,0:T(8,128)S(1)} %get-tuple-element.26), channel_id=1, source_target_pairs={{0,12},{4,0},{8,4},{12,8},{1,13},{5,1},{9,5},{13,9},{2,14},{6,2},{... | collective-permute-start | bytes 147464 | tf_op jit(solution)/shard_map/ppermute | solution.py:23
  17.9 4.1 %collective-permute-start.3 = (f32[4,24,128]{2,1,0:T(8,128)S(1)}, f32[4,24,128]{2,1,0:T(8,128)S(1)}, u32[]{:S(2)}, u32[]{:S(2)}) collective-permute-start(f32[4,24,128]{2,1,0:T(8,128)S(1)} %get-tuple-element.27), channel_id=1, source_target_pairs={{0,2},{2,0},{1,3},{3,1},{4,6},{6,4},{5,7},{7,5},{8,10},{10,8},{9,1... | collective-permute-start | bytes 147464 | tf_op jit(solution)/shard_map/ppermute | solution.py:21
  24.1 24.2 %copy-start.2 = (s32[1,24,48,128]{3,2,1,0:T(8,128)S(1)}, s32[1,24,48,128]{3,2,1,0:T(8,128)}, u32[]{:S(2)}) copy-start(s32[1,24,48,128]{3,2,1,0:T(8,128)} %refs_2_.7) | copy-start | bytes 1769476
  24.1 24.2 %collective-permute-start.6 = (f32[1,24,48,128]{3,2,1,0:T(8,128)S(1)}, f32[1,24,48,128]{3,2,1,0:T(8,128)S(1)}, u32[]{:S(2)}, u32[]{:S(2)}) collective-permute-start(f32[1,24,48,128]{3,2,1,0:T(8,128)S(1)} %get-tuple-element.29.refs_9_.refs_12_), channel_id=1, source_target_pairs={{0,16},{16,0},{1,17},{17,1},{2,18},{18,2},{3,19},{19,3},{4,20},{20... | collective-permute-start | bytes 1769480 | tf_op jit(solution)/shard_map/ppermute | solution.py:21
  36.1 12.3 %collective-permute-start.10 = (f32[1,24,48,128]{3,2,1,0:T(8,128)S(1)}, f32[1,24,48,128]{3,2,1,0:T(8,128)S(1)}, u32[]{:S(2)}, u32[]{:S(2)}) collective-permute-start(f32[1,24,48,128]{3,2,1,0:T(8,128)S(1)} %get-tuple-element.35), channel_id=1, source_target_pairs={{0,1},{1,0},{2,3},{3,2},{4,5},{5,4},{6,7},{7,6},{8,9},{9,8},{10,11... | collective-permute-start | bytes 1769480 | tf_op jit(solution)/shard_map/ppermute | solution.py:21
  36.1 19.0 %collective-permute-start.11 = (f32[1,24,48,128]{3,2,1,0:T(8,128)S(1)}, f32[1,24,48,128]{3,2,1,0:T(8,128)S(1)}, u32[]{:S(2)}, u32[]{:S(2)}) collective-permute-start(f32[1,24,48,128]{3,2,1,0:T(8,128)S(1)} %get-tuple-element.39), channel_id=1, source_target_pairs={{0,16},{16,0},{1,17},{17,1},{2,18},{18,2},{3,19},{19,3},{4,20},{20... | collective-permute-start | bytes 1769480 | tf_op jit(solution)/shard_map/ppermute | solution.py:21
  38.2 6.0 %collective-permute-start.7 = (f32[2,48,128]{2,1,0:T(8,128)S(1)}, f32[2,48,128]{2,1,0:T(8,128)S(1)}, u32[]{:S(2)}, u32[]{:S(2)}) collective-permute-start(f32[2,48,128]{2,1,0:T(8,128)S(1)} %get-tuple-element.32), channel_id=1, source_target_pairs={{0,4},{4,8},{8,12},{12,0},{1,5},{5,9},{9,13},{13,1},{2,6},{6,10},{... | collective-permute-start | bytes 147464 | tf_op jit(solution)/shard_map/ppermute | solution.py:23
  39.8 5.9 %collective-permute-start.8 = (f32[2,48,128]{2,1,0:T(8,128)S(1)}, f32[2,48,128]{2,1,0:T(8,128)S(1)}, u32[]{:S(2)}, u32[]{:S(2)}) collective-permute-start(f32[2,48,128]{2,1,0:T(8,128)S(1)} %get-tuple-element.33), channel_id=1, source_target_pairs={{0,12},{4,0},{8,4},{12,8},{1,13},{5,1},{9,5},{13,9},{2,14},{6,2},{... | collective-permute-start | bytes 147464 | tf_op jit(solution)/shard_map/ppermute | solution.py:23
  44.2 4.1 %collective-permute-start.9 = (f32[4,24,128]{2,1,0:T(8,128)S(1)}, f32[4,24,128]{2,1,0:T(8,128)S(1)}, u32[]{:S(2)}, u32[]{:S(2)}) collective-permute-start(f32[4,24,128]{2,1,0:T(8,128)S(1)} %get-tuple-element.34), channel_id=1, source_target_pairs={{0,2},{2,0},{1,3},{3,1},{4,6},{6,4},{5,7},{7,5},{8,10},{10,8},{9,1... | collective-permute-start | bytes 147464 | tf_op jit(solution)/shard_map/ppermute | solution.py:21

commit v3 on v2

--- a/solution.py
+++ b/solution.py
@@ -48,6 +48,11 @@
         cost_estimate=pl.CostEstimate(flops=flops, bytes_accessed=moved, transcendentals=0),
         name=name,
     )(*unique)
+
+
+def rows(first, stop, step):
+    unroll = 4 if (stop - first) % 4 == 0 else 1
+    lax.fori_loop(first, stop, lambda b, _: step(b), None, unroll=unroll)
 
 
 def iotas(c, d):
@@ -107,7 +112,7 @@
     count, c, d = g_ref.shape[1:]
     row, lane = iotas(c, d)
 
-    def step(b, _):
+    def step(b):
         r = [rates[j, 0, b] for j in range(8)]
         total = ((r[0] + r[1]) + (r[2] + r[3])) + ((r[4] + r[5]) + (r[6] + r[7]))
         f = jnp.where(labels[0, b] == 0, DAMP / total, 0.0)
@@ -124,9 +129,8 @@
         gz_ref[1, pl.ds(b, 1), :] = start[0, b, :1, :]
         gz_ref[2, pl.ds(b, 1), :] = (r[4] * g)[c - 1 :]
         gz_ref[3, pl.ds(b, 1), :] = (r[5] * g)[:1]
-        return 0
-
-    lax.fori_loop(0, count, step, 0)
+
+    rows(0, count, step)
     up_ref[0] = start[0, count - 1]
     up_ref[1] = rates[2, 0, count - 1] * g_ref[0, count - 1]
     down_ref[0] = start[0, 0]
@@ -137,7 +141,7 @@
     count, c, d = q.shape[1:]
     row, lane = iotas(c, d)
 
-    def step(b, _):
+    def step(b):
         f = f_ref[0, b]
         near = neighbours(q, up, down, gz_before, gz_after, wa_before, wa_after, b, row, lane)
         total = sum(rates[2 + k, 0, b] * near[k] for k in range(6))
@@ -149,9 +153,8 @@
         label = labels[0, b]
         s_ref[0, b] = s
         first[0, b] = jnp.where(label == 0, KEEP * q[0, b] + s, jnp.where(label == 2, 1.0, 0.0))
-        return 0
-
-    lax.fori_loop(0, count, step, 0)
+
+    rows(0, count, step)
 
 
 def spread(rates, f_ref, x, g, up, down, gz_before, gz_after, wa_before, wa_after, at, b, row, lane):
@@ -173,7 +176,10 @@
     count, c, d = g.shape[1:]
     row, lane = iotas(c, d)
 
-    def step(b, _):
+    half = len(v_refs) // 2
+    cut = v_refs[0].shape[1]
+
+    def step(b, v, shift):
         out = spread(rates, f_ref, cot[0, b], g, up, down, gz_before, gz_after, wa_before, wa_after, 1, b, row, lane)
         if pair:
             out = out + u_before[0, b]
@@ -183,18 +189,18 @@
         back[0, b] = out
         h_ref[0, b] = h
         if pair:
-            v_refs[0][0, b] = (rates[0, 0, b] + rates[1, 0, b]) * h
-        else:
-            v_refs[0][0, b] = rates[0, 0, b] * h
-            v_refs[1][0, b] = rates[1, 0, b] * h
+            v[0][0, b - shift] = (rates[0, 0, b] + rates[1, 0, b]) * h
+        else:
+            v[0][0, b - shift] = rates[0, 0, b] * h
+            v[1][0, b - shift] = rates[1, 0, b] * h
         w_ref[0, b] = pack_d(first[0, b], rates[7, 0, b] * h, rates[6, 0, b] * h, lane)
         gz_ref[0, pl.ds(b, 1), :] = first[0, b, c - 1 :, :]
         gz_ref[1, pl.ds(b, 1), :] = first[0, b, :1, :]
         gz_ref[2, pl.ds(b, 1), :] = (rates[4, 0, b] * h)[c - 1 :]
         gz_ref[3, pl.ds(b, 1), :] = (rates[5, 0, b] * h)[:1]
-        return 0
-
-    lax.fori_loop(0, count, step, 0)
+
+    rows(0, cut, lambda b: step(b, v_refs[:half], 0))
+    rows(cut, count, lambda b: step(b, v_refs[half:], cut))
     up_ref[0] = first[0, count - 1]
     up_ref[1] = rates[2, 0, count - 1] * h_ref[0, count - 1]
     down_ref[0] = first[0, 0]
@@ -206,7 +212,7 @@
     count, c, d = first.shape[1:]
     row, lane = iotas(c, d)
 
-    def step(b, _):
+    def step(b):
         f = f_ref[0, b]
         near1 = [first_after[0, b], first_before[0, b]]
         near1 += neighbours(first, up1, down1, gz_before1, gz_after1, wa_before1, wa_after1, b, row, lane)
@@ -220,9 +226,35 @@
         for k in range(8):
             out[k, 0, b] = gb * (near1[k] - avg1) + hb * (near0[k] - avg0)
         partial[0, b] = spread(rates, f_ref, back[0, b], h, up1, down1, gz_before1, gz_after1, wa_before1, wa_after1, 1, b, row, lane)
-        return 0
-
-    lax.fori_loop(0, count, step, 0)
+
+    rows(0, count, step)
+
+
+def finish(done, grad, came, first):
+    parts = [came[0]] if came[0] is came[1] else list(came)
+    shape = came[0].shape
+
+    def kernel(*refs):
+        given, refs = refs[: done is not None], refs[done is not None :]
+        grad_ref, came_refs, (out, total, sem) = refs[0], refs[1:-3], refs[-3:]
+        acc = grad_ref[0, first : first + shape[1]]
+        for ref in came_refs:
+            acc = acc + ref[0]
+        total[...] = acc
+        copy = pltpu.make_async_copy(total, out.at[0, pl.ds(first, shape[1])], sem)
+        copy.start()
+        copy.wait()
+
+    given = [] if done is None else [done]
+    return pl.pallas_call(
+        kernel,
+        out_shape=jax.ShapeDtypeStruct(grad.shape, jnp.float32),
+        in_specs=[pl.BlockSpec(memory_space=pl.ANY)] * len(given) + [pl.BlockSpec(memory_space=pltpu.VMEM)] * (1 + len(parts)),
+        out_specs=pl.BlockSpec(memory_space=pl.ANY),
+        scratch_shapes=[pltpu.VMEM(shape[1:], jnp.float32), pltpu.SemaphoreType.DMA],
+        input_output_aliases={0: 0} if given else {},
+        name="finish",
+    )(*given, grad, *parts)
 
 
 def on_device(start, rates, labels, cotangent):
@@ -231,6 +263,7 @@
     cells = b * c * d
     pair = lax.axis_size("grp") == 2
     blocks = [block] * (1 if pair else 2)
+    tail = max(1, b // 6)
     faces = [(2, c, d), (2, c, d), (4, b, d)]
 
     start_before, start_after = both_ways(start, start, "grp")
@@ -255,10 +288,11 @@
         functools.partial(back_body, pair),
         "backward",
         [rates, f, cotangent, g, u_before, u_after, up0, down0, gz_before0, gz_after0, *wa0, first],
-        [block] * 3 + faces + blocks,
+        [block] * 3 + faces + [(1, b - tail, c, d)] * len(blocks) + [(1, tail, c, d)] * len(blocks),
         30 * cells,
     )
-    v_before, v_after = both_ways(v[0], v[-1], "grp")
+    most = both_ways(v[0], v[len(blocks) - 1], "grp")
+    rest = both_ways(v[len(blocks)], v[-1], "grp")
     up1, down1 = both_ways(up, down, "gy")
     gz_before1, gz_after1 = both_ways(gz, gz, "gz")
     wa1 = both_ways(w1, w1, "wa")
@@ -271,7 +305,7 @@
         [block, (8, 1, b, c, d), block],
         120 * cells,
     )
-    grad_start = grad + v_before if pair else grad + v_before + v_after
+    grad_start = finish(finish(None, grad, most, 0), grad, rest, b - tail)
     return committor, grad_start, grad_rates
 
 

time: 56.3 us -> 59.4 us (1.055)
  waiting for transfers between devices: 14.7 us -> 19.3 us
  Pallas kernels: 15.9 us -> 12.3 us
  local copies, waits for them, and re-layouts: 5.54 us -> 7.84 us
  other arithmetic: 0.88 us -> 0 us
    pallas_call x4, Pallas kernels: 15.9 us -> 8.55 us  [call(): pl.pallas_call(kernel, out_shape=[jax.ShapeDtypeStruct(s, jnp.float32) fo...]
    ppermute x8 -> x9, waiting for transfers between devices: 10.4 us -> 15 us  [both_ways(): other = lax.ppermute(up, axis, ring(axis, 1))]
    pallas_call x0 -> x2, Pallas kernels: none -> 3.77 us  [finish(): pl.pallas_call(kernel, out_shape=jax.ShapeDtypeStruct(grad.shape, jnp.flo...]
    unnamed x14 -> x20, local copies, waits for them, and re-layouts: 5.54 us -> 7.84 us
    add x1 -> x0, other arithmetic: 0.88 us -> none  [on_device(): grad_start = grad + v_before if pair else grad + v_before + v_after]
    ppermute x8 -> x9, starting transfers between devices: 10.4 us -> 11 us  [both_ways(): other = lax.ppermute(up, axis, ring(axis, 1))]
  transfers between devices with their start and end apart: 12 -> 13, of which waited for: 6 -> 6; matrix products, arithmetic and copies ran while one was open for 0% -> 0% of each run, Pallas kernels for 28% -> 18%
where the time goes in v3:
time: 59.4 us; the launch traced here: 59.1 us
  waiting for transfers between devices  19.3 us (32%)
  starting transfers between devices  18.9 us (32%)
  Pallas kernels  12.3 us (21%)
  local copies, waits for them, and re-layouts  7.84 us (13%)
  between operations  0.72 us (1%)
    ppermute x9, waiting for transfers between devices, both_ways(): other = lax.ppermute(up, axis, ring(axis, 1))  15 us
    ppermute x9, starting transfers between devices, both_ways(): other = lax.ppermute(up, axis, ring(axis, 1))  11 us
    pallas_call x4, Pallas kernels, call(): pl.pallas_call(kernel, out_shape=[jax.ShapeDtypeStruct(s, jnp.float32) fo...  8.55 us
    unnamed x20, local copies, waits for them, and re-layouts  7.84 us
    ppermute x2, waiting for transfers between devices, both_ways(): lax.ppermute(up, axis, ring(axis, 1))  4.3 us
    ppermute x2, starting transfers between devices, both_ways(): lax.ppermute(down, axis, ring(axis, -1))  4.28 us
    pallas_call x2, Pallas kernels, finish(): pl.pallas_call(kernel, out_shape=jax.ShapeDtypeStruct(grad.shape, jnp.flo...  3.77 us
    ppermute x2, starting transfers between devices, both_ways(): lax.ppermute(up, axis, ring(axis, 1))  3.65 us
  transfers between devices with their start and end apart: 13, of which 6 were waited for; matrix products, arithmetic and copies ran while one was open for 0% of the time, Pallas kernels for 18%

profile of v3, /device:TPU:0, one launch (start us, length us, event | category | flops | bytes accessed | tf_op | source)
XLA Modules:
  0.0 59.1 jit_solution(1158852572130122818)
XLA Ops:
  0.6 3.0 %collective-permute-start.5 = (f32[1,24,48,128]{3,2,1,0:T(8,128)}, f32[1,24,48,128]{3,2,1,0:T(8,128)S(1)}, u32[]{:S(2)}, u32[]{:S(2)}) collective-permute-start(f32[1,24,48,128]{3,2,1,0:T(8,128)} %refs_6_.1), channel_id=1, source_target_pairs={{0,16},{16,0},{1,17},{17,1},{2,18},{18,2},{3,19},{19,3},{4,20},{20... | collective-permute-start | bytes 1769480 | tf_op jit(solution)/shard_map/ppermute | solution.py:21
  3.7 0.0 copy-start
  3.7 2.3 %copy-done = f32[8,1,24,48,128]{4,3,2,1,0:T(8,128)S(1)} copy-done((f32[8,1,24,48,128]{4,3,2,1,0:T(8,128)S(1)}, f32[8,1,24,48,128]{4,3,2,1,0:T(8,128)}, u32[]{:S(2)}) %copy-start) | copy-done | bytes 4718616
  6.0 0.0 copy-start.1
  6.0 1.1 %copy-done.1 = s32[1,24,48,128]{3,2,1,0:T(8,128)S(1)} copy-done((s32[1,24,48,128]{3,2,1,0:T(8,128)S(1)}, s32[1,24,48,128]{3,2,1,0:T(8,128)}, u32[]{:S(2)}) %copy-start.1) | copy-done | bytes 589848
  7.1 0.0 copy-start.3
  7.1 1.1 %copy-done.3 = f32[1,24,48,128]{3,2,1,0:T(8,128)S(1)} copy-done((f32[1,24,48,128]{3,2,1,0:T(8,128)S(1)}, f32[1,24,48,128]{3,2,1,0:T(8,128)}, u32[]{:S(2)}) %copy-start.3) | copy-done | bytes 589848
  8.1 0.0 copy-start.5
  8.1 1.1 %copy-done.5 = f32[1,24,48,128]{3,2,1,0:T(8,128)S(1)} copy-done((f32[1,24,48,128]{3,2,1,0:T(8,128)S(1)}, f32[1,24,48,128]{3,2,1,0:T(8,128)}, u32[]{:S(2)}) %copy-start.5) | copy-done | bytes 589848
  9.2 0.0 copy-start.4
  9.2 0.8 %prepare.1 = (f32[1,24,48,128]{3,2,1,0:T(8,128)S(1)}, f32[1,24,48,128]{3,2,1,0:T(8,128)S(1)}, f32[1,24,48,128]{3,2,1,0:T(8,128)S(1)}, f32[2,48,128]{2,1,0:T(8,12...) custom-call(f32[8,1,24,48,128]{4,3,2,1,0:T(8,128)S(1)} %copy-done, ...), custom_call_target="tpu_custom_call" | custom-call | flops 2949120 | bytes 8994816 | tf_op jit(solution)/shard_map/prepare/pallas_call | solution.py:42
  10.0 0.0 copy-start.6
  10.0 0.1 collective-permute-start.4
  10.1 0.1 collective-permute-start
  10.2 2.1 %collective-permute-start.1 = (f32[2,48,128]{2,1,0:T(8,128)S(1)}, f32[2,48,128]{2,1,0:T(8,128)S(1)}, u32[]{:S(2)}, u32[]{:S(2)}) collective-permute-start(f32[2,48,128]{2,1,0:T(8,128)S(1)} %get-tuple-element.26), channel_id=1, source_target_pairs={{0,4},{4,8},{8,12},{12,0},{1,5},{5,9},{9,13},{13,1},{2,6},{6,10},{... | collective-permute-start | bytes 147464 | tf_op jit(solution)/shard_map/ppermute | solution.py:23
  12.3 2.0 %collective-permute-start.2 = (f32[2,48,128]{2,1,0:T(8,128)S(1)}, f32[2,48,128]{2,1,0:T(8,128)S(1)}, u32[]{:S(2)}, u32[]{:S(2)}) collective-permute-start(f32[2,48,128]{2,1,0:T(8,128)S(1)} %get-tuple-element.27), channel_id=1, source_target_pairs={{0,12},{4,0},{8,4},{12,8},{1,13},{5,1},{9,5},{13,9},{2,14},{6,2},{... | collective-permute-start | bytes 147464 | tf_op jit(solution)/shard_map/ppermute | solution.py:23
  14.3 2.1 %collective-permute-done.1.refs_5_.refs_8_ = f32[2,48,128]{2,1,0:T(8,128)S(1)} collective-permute-done((f32[2,48,128]{2,1,0:T(8,128)S(1)}, f32[2,48,128]{2,1,0:T(8,128)S(1)}, u32[]{:S(2)}, u32[]{:S(2)}) %collective-permute-start.1) | collective-permute-done | bytes 49184 | tf_op jit(solution)/shard_map/ppermute | solution.py:23
  16.4 1.8 %collective-permute-start.3 = (f32[4,24,128]{2,1,0:T(8,128)S(1)}, f32[4,24,128]{2,1,0:T(8,128)S(1)}, u32[]{:S(2)}, u32[]{:S(2)}) collective-permute-start(f32[4,24,128]{2,1,0:T(8,128)S(1)} %get-tuple-element.28), channel_id=1, source_target_pairs={{0,2},{2,0},{1,3},{3,1},{4,6},{6,4},{5,7},{7,5},{8,10},{10,8},{9,1... | collective-permute-start | bytes 147464 | tf_op jit(solution)/shard_map/ppermute | solution.py:21
  18.2 0.0 collective-permute-done.2.refs_6_.refs_9_
  18.2 2.3 %collective-permute-done.3.refs_7_.refs_10_ = f32[4,24,128]{2,1,0:T(8,128)S(1)} collective-permute-done((f32[4,24,128]{2,1,0:T(8,128)S(1)}, f32[4,24,128]{2,1,0:T(8,128)S(1)}, u32[]{:S(2)}, u32[]{:S(2)}) %collective-permute-start.3) | collective-permute-done | bytes 49184 | tf_op jit(solution)/shard_map/ppermute | solution.py:21
  20.5 0.0 collective-permute-done.5.refs_4_.refs_7_
  20.5 0.0 collective-permute-done.4.refs_8_.refs_11_
  20.5 0.0 copy-done.4
  20.5 0.9 %forward.1 = (f32[1,24,48,128]{3,2,1,0:T(8,128)S(1)}, f32[1,24,48,128]{3,2,1,0:T(8,128)S(1)}) custom-call(f32[8,1,24,48,128]{4,3,2,1,0:T(8,128)S(1)} %copy-done, f32[1,24,48,128]{3,2,1,0:T(8,128)S(1)} %get-tuple-element.23.refs_1_, s32[1,24,48,128]{3,2,1,0:T(8,128)S(1)} %copy-done.1, f32[1,24,48,128]{3,2,1,0:T(8,128)S(1)} %copy-done.4, ...), custom_call_target="tpu_custom_call" | custom-call | flops 4423680 | bytes 8994816 | tf_op jit(solution)/shard_map/forward/pallas_call | solution.py:42
  21.4 0.0 copy-start.2
  21.4 1.9 %collective-permute-start.6 = (f32[1,24,48,128]{3,2,1,0:T(8,128)S(1)}, f32[1,24,48,128]{3,2,1,0:T(8,128)S(1)}, u32[]{:S(2)}, u32[]{:S(2)}) collective-permute-start(f32[1,24,48,128]{3,2,1,0:T(8,128)S(1)} %get-tuple-element.30.refs_9_.refs_12_), channel_id=1, source_target_pairs={{0,16},{16,0},{1,17},{17,1},{2,18},{18,2},{3,19},{19,3},{4,20},{20... | collective-permute-start | bytes 1769480 | tf_op jit(solution)/shard_map/ppermute | solution.py:21
  23.2 7.4 %collective-permute-done.refs_4_ = f32[1,24,48,128]{3,2,1,0:T(8,128)S(1)} collective-permute-done((f32[1,24,48,128]{3,2,1,0:T(8,128)S(1)}, f32[1,24,48,128]{3,2,1,0:T(8,128)S(1)}, u32[]{:S(2)}, u32[]{:S(2)}) %collective-permute-start) | collective-permute-done | bytes 589856 | tf_op jit(solution)/shard_map/ppermute | solution.py:21
  30.7 0.0 copy-done.6
  30.7 1.6 %backward.1 = (f32[1,24,48,128]{3,2,1,0:T(8,128)S(1)}, f32[1,24,48,128]{3,2,1,0:T(8,128)S(1)}, f32[1,24,48,128]{3,2,1,0:T(8,128)S(1)}, f32[2,48,128]{2,1,0:T(8,1...) custom-call(f32[8,1,24,48,128]{4,3,2,1,0:T(8,128)S(1)} %copy-done, ...), custom_call_target="tpu_custom_call" | custom-call | flops 4423680 | bytes 10911744 | tf_op jit(solution)/shard_map/backward/pallas_call | solution.py:42
  32.3 0.1 collective-permute-start.10
  32.4 2.1 %collective-permute-start.11 = (f32[1,20,48,128]{3,2,1,0:T(8,128)S(1)}, f32[1,20,48,128]{3,2,1,0:T(8,128)S(1)}, u32[]{:S(2)}, u32[]{:S(2)}) collective-permute-start(f32[1,20,48,128]{3,2,1,0:T(8,128)S(1)} %get-tuple-element.40), channel_id=1, source_target_pairs={{0,16},{16,0},{1,17},{17,1},{2,18},{18,2},{3,19},{19,3},{4,20},{20... | collective-permute-start | bytes 1474568 | tf_op jit(solution)/shard_map/ppermute | solution.py:21
  34.5 1.6 %collective-permute-start.7 = (f32[2,48,128]{2,1,0:T(8,128)S(1)}, f32[2,48,128]{2,1,0:T(8,128)S(1)}, u32[]{:S(2)}, u32[]{:S(2)}) collective-permute-start(f32[2,48,128]{2,1,0:T(8,128)S(1)} %get-tuple-element.33), channel_id=1, source_target_pairs={{0,4},{4,8},{8,12},{12,0},{1,5},{5,9},{9,13},{13,1},{2,6},{6,10},{... | collective-permute-start | bytes 147464 | tf_op jit(solution)/shard_map/ppermute | solution.py:23
  36.1 2.2 %collective-permute-start.8 = (f32[2,48,128]{2,1,0:T(8,128)S(1)}, f32[2,48,128]{2,1,0:T(8,128)S(1)}, u32[]{:S(2)}, u32[]{:S(2)}) collective-permute-start(f32[2,48,128]{2,1,0:T(8,128)S(1)} %get-tuple-element.34), channel_id=1, source_target_pairs={{0,12},{4,0},{8,4},{12,8},{1,13},{5,1},{9,5},{13,9},{2,14},{6,2},{... | collective-permute-start | bytes 147464 | tf_op jit(solution)/shard_map/ppermute | solution.py:23
  38.3 2.2 %collective-permute-done.7.refs_14_ = f32[2,48,128]{2,1,0:T(8,128)S(1)} collective-permute-done((f32[2,48,128]{2,1,0:T(8,128)S(1)}, f32[2,48,128]{2,1,0:T(8,128)S(1)}, u32[]{:S(2)}, u32[]{:S(2)}) %collective-permute-start.7) | collective-permute-done | bytes 49184 | tf_op jit(solution)/shard_map/ppermute | solution.py:23
  40.5 0.2 collective-permute-start.12
  40.7 0.0 collective-permute-done.8.refs_15_
  40.7 1.8 %collective-permute-start.9 = (f32[4,24,128]{2,1,0:T(8,128)S(1)}, f32[4,24,128]{2,1,0:T(8,128)S(1)}, u32[]{:S(2)}, u32[]{:S(2)}) collective-permute-start(f32[4,24,128]{2,1,0:T(8,128)S(1)} %get-tuple-element.35), channel_id=1, source_target_pairs={{0,2},{2,0},{1,3},{3,1},{4,6},{6,4},{5,7},{7,5},{8,10},{10,8},{9,1... | collective-permute-start | bytes 147464 | tf_op jit(solution)/shard_map/ppermute | solution.py:21
  42.5 2.3 %collective-permute-done.9.refs_16_ = f32[4,24,128]{2,1,0:T(8,128)S(1)} collective-permute-done((f32[4,24,128]{2,1,0:T(8,128)S(1)}, f32[4,24,128]{2,1,0:T(8,128)S(1)}, u32[]{:S(2)}, u32[]{:S(2)}) %collective-permute-start.9) | collective-permute-done | bytes 49184 | tf_op jit(solution)/shard_map/ppermute | solution.py:21
  44.8 0.0 collective-permute-done.6.refs_13_
  44.8 0.0 collective-permute-done.10.refs_17_
  44.8 0.0 copy-done.2
  44.8 5.3 %last.1 = (f32[1,24,48,128]{3,2,1,0:T(8,128)}, f32[8,1,24,48,128]{4,3,2,1,0:T(8,128)}, f32[1,24,48,128]{3,2,1,0:T(8,128)S(1)}) custom-call(f32[8,1,24,48,128]{4,3,2,1,0:T(8,128)S(1)} %copy-done, f32[1,24,48,128]{3,2,1,0:T(8,128)S(1)} %get-tuple-element.23.refs_1_, s32[1,24,48,128]{3,2,1,0:T(8,128)S(1)} %copy-done.2, ...), custom_call_target="tpu_custom_call" | custom-call | flops 17694720 | bytes 17989632 | tf_op jit(solution)/shard_map/last/pallas_call | solution.py:42
  50.1 0.0 copy-start.7
  50.1 0.9 %copy-done.7 = f32[1,24,48,128]{3,2,1,0:T(8,128)} copy-done((f32[1,24,48,128]{3,2,1,0:T(8,128)}, f32[1,24,48,128]{3,2,1,0:T(8,128)S(1)}, u32[]{:S(2)}) %copy-start.7) | copy-done | bytes 589848
  51.0 2.9 %collective-permute-done.11.refs_1_ = f32[1,20,48,128]{3,2,1,0:T(8,128)S(1)} collective-permute-done((f32[1,20,48,128]{3,2,1,0:T(8,128)S(1)}, f32[1,20,48,128]{3,2,1,0:T(8,128)S(1)}, u32[]{:S(2)}, u32[]{:S(2)}) %collective-permute-start.11) | collective-permute-done | bytes 491552 | tf_op jit(solution)/shard_map/ppermute | solution.py:21
  53.8 0.0 copy-start.8
  53.8 0.8 %copy-done.8 = f32[1,20,48,128]{3,2,1,0:T(8,128)} copy-done((f32[1,20,48,128]{3,2,1,0:T(8,128)}, f32[1,20,48,128]{3,2,1,0:T(8,128)S(1)}, u32[]{:S(2)}) %copy-start.8) | copy-done | bytes 491544
  54.6 2.0 %finish.2.refs_0_ = f32[1,24,48,128]{3,2,1,0:T(8,128)} custom-call(f32[1,24,48,128]{3,2,1,0:T(8,128)} %copy-done.7, f32[1,20,48,128]{3,2,1,0:T(8,128)} %copy-done.8), custom_call_target="tpu_custom_call" | custom-call | tf_op jit(solution)/shard_map/finish/pallas_call | solution.py:249
  56.7 0.0 collective-permute-done.12.refs_2_
  56.7 0.0 copy-start.9
  56.7 0.6 %copy-done.9 = f32[1,4,48,128]{3,2,1,0:T(8,128)} copy-done((f32[1,4,48,128]{3,2,1,0:T(8,128)}, f32[1,4,48,128]{3,2,1,0:T(8,128)S(1)}, u32[]{:S(2)}) %copy-start.9) | copy-done | bytes 98328
  57.4 1.7 %finish.3 = f32[1,24,48,128]{3,2,1,0:T(8,128)} custom-call(f32[1,24,48,128]{3,2,1,0:T(8,128)} %finish.2.refs_0_, f32[1,24,48,128]{3,2,1,0:T(8,128)} %copy-done.7, f32[1,4,48,128]{3,2,1,0:T(8,128)} %copy-done.9), custom_call_target="tpu_custom_call", output_to_operand_aliasing={{}: (0, {})} | custom-call | tf_op jit(solution)/shard_map/finish/pallas_call | solution.py:249
Async XLA Ops:
  0.6 19.9 %collective-permute-start.5 = (f32[1,24,48,128]{3,2,1,0:T(8,128)}, f32[1,24,48,128]{3,2,1,0:T(8,128)S(1)}, u32[]{:S(2)}, u32[]{:S(2)}) collective-permute-start(f32[1,24,48,128]{3,2,1,0:T(8,128)} %refs_6_.1), channel_id=1, source_target_pairs={{0,16},{16,0},{1,17},{17,1},{2,18},{18,2},{3,19},{19,3},{4,20},{20... | collective-permute-start | bytes 1769480 | tf_op jit(solution)/shard_map/ppermute | solution.py:21
  3.7 2.3 %copy-start = (f32[8,1,24,48,128]{4,3,2,1,0:T(8,128)S(1)}, f32[8,1,24,48,128]{4,3,2,1,0:T(8,128)}, u32[]{:S(2)}) copy-start(f32[8,1,24,48,128]{4,3,2,1,0:T(8,128)} %refs_0_.7) | copy-start | bytes 14155780
  6.0 1.1 %copy-start.1 = (s32[1,24,48,128]{3,2,1,0:T(8,128)S(1)}, s32[1,24,48,128]{3,2,1,0:T(8,128)}, u32[]{:S(2)}) copy-start(s32[1,24,48,128]{3,2,1,0:T(8,128)} %refs_2_.7) | copy-start | bytes 1769476
  7.1 1.1 %copy-start.3 = (f32[1,24,48,128]{3,2,1,0:T(8,128)S(1)}, f32[1,24,48,128]{3,2,1,0:T(8,128)}, u32[]{:S(2)}) copy-start(f32[1,24,48,128]{3,2,1,0:T(8,128)} %refs_6_.1) | copy-start | bytes 1769476
  8.1 1.1 %copy-start.5 = (f32[1,24,48,128]{3,2,1,0:T(8,128)S(1)}, f32[1,24,48,128]{3,2,1,0:T(8,128)}, u32[]{:S(2)}) copy-start(f32[1,24,48,128]{3,2,1,0:T(8,128)} %refs_2_.6) | copy-start | bytes 1769476
  9.2 11.3 %copy-start.4 = (f32[1,24,48,128]{3,2,1,0:T(8,128)S(1)}, f32[1,24,48,128]{3,2,1,0:T(8,128)}, u32[]{:S(2)}) copy-start(f32[1,24,48,128]{3,2,1,0:T(8,128)} %refs_6_.1) | copy-start | bytes 1769476
  10.0 20.7 %copy-start.6 = (f32[1,24,48,128]{3,2,1,0:T(8,128)S(1)}, f32[1,24,48,128]{3,2,1,0:T(8,128)}, u32[]{:S(2)}) copy-start(f32[1,24,48,128]{3,2,1,0:T(8,128)} %refs_2_.6) | copy-start | bytes 1769476
  10.0 10.5 %collective-permute-start.4 = (f32[1,24,48,128]{3,2,1,0:T(8,128)S(1)}, f32[1,24,48,128]{3,2,1,0:T(8,128)S(1)}, u32[]{:S(2)}, u32[]{:S(2)}) collective-permute-start(f32[1,24,48,128]{3,2,1,0:T(8,128)S(1)} %get-tuple-element.29), channel_id=1, source_target_pairs={{0,1},{1,0},{2,3},{3,2},{4,5},{5,4},{6,7},{7,6},{8,9},{9,8},{10,11... | collective-permute-start | bytes 1769480 | tf_op jit(solution)/shard_map/ppermute | solution.py:21
  10.1 20.6 %collective-permute-start = (f32[1,24,48,128]{3,2,1,0:T(8,128)S(1)}, f32[1,24,48,128]{3,2,1,0:T(8,128)S(1)}, u32[]{:S(2)}, u32[]{:S(2)}) collective-permute-start(f32[1,24,48,128]{3,2,1,0:T(8,128)S(1)} %get-tuple-element.25), channel_id=1, source_target_pairs={{0,16},{16,0},{1,17},{17,1},{2,18},{18,2},{3,19},{19,3},{4,20},{20... | collective-permute-start | bytes 1769480 | tf_op jit(solution)/shard_map/ppermute | solution.py:21
  10.2 6.2 %collective-permute-start.1 = (f32[2,48,128]{2,1,0:T(8,128)S(1)}, f32[2,48,128]{2,1,0:T(8,128)S(1)}, u32[]{:S(2)}, u32[]{:S(2)}) collective-permute-start(f32[2,48,128]{2,1,0:T(8,128)S(1)} %get-tuple-element.26), channel_id=1, source_target_pairs={{0,4},{4,8},{8,12},{12,0},{1,5},{5,9},{9,13},{13,1},{2,6},{6,10},{... | collective-permute-start | bytes 147464 | tf_op jit(solution)/shard_map/ppermute | solution.py:23
  12.3 5.9 %collective-permute-start.2 = (f32[2,48,128]{2,1,0:T(8,128)S(1)}, f32[2,48,128]{2,1,0:T(8,128)S(1)}, u32[]{:S(2)}, u32[]{:S(2)}) collective-permute-start(f32[2,48,128]{2,1,0:T(8,128)S(1)} %get-tuple-element.27), channel_id=1, source_target_pairs={{0,12},{4,0},{8,4},{12,8},{1,13},{5,1},{9,5},{13,9},{2,14},{6,2},{... | collective-permute-start | bytes 147464 | tf_op jit(solution)/shard_map/ppermute | solution.py:23
  16.4 4.1 %collective-permute-start.3 = (f32[4,24,128]{2,1,0:T(8,128)S(1)}, f32[4,24,128]{2,1,0:T(8,128)S(1)}, u32[]{:S(2)}, u32[]{:S(2)}) collective-permute-start(f32[4,24,128]{2,1,0:T(8,128)S(1)} %get-tuple-element.28), channel_id=1, source_target_pairs={{0,2},{2,0},{1,3},{3,1},{4,6},{6,4},{5,7},{7,5},{8,10},{10,8},{9,1... | collective-permute-start | bytes 147464 | tf_op jit(solution)/shard_map/ppermute | solution.py:21
  21.4 23.5 %copy-start.2 = (s32[1,24,48,128]{3,2,1,0:T(8,128)S(1)}, s32[1,24,48,128]{3,2,1,0:T(8,128)}, u32[]{:S(2)}) copy-start(s32[1,24,48,128]{3,2,1,0:T(8,128)} %refs_2_.7) | copy-start | bytes 1769476
  21.4 23.5 %collective-permute-start.6 = (f32[1,24,48,128]{3,2,1,0:T(8,128)S(1)}, f32[1,24,48,128]{3,2,1,0:T(8,128)S(1)}, u32[]{:S(2)}, u32[]{:S(2)}) collective-permute-start(f32[1,24,48,128]{3,2,1,0:T(8,128)S(1)} %get-tuple-element.30.refs_9_.refs_12_), channel_id=1, source_target_pairs={{0,16},{16,0},{1,17},{17,1},{2,18},{18,2},{3,19},{19,3},{4,20},{20... | collective-permute-start | bytes 1769480 | tf_op jit(solution)/shard_map/ppermute | solution.py:21
  32.3 12.5 %collective-permute-start.10 = (f32[1,24,48,128]{3,2,1,0:T(8,128)S(1)}, f32[1,24,48,128]{3,2,1,0:T(8,128)S(1)}, u32[]{:S(2)}, u32[]{:S(2)}) collective-permute-start(f32[1,24,48,128]{3,2,1,0:T(8,128)S(1)} %get-tuple-element.36), channel_id=1, source_target_pairs={{0,1},{1,0},{2,3},{3,2},{4,5},{5,4},{6,7},{7,6},{8,9},{9,8},{10,11... | collective-permute-start | bytes 1769480 | tf_op jit(solution)/shard_map/ppermute | solution.py:21
  32.4 21.5 %collective-permute-start.11 = (f32[1,20,48,128]{3,2,1,0:T(8,128)S(1)}, f32[1,20,48,128]{3,2,1,0:T(8,128)S(1)}, u32[]{:S(2)}, u32[]{:S(2)}) collective-permute-start(f32[1,20,48,128]{3,2,1,0:T(8,128)S(1)} %get-tuple-element.40), channel_id=1, source_target_pairs={{0,16},{16,0},{1,17},{17,1},{2,18},{18,2},{3,19},{19,3},{4,20},{20... | collective-permute-start | bytes 1474568 | tf_op jit(solution)/shard_map/ppermute | solution.py:21
  34.5 6.0 %collective-permute-start.7 = (f32[2,48,128]{2,1,0:T(8,128)S(1)}, f32[2,48,128]{2,1,0:T(8,128)S(1)}, u32[]{:S(2)}, u32[]{:S(2)}) collective-permute-start(f32[2,48,128]{2,1,0:T(8,128)S(1)} %get-tuple-element.33), channel_id=1, source_target_pairs={{0,4},{4,8},{8,12},{12,0},{1,5},{5,9},{9,13},{13,1},{2,6},{6,10},{... | collective-permute-start | bytes 147464 | tf_op jit(solution)/shard_map/ppermute | solution.py:23
  36.1 4.7 %collective-permute-start.8 = (f32[2,48,128]{2,1,0:T(8,128)S(1)}, f32[2,48,128]{2,1,0:T(8,128)S(1)}, u32[]{:S(2)}, u32[]{:S(2)}) collective-permute-start(f32[2,48,128]{2,1,0:T(8,128)S(1)} %get-tuple-element.34), channel_id=1, source_target_pairs={{0,12},{4,0},{8,4},{12,8},{1,13},{5,1},{9,5},{13,9},{2,14},{6,2},{... | collective-permute-start | bytes 147464 | tf_op jit(solution)/shard_map/ppermute | solution.py:23
  40.5 16.2 %collective-permute-start.12 = (f32[1,4,48,128]{3,2,1,0:T(8,128)S(1)}, f32[1,4,48,128]{3,2,1,0:T(8,128)S(1)}, u32[]{:S(2)}, u32[]{:S(2)}) collective-permute-start(f32[1,4,48,128]{3,2,1,0:T(8,128)S(1)} %get-tuple-element.41), channel_id=1, source_target_pairs={{0,16},{16,0},{1,17},{17,1},{2,18},{18,2},{3,19},{19,3},{4,20},{20... | collective-permute-start | bytes 294920 | tf_op jit(solution)/shard_map/ppermute | solution.py:21
  40.7 4.1 %collective-permute-start.9 = (f32[4,24,128]{2,1,0:T(8,128)S(1)}, f32[4,24,128]{2,1,0:T(8,128)S(1)}, u32[]{:S(2)}, u32[]{:S(2)}) collective-permute-start(f32[4,24,128]{2,1,0:T(8,128)S(1)} %get-tuple-element.35), channel_id=1, source_target_pairs={{0,2},{2,0},{1,3},{3,1},{4,6},{6,4},{5,7},{7,5},{8,10},{10,8},{9,1... | collective-permute-start | bytes 147464 | tf_op jit(solution)/shard_map/ppermute | solution.py:21
  50.1 0.9 %copy-start.7 = (f32[1,24,48,128]{3,2,1,0:T(8,128)}, f32[1,24,48,128]{3,2,1,0:T(8,128)S(1)}, u32[]{:S(2)}) copy-start(f32[1,24,48,128]{3,2,1,0:T(8,128)S(1)} %get-tuple-element.39.refs_0_.refs_1_) | copy-start | bytes 1769476
  53.8 0.8 %copy-start.8 = (f32[1,20,48,128]{3,2,1,0:T(8,128)}, f32[1,20,48,128]{3,2,1,0:T(8,128)S(1)}, u32[]{:S(2)}) copy-start(f32[1,20,48,128]{3,2,1,0:T(8,128)S(1)} %collective-permute-done.11.refs_1_) | copy-start | bytes 1474564
  56.7 0.6 %copy-start.9 = (f32[1,4,48,128]{3,2,1,0:T(8,128)}, f32[1,4,48,128]{3,2,1,0:T(8,128)S(1)}, u32[]{:S(2)}) copy-start(f32[1,4,48,128]{3,2,1,0:T(8,128)S(1)} %collective-permute-done.12.refs_2_) | copy-start | bytes 294916

commit v4 on v3

--- a/solution.py
+++ b/solution.py
@@ -253,6 +253,7 @@
         out_specs=pl.BlockSpec(memory_space=pl.ANY),
         scratch_shapes=[pltpu.VMEM(shape[1:], jnp.float32), pltpu.SemaphoreType.DMA],
         input_output_aliases={0: 0} if given else {},
+        compiler_params=pltpu.CompilerParams(vmem_limit_bytes=4 * 1024 * 1024),
         name="finish",
     )(*given, grad, *parts)
 

time: 59.4 us -> 56.1 us (0.944)
  Pallas kernels: 12.3 us -> 10 us
  local copies, waits for them, and re-layouts: 7.84 us -> 5.54 us
  waiting for transfers between devices: 19.3 us -> 20.6 us
    unnamed x20 -> x14, local copies, waits for them, and re-layouts: 7.84 us -> 5.54 us
    pallas_call x2, Pallas kernels: 3.77 us -> 1.5 us  [finish(): pl.pallas_call(kernel, out_shape=jax.ShapeDtypeStruct(grad.shape, jnp.flo...]
    ppermute x9, waiting for transfers between devices: 15 us -> 16.3 us  [both_ways(): other = lax.ppermute(up, axis, ring(axis, 1))]
  transfers between devices with their start and end apart: 13 -> 13, of which waited for: 6 -> 7; matrix products, arithmetic and copies ran while one was open for 0% -> 0% of each run, Pallas kernels for 18% -> 17%
where the time goes in v4:
time: 56.1 us; the launch traced here: 55.8 us
  waiting for transfers between devices  20.6 us (37%)
  starting transfers between devices  18.9 us (34%)
  Pallas kernels  10 us (18%)
  local copies, waits for them, and re-layouts  5.54 us (10%)
  between operations  0.71 us (1%)
    ppermute x9, waiting for transfers between devices, both_ways(): other = lax.ppermute(up, axis, ring(axis, 1))  16.3 us
    ppermute x9, starting transfers between devices, both_ways(): other = lax.ppermute(up, axis, ring(axis, 1))  11 us
    pallas_call x4, Pallas kernels, call(): pl.pallas_call(kernel, out_shape=[jax.ShapeDtypeStruct(s, jnp.float32) fo...  8.55 us
    unnamed x14, local copies, waits for them, and re-layouts  5.54 us
    ppermute x2, waiting for transfers between devices, both_ways(): lax.ppermute(up, axis, ring(axis, 1))  4.3 us
    ppermute x2, starting transfers between devices, both_ways(): lax.ppermute(down, axis, ring(axis, -1))  4.28 us
    ppermute x2, starting transfers between devices, both_ways(): lax.ppermute(up, axis, ring(axis, 1))  3.65 us
    pallas_call x2, Pallas kernels, finish(): pl.pallas_call(kernel, out_shape=jax.ShapeDtypeStruct(grad.shape, jnp.flo...  1.5 us
  transfers between devices with their start and end apart: 13, of which 7 were waited for; matrix products, arithmetic and copies ran while one was open for 0% of the time, Pallas kernels for 17%

profile of v4, /device:TPU:0, one launch (start us, length us, event | category | flops | bytes accessed | tf_op | source)
XLA Modules:
  0.0 55.8 jit_solution(4683504713006879643)
XLA Ops:
  0.6 3.0 %collective-permute-start.5 = (f32[1,24,48,128]{3,2,1,0:T(8,128)}, f32[1,24,48,128]{3,2,1,0:T(8,128)S(1)}, u32[]{:S(2)}, u32[]{:S(2)}) collective-permute-start(f32[1,24,48,128]{3,2,1,0:T(8,128)} %refs_6_.1), channel_id=1, source_target_pairs={{0,16},{16,0},{1,17},{17,1},{2,18},{18,2},{3,19},{19,3},{4,20},{20... | collective-permute-start | bytes 1769480 | tf_op jit(solution)/shard_map/ppermute | solution.py:21
  3.7 0.0 copy-start
  3.7 2.3 %copy-done = f32[8,1,24,48,128]{4,3,2,1,0:T(8,128)S(1)} copy-done((f32[8,1,24,48,128]{4,3,2,1,0:T(8,128)S(1)}, f32[8,1,24,48,128]{4,3,2,1,0:T(8,128)}, u32[]{:S(2)}) %copy-start) | copy-done | bytes 4718616
  6.0 0.0 copy-start.1
  6.0 1.1 %copy-done.1 = s32[1,24,48,128]{3,2,1,0:T(8,128)S(1)} copy-done((s32[1,24,48,128]{3,2,1,0:T(8,128)S(1)}, s32[1,24,48,128]{3,2,1,0:T(8,128)}, u32[]{:S(2)}) %copy-start.1) | copy-done | bytes 589848
  7.1 0.0 copy-start.3
  7.1 1.1 %copy-done.3 = f32[1,24,48,128]{3,2,1,0:T(8,128)S(1)} copy-done((f32[1,24,48,128]{3,2,1,0:T(8,128)S(1)}, f32[1,24,48,128]{3,2,1,0:T(8,128)}, u32[]{:S(2)}) %copy-start.3) | copy-done | bytes 589848
  8.1 0.0 copy-start.5
  8.1 1.1 %copy-done.5 = f32[1,24,48,128]{3,2,1,0:T(8,128)S(1)} copy-done((f32[1,24,48,128]{3,2,1,0:T(8,128)S(1)}, f32[1,24,48,128]{3,2,1,0:T(8,128)}, u32[]{:S(2)}) %copy-start.5) | copy-done | bytes 589848
  9.2 0.0 copy-start.4
  9.2 0.8 %prepare.1 = (f32[1,24,48,128]{3,2,1,0:T(8,128)S(1)}, f32[1,24,48,128]{3,2,1,0:T(8,128)S(1)}, f32[1,24,48,128]{3,2,1,0:T(8,128)S(1)}, f32[2,48,128]{2,1,0:T(8,12...) custom-call(f32[8,1,24,48,128]{4,3,2,1,0:T(8,128)S(1)} %copy-done, ...), custom_call_target="tpu_custom_call" | custom-call | flops 2949120 | bytes 8994816 | tf_op jit(solution)/shard_map/prepare/pallas_call | solution.py:42
  10.0 0.0 copy-start.6
  10.0 0.1 collective-permute-start.4
  10.1 0.1 collective-permute-start
  10.2 2.1 %collective-permute-start.1 = (f32[2,48,128]{2,1,0:T(8,128)S(1)}, f32[2,48,128]{2,1,0:T(8,128)S(1)}, u32[]{:S(2)}, u32[]{:S(2)}) collective-permute-start(f32[2,48,128]{2,1,0:T(8,128)S(1)} %get-tuple-element.26), channel_id=1, source_target_pairs={{0,4},{4,8},{8,12},{12,0},{1,5},{5,9},{9,13},{13,1},{2,6},{6,10},{... | collective-permute-start | bytes 147464 | tf_op jit(solution)/shard_map/ppermute | solution.py:23
  12.3 2.0 %collective-permute-start.2 = (f32[2,48,128]{2,1,0:T(8,128)S(1)}, f32[2,48,128]{2,1,0:T(8,128)S(1)}, u32[]{:S(2)}, u32[]{:S(2)}) collective-permute-start(f32[2,48,128]{2,1,0:T(8,128)S(1)} %get-tuple-element.27), channel_id=1, source_target_pairs={{0,12},{4,0},{8,4},{12,8},{1,13},{5,1},{9,5},{13,9},{2,14},{6,2},{... | collective-permute-start | bytes 147464 | tf_op jit(solution)/shard_map/ppermute | solution.py:23
  14.3 2.1 %collective-permute-done.1.refs_5_.refs_8_ = f32[2,48,128]{2,1,0:T(8,128)S(1)} collective-permute-done((f32[2,48,128]{2,1,0:T(8,128)S(1)}, f32[2,48,128]{2,1,0:T(8,128)S(1)}, u32[]{:S(2)}, u32[]{:S(2)}) %collective-permute-start.1) | collective-permute-done | bytes 49184 | tf_op jit(solution)/shard_map/ppermute | solution.py:23
  16.4 1.8 %collective-permute-start.3 = (f32[4,24,128]{2,1,0:T(8,128)S(1)}, f32[4,24,128]{2,1,0:T(8,128)S(1)}, u32[]{:S(2)}, u32[]{:S(2)}) collective-permute-start(f32[4,24,128]{2,1,0:T(8,128)S(1)} %get-tuple-element.28), channel_id=1, source_target_pairs={{0,2},{2,0},{1,3},{3,1},{4,6},{6,4},{5,7},{7,5},{8,10},{10,8},{9,1... | collective-permute-start | bytes 147464 | tf_op jit(solution)/shard_map/ppermute | solution.py:21
  18.2 0.0 collective-permute-done.2.refs_6_.refs_9_
  18.2 2.3 %collective-permute-done.3.refs_7_.refs_10_ = f32[4,24,128]{2,1,0:T(8,128)S(1)} collective-permute-done((f32[4,24,128]{2,1,0:T(8,128)S(1)}, f32[4,24,128]{2,1,0:T(8,128)S(1)}, u32[]{:S(2)}, u32[]{:S(2)}) %collective-permute-start.3) | collective-permute-done | bytes 49184 | tf_op jit(solution)/shard_map/ppermute | solution.py:21
  20.5 0.0 collective-permute-done.5.refs_4_.refs_7_
  20.5 0.0 collective-permute-done.4.refs_8_.refs_11_
  20.5 0.0 copy-done.4
  20.5 0.9 %forward.1 = (f32[1,24,48,128]{3,2,1,0:T(8,128)S(1)}, f32[1,24,48,128]{3,2,1,0:T(8,128)S(1)}) custom-call(f32[8,1,24,48,128]{4,3,2,1,0:T(8,128)S(1)} %copy-done, f32[1,24,48,128]{3,2,1,0:T(8,128)S(1)} %get-tuple-element.23.refs_1_, s32[1,24,48,128]{3,2,1,0:T(8,128)S(1)} %copy-done.1, f32[1,24,48,128]{3,2,1,0:T(8,128)S(1)} %copy-done.4, ...), custom_call_target="tpu_custom_call" | custom-call | flops 4423680 | bytes 8994816 | tf_op jit(solution)/shard_map/forward/pallas_call | solution.py:42
  21.4 0.0 copy-start.2
  21.4 1.9 %collective-permute-start.6 = (f32[1,24,48,128]{3,2,1,0:T(8,128)S(1)}, f32[1,24,48,128]{3,2,1,0:T(8,128)S(1)}, u32[]{:S(2)}, u32[]{:S(2)}) collective-permute-start(f32[1,24,48,128]{3,2,1,0:T(8,128)S(1)} %get-tuple-element.30.refs_9_.refs_12_), channel_id=1, source_target_pairs={{0,16},{16,0},{1,17},{17,1},{2,18},{18,2},{3,19},{19,3},{4,20},{20... | collective-permute-start | bytes 1769480 | tf_op jit(solution)/shard_map/ppermute | solution.py:21
  23.2 7.4 %collective-permute-done.refs_4_ = f32[1,24,48,128]{3,2,1,0:T(8,128)S(1)} collective-permute-done((f32[1,24,48,128]{3,2,1,0:T(8,128)S(1)}, f32[1,24,48,128]{3,2,1,0:T(8,128)S(1)}, u32[]{:S(2)}, u32[]{:S(2)}) %collective-permute-start) | collective-permute-done | bytes 589856 | tf_op jit(solution)/shard_map/ppermute | solution.py:21
  30.7 0.0 copy-done.6
  30.7 1.6 %backward.1 = (f32[1,24,48,128]{3,2,1,0:T(8,128)S(1)}, f32[1,24,48,128]{3,2,1,0:T(8,128)S(1)}, f32[1,24,48,128]{3,2,1,0:T(8,128)S(1)}, f32[2,48,128]{2,1,0:T(8,1...) custom-call(f32[8,1,24,48,128]{4,3,2,1,0:T(8,128)S(1)} %copy-done, ...), custom_call_target="tpu_custom_call" | custom-call | flops 4423680 | bytes 10911744 | tf_op jit(solution)/shard_map/backward/pallas_call | solution.py:42
  32.3 0.1 collective-permute-start.10
  32.4 2.1 %collective-permute-start.11 = (f32[1,20,48,128]{3,2,1,0:T(8,128)S(1)}, f32[1,20,48,128]{3,2,1,0:T(8,128)S(1)}, u32[]{:S(2)}, u32[]{:S(2)}) collective-permute-start(f32[1,20,48,128]{3,2,1,0:T(8,128)S(1)} %get-tuple-element.40), channel_id=1, source_target_pairs={{0,16},{16,0},{1,17},{17,1},{2,18},{18,2},{3,19},{19,3},{4,20},{20... | collective-permute-start | bytes 1474568 | tf_op jit(solution)/shard_map/ppermute | solution.py:21
  34.5 1.6 %collective-permute-start.7 = (f32[2,48,128]{2,1,0:T(8,128)S(1)}, f32[2,48,128]{2,1,0:T(8,128)S(1)}, u32[]{:S(2)}, u32[]{:S(2)}) collective-permute-start(f32[2,48,128]{2,1,0:T(8,128)S(1)} %get-tuple-element.33), channel_id=1, source_target_pairs={{0,4},{4,8},{8,12},{12,0},{1,5},{5,9},{9,13},{13,1},{2,6},{6,10},{... | collective-permute-start | bytes 147464 | tf_op jit(solution)/shard_map/ppermute | solution.py:23
  36.1 2.2 %collective-permute-start.8 = (f32[2,48,128]{2,1,0:T(8,128)S(1)}, f32[2,48,128]{2,1,0:T(8,128)S(1)}, u32[]{:S(2)}, u32[]{:S(2)}) collective-permute-start(f32[2,48,128]{2,1,0:T(8,128)S(1)} %get-tuple-element.34), channel_id=1, source_target_pairs={{0,12},{4,0},{8,4},{12,8},{1,13},{5,1},{9,5},{13,9},{2,14},{6,2},{... | collective-permute-start | bytes 147464 | tf_op jit(solution)/shard_map/ppermute | solution.py:23
  38.3 2.2 %collective-permute-done.7.refs_14_ = f32[2,48,128]{2,1,0:T(8,128)S(1)} collective-permute-done((f32[2,48,128]{2,1,0:T(8,128)S(1)}, f32[2,48,128]{2,1,0:T(8,128)S(1)}, u32[]{:S(2)}, u32[]{:S(2)}) %collective-permute-start.7) | collective-permute-done | bytes 49184 | tf_op jit(solution)/shard_map/ppermute | solution.py:23
  40.5 0.2 collective-permute-start.12
  40.7 0.0 collective-permute-done.8.refs_15_
  40.7 1.8 %collective-permute-start.9 = (f32[4,24,128]{2,1,0:T(8,128)S(1)}, f32[4,24,128]{2,1,0:T(8,128)S(1)}, u32[]{:S(2)}, u32[]{:S(2)}) collective-permute-start(f32[4,24,128]{2,1,0:T(8,128)S(1)} %get-tuple-element.35), channel_id=1, source_target_pairs={{0,2},{2,0},{1,3},{3,1},{4,6},{6,4},{5,7},{7,5},{8,10},{10,8},{9,1... | collective-permute-start | bytes 147464 | tf_op jit(solution)/shard_map/ppermute | solution.py:21
  42.5 2.3 %collective-permute-done.9.refs_16_ = f32[4,24,128]{2,1,0:T(8,128)S(1)} collective-permute-done((f32[4,24,128]{2,1,0:T(8,128)S(1)}, f32[4,24,128]{2,1,0:T(8,128)S(1)}, u32[]{:S(2)}, u32[]{:S(2)}) %collective-permute-start.9) | collective-permute-done | bytes 49184 | tf_op jit(solution)/shard_map/ppermute | solution.py:21
  44.8 0.0 collective-permute-done.6.refs_13_
  44.8 0.0 collective-permute-done.10.refs_17_
  44.8 0.0 copy-done.2
  44.8 5.3 %last.1 = (f32[1,24,48,128]{3,2,1,0:T(8,128)}, f32[8,1,24,48,128]{4,3,2,1,0:T(8,128)}, f32[1,24,48,128]{3,2,1,0:T(8,128)S(1)}) custom-call(f32[8,1,24,48,128]{4,3,2,1,0:T(8,128)S(1)} %copy-done, f32[1,24,48,128]{3,2,1,0:T(8,128)S(1)} %get-tuple-element.23.refs_1_, s32[1,24,48,128]{3,2,1,0:T(8,128)S(1)} %copy-done.2, ...), custom_call_target="tpu_custom_call" | custom-call | flops 17694720 | bytes 17989632 | tf_op jit(solution)/shard_map/last/pallas_call | solution.py:42
  50.1 3.7 %collective-permute-done.11.refs_1_ = f32[1,20,48,128]{3,2,1,0:T(8,128)S(1)} collective-permute-done((f32[1,20,48,128]{3,2,1,0:T(8,128)S(1)}, f32[1,20,48,128]{3,2,1,0:T(8,128)S(1)}, u32[]{:S(2)}, u32[]{:S(2)}) %collective-permute-start.11) | collective-permute-done | bytes 491552 | tf_op jit(solution)/shard_map/ppermute | solution.py:21
  53.8 0.8 %finish.2.refs_0_ = f32[1,24,48,128]{3,2,1,0:T(8,128)} custom-call(f32[1,24,48,128]{3,2,1,0:T(8,128)S(1)} %get-tuple-element.39.refs_0_.refs_1_, f32[1,20,48,128]{3,2,1,0:T(8,128)S(1)} %collective-permute-done.11.refs_1_), custom_call_target="tpu_custom_call" | custom-call | tf_op jit(solution)/shard_map/finish/pallas_call | solution.py:249
  54.7 0.4 collective-permute-done.12.refs_2_
  55.1 0.7 %finish.3 = f32[1,24,48,128]{3,2,1,0:T(8,128)} custom-call(f32[1,24,48,128]{3,2,1,0:T(8,128)} %finish.2.refs_0_, f32[1,24,48,128]{3,2,1,0:T(8,128)S(1)} %get-tuple-element.39.refs_0_.refs_1_, f32[1,4,48,128]{3,2,1,0:T(8,128)S(1)} %collective-permute-done.12.refs_2_), custom_call_target="tpu_custom_call", output_to_operand_aliasing={{}: (0, {})} | custom-call | tf_op jit(solution)/shard_map/finish/pallas_call | solution.py:249
Async XLA Ops:
  0.6 19.9 %collective-permute-start.5 = (f32[1,24,48,128]{3,2,1,0:T(8,128)}, f32[1,24,48,128]{3,2,1,0:T(8,128)S(1)}, u32[]{:S(2)}, u32[]{:S(2)}) collective-permute-start(f32[1,24,48,128]{3,2,1,0:T(8,128)} %refs_6_.1), channel_id=1, source_target_pairs={{0,16},{16,0},{1,17},{17,1},{2,18},{18,2},{3,19},{19,3},{4,20},{20... | collective-permute-start | bytes 1769480 | tf_op jit(solution)/shard_map/ppermute | solution.py:21
  3.7 2.3 %copy-start = (f32[8,1,24,48,128]{4,3,2,1,0:T(8,128)S(1)}, f32[8,1,24,48,128]{4,3,2,1,0:T(8,128)}, u32[]{:S(2)}) copy-start(f32[8,1,24,48,128]{4,3,2,1,0:T(8,128)} %refs_0_.7) | copy-start | bytes 14155780
  6.0 1.1 %copy-start.1 = (s32[1,24,48,128]{3,2,1,0:T(8,128)S(1)}, s32[1,24,48,128]{3,2,1,0:T(8,128)}, u32[]{:S(2)}) copy-start(s32[1,24,48,128]{3,2,1,0:T(8,128)} %refs_2_.7) | copy-start | bytes 1769476
  7.1 1.1 %copy-start.3 = (f32[1,24,48,128]{3,2,1,0:T(8,128)S(1)}, f32[1,24,48,128]{3,2,1,0:T(8,128)}, u32[]{:S(2)}) copy-start(f32[1,24,48,128]{3,2,1,0:T(8,128)} %refs_6_.1) | copy-start | bytes 1769476
  8.1 1.1 %copy-start.5 = (f32[1,24,48,128]{3,2,1,0:T(8,128)S(1)}, f32[1,24,48,128]{3,2,1,0:T(8,128)}, u32[]{:S(2)}) copy-start(f32[1,24,48,128]{3,2,1,0:T(8,128)} %refs_2_.6) | copy-start | bytes 1769476
  9.2 11.3 %copy-start.4 = (f32[1,24,48,128]{3,2,1,0:T(8,128)S(1)}, f32[1,24,48,128]{3,2,1,0:T(8,128)}, u32[]{:S(2)}) copy-start(f32[1,24,48,128]{3,2,1,0:T(8,128)} %refs_6_.1) | copy-start | bytes 1769476
  10.0 20.7 %copy-start.6 = (f32[1,24,48,128]{3,2,1,0:T(8,128)S(1)}, f32[1,24,48,128]{3,2,1,0:T(8,128)}, u32[]{:S(2)}) copy-start(f32[1,24,48,128]{3,2,1,0:T(8,128)} %refs_2_.6) | copy-start | bytes 1769476
  10.0 10.5 %collective-permute-start.4 = (f32[1,24,48,128]{3,2,1,0:T(8,128)S(1)}, f32[1,24,48,128]{3,2,1,0:T(8,128)S(1)}, u32[]{:S(2)}, u32[]{:S(2)}) collective-permute-start(f32[1,24,48,128]{3,2,1,0:T(8,128)S(1)} %get-tuple-element.29), channel_id=1, source_target_pairs={{0,1},{1,0},{2,3},{3,2},{4,5},{5,4},{6,7},{7,6},{8,9},{9,8},{10,11... | collective-permute-start | bytes 1769480 | tf_op jit(solution)/shard_map/ppermute | solution.py:21
  10.1 20.6 %collective-permute-start = (f32[1,24,48,128]{3,2,1,0:T(8,128)S(1)}, f32[1,24,48,128]{3,2,1,0:T(8,128)S(1)}, u32[]{:S(2)}, u32[]{:S(2)}) collective-permute-start(f32[1,24,48,128]{3,2,1,0:T(8,128)S(1)} %get-tuple-element.25), channel_id=1, source_target_pairs={{0,16},{16,0},{1,17},{17,1},{2,18},{18,2},{3,19},{19,3},{4,20},{20... | collective-permute-start | bytes 1769480 | tf_op jit(solution)/shard_map/ppermute | solution.py:21
  10.2 6.2 %collective-permute-start.1 = (f32[2,48,128]{2,1,0:T(8,128)S(1)}, f32[2,48,128]{2,1,0:T(8,128)S(1)}, u32[]{:S(2)}, u32[]{:S(2)}) collective-permute-start(f32[2,48,128]{2,1,0:T(8,128)S(1)} %get-tuple-element.26), channel_id=1, source_target_pairs={{0,4},{4,8},{8,12},{12,0},{1,5},{5,9},{9,13},{13,1},{2,6},{6,10},{... | collective-permute-start | bytes 147464 | tf_op jit(solution)/shard_map/ppermute | solution.py:23
  12.3 5.9 %collective-permute-start.2 = (f32[2,48,128]{2,1,0:T(8,128)S(1)}, f32[2,48,128]{2,1,0:T(8,128)S(1)}, u32[]{:S(2)}, u32[]{:S(2)}) collective-permute-start(f32[2,48,128]{2,1,0:T(8,128)S(1)} %get-tuple-element.27), channel_id=1, source_target_pairs={{0,12},{4,0},{8,4},{12,8},{1,13},{5,1},{9,5},{13,9},{2,14},{6,2},{... | collective-permute-start | bytes 147464 | tf_op jit(solution)/shard_map/ppermute | solution.py:23
  16.4 4.1 %collective-permute-start.3 = (f32[4,24,128]{2,1,0:T(8,128)S(1)}, f32[4,24,128]{2,1,0:T(8,128)S(1)}, u32[]{:S(2)}, u32[]{:S(2)}) collective-permute-start(f32[4,24,128]{2,1,0:T(8,128)S(1)} %get-tuple-element.28), channel_id=1, source_target_pairs={{0,2},{2,0},{1,3},{3,1},{4,6},{6,4},{5,7},{7,5},{8,10},{10,8},{9,1... | collective-permute-start | bytes 147464 | tf_op jit(solution)/shard_map/ppermute | solution.py:21
  21.4 23.5 %copy-start.2 = (s32[1,24,48,128]{3,2,1,0:T(8,128)S(1)}, s32[1,24,48,128]{3,2,1,0:T(8,128)}, u32[]{:S(2)}) copy-start(s32[1,24,48,128]{3,2,1,0:T(8,128)} %refs_2_.7) | copy-start | bytes 1769476
  21.4 23.5 %collective-permute-start.6 = (f32[1,24,48,128]{3,2,1,0:T(8,128)S(1)}, f32[1,24,48,128]{3,2,1,0:T(8,128)S(1)}, u32[]{:S(2)}, u32[]{:S(2)}) collective-permute-start(f32[1,24,48,128]{3,2,1,0:T(8,128)S(1)} %get-tuple-element.30.refs_9_.refs_12_), channel_id=1, source_target_pairs={{0,16},{16,0},{1,17},{17,1},{2,18},{18,2},{3,19},{19,3},{4,20},{20... | collective-permute-start | bytes 1769480 | tf_op jit(solution)/shard_map/ppermute | solution.py:21
  32.3 12.5 %collective-permute-start.10 = (f32[1,24,48,128]{3,2,1,0:T(8,128)S(1)}, f32[1,24,48,128]{3,2,1,0:T(8,128)S(1)}, u32[]{:S(2)}, u32[]{:S(2)}) collective-permute-start(f32[1,24,48,128]{3,2,1,0:T(8,128)S(1)} %get-tuple-element.36), channel_id=1, source_target_pairs={{0,1},{1,0},{2,3},{3,2},{4,5},{5,4},{6,7},{7,6},{8,9},{9,8},{10,11... | collective-permute-start | bytes 1769480 | tf_op jit(solution)/shard_map/ppermute | solution.py:21
  32.4 21.5 %collective-permute-start.11 = (f32[1,20,48,128]{3,2,1,0:T(8,128)S(1)}, f32[1,20,48,128]{3,2,1,0:T(8,128)S(1)}, u32[]{:S(2)}, u32[]{:S(2)}) collective-permute-start(f32[1,20,48,128]{3,2,1,0:T(8,128)S(1)} %get-tuple-element.40), channel_id=1, source_target_pairs={{0,16},{16,0},{1,17},{17,1},{2,18},{18,2},{3,19},{19,3},{4,20},{20... | collective-permute-start | bytes 1474568 | tf_op jit(solution)/shard_map/ppermute | solution.py:21
  34.5 6.0 %collective-permute-start.7 = (f32[2,48,128]{2,1,0:T(8,128)S(1)}, f32[2,48,128]{2,1,0:T(8,128)S(1)}, u32[]{:S(2)}, u32[]{:S(2)}) collective-permute-start(f32[2,48,128]{2,1,0:T(8,128)S(1)} %get-tuple-element.33), channel_id=1, source_target_pairs={{0,4},{4,8},{8,12},{12,0},{1,5},{5,9},{9,13},{13,1},{2,6},{6,10},{... | collective-permute-start | bytes 147464 | tf_op jit(solution)/shard_map/ppermute | solution.py:23
  36.1 4.7 %collective-permute-start.8 = (f32[2,48,128]{2,1,0:T(8,128)S(1)}, f32[2,48,128]{2,1,0:T(8,128)S(1)}, u32[]{:S(2)}, u32[]{:S(2)}) collective-permute-start(f32[2,48,128]{2,1,0:T(8,128)S(1)} %get-tuple-element.34), channel_id=1, source_target_pairs={{0,12},{4,0},{8,4},{12,8},{1,13},{5,1},{9,5},{13,9},{2,14},{6,2},{... | collective-permute-start | bytes 147464 | tf_op jit(solution)/shard_map/ppermute | solution.py:23
  40.5 14.6 %collective-permute-start.12 = (f32[1,4,48,128]{3,2,1,0:T(8,128)S(1)}, f32[1,4,48,128]{3,2,1,0:T(8,128)S(1)}, u32[]{:S(2)}, u32[]{:S(2)}) collective-permute-start(f32[1,4,48,128]{3,2,1,0:T(8,128)S(1)} %get-tuple-element.41), channel_id=1, source_target_pairs={{0,16},{16,0},{1,17},{17,1},{2,18},{18,2},{3,19},{19,3},{4,20},{20... | collective-permute-start | bytes 294920 | tf_op jit(solution)/shard_map/ppermute | solution.py:21
  40.7 4.1 %collective-permute-start.9 = (f32[4,24,128]{2,1,0:T(8,128)S(1)}, f32[4,24,128]{2,1,0:T(8,128)S(1)}, u32[]{:S(2)}, u32[]{:S(2)}) collective-permute-start(f32[4,24,128]{2,1,0:T(8,128)S(1)} %get-tuple-element.35), channel_id=1, source_target_pairs={{0,2},{2,0},{1,3},{3,1},{4,6},{6,4},{5,7},{7,5},{8,10},{10,8},{9,1... | collective-permute-start | bytes 147464 | tf_op jit(solution)/shard_map/ppermute | solution.py:21

commit v5 on v4

--- a/solution.py
+++ b/solution.py
@@ -230,32 +230,29 @@
     rows(0, count, step)
 
 
-def finish(done, grad, came, first):
+def finish(grad, came):
     parts = [came[0]] if came[0] is came[1] else list(came)
     shape = came[0].shape
 
     def kernel(*refs):
-        given, refs = refs[: done is not None], refs[done is not None :]
         grad_ref, came_refs, (out, total, sem) = refs[0], refs[1:-3], refs[-3:]
-        acc = grad_ref[0, first : first + shape[1]]
+        acc = grad_ref[0, : shape[1]]
         for ref in came_refs:
             acc = acc + ref[0]
         total[...] = acc
-        copy = pltpu.make_async_copy(total, out.at[0, pl.ds(first, shape[1])], sem)
+        copy = pltpu.make_async_copy(total, out.at[0, pl.ds(0, shape[1])], sem)
         copy.start()
         copy.wait()
 
-    given = [] if done is None else [done]
     return pl.pallas_call(
         kernel,
         out_shape=jax.ShapeDtypeStruct(grad.shape, jnp.float32),
-        in_specs=[pl.BlockSpec(memory_space=pl.ANY)] * len(given) + [pl.BlockSpec(memory_space=pltpu.VMEM)] * (1 + len(parts)),
+        in_specs=[pl.BlockSpec(memory_space=pltpu.VMEM)] * (1 + len(parts)),
         out_specs=pl.BlockSpec(memory_space=pl.ANY),
         scratch_shapes=[pltpu.VMEM(shape[1:], jnp.float32), pltpu.SemaphoreType.DMA],
-        input_output_aliases={0: 0} if given else {},
         compiler_params=pltpu.CompilerParams(vmem_limit_bytes=4 * 1024 * 1024),
         name="finish",
-    )(*given, grad, *parts)
+    )(grad, *parts)
 
 
 def on_device(start, rates, labels, cotangent):
@@ -306,7 +303,10 @@
         [block, (8, 1, b, c, d), block],
         120 * cells,
     )
-    grad_start = finish(finish(None, grad, most, 0), grad, rest, b - tail)
+    last_rows = grad[:, b - tail :] + rest[0]
+    if not pair:
+        last_rows = last_rows + rest[1]
+    grad_start = lax.dynamic_update_slice(finish(grad, most), last_rows, (0, b - tail, 0, 0))
     return committor, grad_start, grad_rates
 
 

time: 56.1 us -> 56.1 us (level)
  other arithmetic: 0 us -> 0.65 us
  Pallas kernels: 10 us -> 9.38 us
    pallas_call x2 -> x1, Pallas kernels: 1.5 us -> 0.84 us  [finish(): pl.pallas_call(kernel, out_shape=jax.ShapeDtypeStruct(grad.shape, jnp.flo...]
    dynamic_update_slice x0 -> x1, other arithmetic: none -> 0.65 us  [on_device(): lax.dynamic_update_slice(finish(grad, most), last_rows, (0, b - tail, 0, 0))]
where the time goes in v5:
time: 56.1 us; the launch traced here: 55.8 us
  waiting for transfers between devices  20.6 us (37%)
  starting transfers between devices  18.9 us (34%)
  Pallas kernels  9.38 us (17%)
  local copies, waits for them, and re-layouts  5.54 us (10%)
  between operations  0.71 us (1%)
  other arithmetic  0.65 us (1%)
    ppermute x9, waiting for transfers between devices, both_ways(): other = lax.ppermute(up, axis, ring(axis, 1))  16.3 us
    ppermute x9, starting transfers between devices, both_ways(): other = lax.ppermute(up, axis, ring(axis, 1))  11 us
    pallas_call x4, Pallas kernels, call(): pl.pallas_call(kernel, out_shape=[jax.ShapeDtypeStruct(s, jnp.float32) fo...  8.55 us
    unnamed x14, local copies, waits for them, and re-layouts  5.54 us
    ppermute x2, waiting for transfers between devices, both_ways(): lax.ppermute(up, axis, ring(axis, 1))  4.3 us
    ppermute x2, starting transfers between devices, both_ways(): lax.ppermute(down, axis, ring(axis, -1))  4.28 us
    ppermute x2, starting transfers between devices, both_ways(): lax.ppermute(up, axis, ring(axis, 1))  3.65 us
  transfers between devices with their start and end apart: 13, of which 7 were waited for; matrix products, arithmetic and copies ran while one was open for 0% of the time, Pallas kernels for 17%

profile of v5, /device:TPU:0, one launch (start us, length us, event | category | flops | bytes accessed | tf_op | source)
XLA Modules:
  0.0 55.8 jit_solution(12729716830528667150)
XLA Ops:
  0.6 3.0 %collective-permute-start.5 = (f32[1,24,48,128]{3,2,1,0:T(8,128)}, f32[1,24,48,128]{3,2,1,0:T(8,128)S(1)}, u32[]{:S(2)}, u32[]{:S(2)}) collective-permute-start(f32[1,24,48,128]{3,2,1,0:T(8,128)} %refs_6_.1), channel_id=1, source_target_pairs={{0,16},{16,0},{1,17},{17,1},{2,18},{18,2},{3,19},{19,3},{4,20},{20... | collective-permute-start | bytes 1769480 | tf_op jit(solution)/shard_map/ppermute | solution.py:21
  3.7 0.0 copy-start
  3.7 2.3 %copy-done = f32[8,1,24,48,128]{4,3,2,1,0:T(8,128)S(1)} copy-done((f32[8,1,24,48,128]{4,3,2,1,0:T(8,128)S(1)}, f32[8,1,24,48,128]{4,3,2,1,0:T(8,128)}, u32[]{:S(2)}) %copy-start) | copy-done | bytes 4718616
  6.0 0.0 copy-start.1
  6.0 1.1 %copy-done.1 = s32[1,24,48,128]{3,2,1,0:T(8,128)S(1)} copy-done((s32[1,24,48,128]{3,2,1,0:T(8,128)S(1)}, s32[1,24,48,128]{3,2,1,0:T(8,128)}, u32[]{:S(2)}) %copy-start.1) | copy-done | bytes 589848
  7.1 0.0 copy-start.3
  7.1 1.1 %copy-done.3 = f32[1,24,48,128]{3,2,1,0:T(8,128)S(1)} copy-done((f32[1,24,48,128]{3,2,1,0:T(8,128)S(1)}, f32[1,24,48,128]{3,2,1,0:T(8,128)}, u32[]{:S(2)}) %copy-start.3) | copy-done | bytes 589848
  8.1 0.0 copy-start.5
  8.1 1.1 %copy-done.5 = f32[1,24,48,128]{3,2,1,0:T(8,128)S(1)} copy-done((f32[1,24,48,128]{3,2,1,0:T(8,128)S(1)}, f32[1,24,48,128]{3,2,1,0:T(8,128)}, u32[]{:S(2)}) %copy-start.5) | copy-done | bytes 589848
  9.2 0.0 copy-start.4
  9.2 0.8 %prepare.1 = (f32[1,24,48,128]{3,2,1,0:T(8,128)S(1)}, f32[1,24,48,128]{3,2,1,0:T(8,128)S(1)}, f32[1,24,48,128]{3,2,1,0:T(8,128)S(1)}, f32[2,48,128]{2,1,0:T(8,12...) custom-call(f32[8,1,24,48,128]{4,3,2,1,0:T(8,128)S(1)} %copy-done, ...), custom_call_target="tpu_custom_call" | custom-call | flops 2949120 | bytes 8994816 | tf_op jit(solution)/shard_map/prepare/pallas_call | solution.py:42
  10.0 0.0 copy-start.6
  10.0 0.1 collective-permute-start.4
  10.1 0.1 collective-permute-start
  10.2 2.1 %collective-permute-start.1 = (f32[2,48,128]{2,1,0:T(8,128)S(1)}, f32[2,48,128]{2,1,0:T(8,128)S(1)}, u32[]{:S(2)}, u32[]{:S(2)}) collective-permute-start(f32[2,48,128]{2,1,0:T(8,128)S(1)} %get-tuple-element.26), channel_id=1, source_target_pairs={{0,4},{4,8},{8,12},{12,0},{1,5},{5,9},{9,13},{13,1},{2,6},{6,10},{... | collective-permute-start | bytes 147464 | tf_op jit(solution)/shard_map/ppermute | solution.py:23
  12.3 2.0 %collective-permute-start.2 = (f32[2,48,128]{2,1,0:T(8,128)S(1)}, f32[2,48,128]{2,1,0:T(8,128)S(1)}, u32[]{:S(2)}, u32[]{:S(2)}) collective-permute-start(f32[2,48,128]{2,1,0:T(8,128)S(1)} %get-tuple-element.27), channel_id=1, source_target_pairs={{0,12},{4,0},{8,4},{12,8},{1,13},{5,1},{9,5},{13,9},{2,14},{6,2},{... | collective-permute-start | bytes 147464 | tf_op jit(solution)/shard_map/ppermute | solution.py:23
  14.3 2.1 %collective-permute-done.1.refs_5_.refs_8_ = f32[2,48,128]{2,1,0:T(8,128)S(1)} collective-permute-done((f32[2,48,128]{2,1,0:T(8,128)S(1)}, f32[2,48,128]{2,1,0:T(8,128)S(1)}, u32[]{:S(2)}, u32[]{:S(2)}) %collective-permute-start.1) | collective-permute-done | bytes 49184 | tf_op jit(solution)/shard_map/ppermute | solution.py:23
  16.4 1.8 %collective-permute-start.3 = (f32[4,24,128]{2,1,0:T(8,128)S(1)}, f32[4,24,128]{2,1,0:T(8,128)S(1)}, u32[]{:S(2)}, u32[]{:S(2)}) collective-permute-start(f32[4,24,128]{2,1,0:T(8,128)S(1)} %get-tuple-element.28), channel_id=1, source_target_pairs={{0,2},{2,0},{1,3},{3,1},{4,6},{6,4},{5,7},{7,5},{8,10},{10,8},{9,1... | collective-permute-start | bytes 147464 | tf_op jit(solution)/shard_map/ppermute | solution.py:21
  18.2 0.0 collective-permute-done.2.refs_6_.refs_9_
  18.2 2.3 %collective-permute-done.3.refs_7_.refs_10_ = f32[4,24,128]{2,1,0:T(8,128)S(1)} collective-permute-done((f32[4,24,128]{2,1,0:T(8,128)S(1)}, f32[4,24,128]{2,1,0:T(8,128)S(1)}, u32[]{:S(2)}, u32[]{:S(2)}) %collective-permute-start.3) | collective-permute-done | bytes 49184 | tf_op jit(solution)/shard_map/ppermute | solution.py:21
  20.5 0.0 collective-permute-done.5.refs_4_.refs_7_
  20.5 0.0 collective-permute-done.4.refs_8_.refs_11_
  20.5 0.0 copy-done.4
  20.5 0.9 %forward.1 = (f32[1,24,48,128]{3,2,1,0:T(8,128)S(1)}, f32[1,24,48,128]{3,2,1,0:T(8,128)S(1)}) custom-call(f32[8,1,24,48,128]{4,3,2,1,0:T(8,128)S(1)} %copy-done, f32[1,24,48,128]{3,2,1,0:T(8,128)S(1)} %get-tuple-element.23.refs_1_, s32[1,24,48,128]{3,2,1,0:T(8,128)S(1)} %copy-done.1, f32[1,24,48,128]{3,2,1,0:T(8,128)S(1)} %copy-done.4, ...), custom_call_target="tpu_custom_call" | custom-call | flops 4423680 | bytes 8994816 | tf_op jit(solution)/shard_map/forward/pallas_call | solution.py:42
  21.4 0.0 copy-start.2
  21.4 1.9 %collective-permute-start.6 = (f32[1,24,48,128]{3,2,1,0:T(8,128)S(1)}, f32[1,24,48,128]{3,2,1,0:T(8,128)S(1)}, u32[]{:S(2)}, u32[]{:S(2)}) collective-permute-start(f32[1,24,48,128]{3,2,1,0:T(8,128)S(1)} %get-tuple-element.30.refs_9_.refs_12_), channel_id=1, source_target_pairs={{0,16},{16,0},{1,17},{17,1},{2,18},{18,2},{3,19},{19,3},{4,20},{20... | collective-permute-start | bytes 1769480 | tf_op jit(solution)/shard_map/ppermute | solution.py:21
  23.2 7.4 %collective-permute-done.refs_4_ = f32[1,24,48,128]{3,2,1,0:T(8,128)S(1)} collective-permute-done((f32[1,24,48,128]{3,2,1,0:T(8,128)S(1)}, f32[1,24,48,128]{3,2,1,0:T(8,128)S(1)}, u32[]{:S(2)}, u32[]{:S(2)}) %collective-permute-start) | collective-permute-done | bytes 589856 | tf_op jit(solution)/shard_map/ppermute | solution.py:21
  30.7 0.0 copy-done.6
  30.7 1.6 %backward.1 = (f32[1,24,48,128]{3,2,1,0:T(8,128)S(1)}, f32[1,24,48,128]{3,2,1,0:T(8,128)S(1)}, f32[1,24,48,128]{3,2,1,0:T(8,128)S(1)}, f32[2,48,128]{2,1,0:T(8,1...) custom-call(f32[8,1,24,48,128]{4,3,2,1,0:T(8,128)S(1)} %copy-done, ...), custom_call_target="tpu_custom_call" | custom-call | flops 4423680 | bytes 10911744 | tf_op jit(solution)/shard_map/backward/pallas_call | solution.py:42
  32.3 0.1 collective-permute-start.10
  32.4 2.1 %collective-permute-start.11 = (f32[1,20,48,128]{3,2,1,0:T(8,128)S(1)}, f32[1,20,48,128]{3,2,1,0:T(8,128)S(1)}, u32[]{:S(2)}, u32[]{:S(2)}) collective-permute-start(f32[1,20,48,128]{3,2,1,0:T(8,128)S(1)} %get-tuple-element.40), channel_id=1, source_target_pairs={{0,16},{16,0},{1,17},{17,1},{2,18},{18,2},{3,19},{19,3},{4,20},{20... | collective-permute-start | bytes 1474568 | tf_op jit(solution)/shard_map/ppermute | solution.py:21
  34.5 1.6 %collective-permute-start.7 = (f32[2,48,128]{2,1,0:T(8,128)S(1)}, f32[2,48,128]{2,1,0:T(8,128)S(1)}, u32[]{:S(2)}, u32[]{:S(2)}) collective-permute-start(f32[2,48,128]{2,1,0:T(8,128)S(1)} %get-tuple-element.33), channel_id=1, source_target_pairs={{0,4},{4,8},{8,12},{12,0},{1,5},{5,9},{9,13},{13,1},{2,6},{6,10},{... | collective-permute-start | bytes 147464 | tf_op jit(solution)/shard_map/ppermute | solution.py:23
  36.1 2.2 %collective-permute-start.8 = (f32[2,48,128]{2,1,0:T(8,128)S(1)}, f32[2,48,128]{2,1,0:T(8,128)S(1)}, u32[]{:S(2)}, u32[]{:S(2)}) collective-permute-start(f32[2,48,128]{2,1,0:T(8,128)S(1)} %get-tuple-element.34), channel_id=1, source_target_pairs={{0,12},{4,0},{8,4},{12,8},{1,13},{5,1},{9,5},{13,9},{2,14},{6,2},{... | collective-permute-start | bytes 147464 | tf_op jit(solution)/shard_map/ppermute | solution.py:23
  38.3 2.2 %collective-permute-done.7.refs_14_ = f32[2,48,128]{2,1,0:T(8,128)S(1)} collective-permute-done((f32[2,48,128]{2,1,0:T(8,128)S(1)}, f32[2,48,128]{2,1,0:T(8,128)S(1)}, u32[]{:S(2)}, u32[]{:S(2)}) %collective-permute-start.7) | collective-permute-done | bytes 49184 | tf_op jit(solution)/shard_map/ppermute | solution.py:23
  40.5 0.2 collective-permute-start.12
  40.7 0.0 collective-permute-done.8.refs_15_
  40.7 1.8 %collective-permute-start.9 = (f32[4,24,128]{2,1,0:T(8,128)S(1)}, f32[4,24,128]{2,1,0:T(8,128)S(1)}, u32[]{:S(2)}, u32[]{:S(2)}) collective-permute-start(f32[4,24,128]{2,1,0:T(8,128)S(1)} %get-tuple-element.35), channel_id=1, source_target_pairs={{0,2},{2,0},{1,3},{3,1},{4,6},{6,4},{5,7},{7,5},{8,10},{10,8},{9,1... | collective-permute-start | bytes 147464 | tf_op jit(solution)/shard_map/ppermute | solution.py:21
  42.5 2.3 %collective-permute-done.9.refs_16_ = f32[4,24,128]{2,1,0:T(8,128)S(1)} collective-permute-done((f32[4,24,128]{2,1,0:T(8,128)S(1)}, f32[4,24,128]{2,1,0:T(8,128)S(1)}, u32[]{:S(2)}, u32[]{:S(2)}) %collective-permute-start.9) | collective-permute-done | bytes 49184 | tf_op jit(solution)/shard_map/ppermute | solution.py:21
  44.8 0.0 collective-permute-done.6.refs_13_
  44.8 0.0 collective-permute-done.10.refs_17_
  44.8 0.0 copy-done.2
  44.8 5.3 %last.1 = (f32[1,24,48,128]{3,2,1,0:T(8,128)}, f32[8,1,24,48,128]{4,3,2,1,0:T(8,128)}, f32[1,24,48,128]{3,2,1,0:T(8,128)S(1)}) custom-call(f32[8,1,24,48,128]{4,3,2,1,0:T(8,128)S(1)} %copy-done, f32[1,24,48,128]{3,2,1,0:T(8,128)S(1)} %get-tuple-element.23.refs_1_, s32[1,24,48,128]{3,2,1,0:T(8,128)S(1)} %copy-done.2, ...), custom_call_target="tpu_custom_call" | custom-call | flops 17694720 | bytes 17989632 | tf_op jit(solution)/shard_map/last/pallas_call | solution.py:42
  50.1 3.7 %collective-permute-done.11.refs_1_ = f32[1,20,48,128]{3,2,1,0:T(8,128)S(1)} collective-permute-done((f32[1,20,48,128]{3,2,1,0:T(8,128)S(1)}, f32[1,20,48,128]{3,2,1,0:T(8,128)S(1)}, u32[]{:S(2)}, u32[]{:S(2)}) %collective-permute-start.11) | collective-permute-done | bytes 491552 | tf_op jit(solution)/shard_map/ppermute | solution.py:21
  53.8 0.8 %finish.1 = f32[1,24,48,128]{3,2,1,0:T(8,128)} custom-call(f32[1,24,48,128]{3,2,1,0:T(8,128)S(1)} %get-tuple-element.39.refs_0_, f32[1,20,48,128]{3,2,1,0:T(8,128)S(1)} %collective-permute-done.11.refs_1_), custom_call_target="tpu_custom_call" | custom-call | tf_op jit(solution)/shard_map/finish/pallas_call | solution.py:247
  54.7 0.4 collective-permute-done.12
  55.1 0.7 %add_dynamic-update-slice_fusion = f32[1,24,48,128]{3,2,1,0:T(8,128)} fusion(f32[1,24,48,128]{3,2,1,0:T(8,128)} %finish.1, f32[1,4,48,128]{3,2,1,0:T(8,128)S(1)} %collective-permute-done.12, f32[1,24,48,128]{3,2,1,0:T(8,128)S(1)} %get-tuple-element.39.refs_0_), kind=kLoop, calls=%fused_computation | loop fusion | flops 24576 | bytes 294912 | tf_op jit(solution)/shard_map/dynamic_update_slice | solution.py:309
Async XLA Ops:
  0.6 19.9 %collective-permute-start.5 = (f32[1,24,48,128]{3,2,1,0:T(8,128)}, f32[1,24,48,128]{3,2,1,0:T(8,128)S(1)}, u32[]{:S(2)}, u32[]{:S(2)}) collective-permute-start(f32[1,24,48,128]{3,2,1,0:T(8,128)} %refs_6_.1), channel_id=1, source_target_pairs={{0,16},{16,0},{1,17},{17,1},{2,18},{18,2},{3,19},{19,3},{4,20},{20... | collective-permute-start | bytes 1769480 | tf_op jit(solution)/shard_map/ppermute | solution.py:21
  3.7 2.3 %copy-start = (f32[8,1,24,48,128]{4,3,2,1,0:T(8,128)S(1)}, f32[8,1,24,48,128]{4,3,2,1,0:T(8,128)}, u32[]{:S(2)}) copy-start(f32[8,1,24,48,128]{4,3,2,1,0:T(8,128)} %refs_0_.7) | copy-start | bytes 14155780
  6.0 1.1 %copy-start.1 = (s32[1,24,48,128]{3,2,1,0:T(8,128)S(1)}, s32[1,24,48,128]{3,2,1,0:T(8,128)}, u32[]{:S(2)}) copy-start(s32[1,24,48,128]{3,2,1,0:T(8,128)} %refs_2_.7) | copy-start | bytes 1769476
  7.1 1.1 %copy-start.3 = (f32[1,24,48,128]{3,2,1,0:T(8,128)S(1)}, f32[1,24,48,128]{3,2,1,0:T(8,128)}, u32[]{:S(2)}) copy-start(f32[1,24,48,128]{3,2,1,0:T(8,128)} %refs_6_.1) | copy-start | bytes 1769476
  8.1 1.1 %copy-start.5 = (f32[1,24,48,128]{3,2,1,0:T(8,128)S(1)}, f32[1,24,48,128]{3,2,1,0:T(8,128)}, u32[]{:S(2)}) copy-start(f32[1,24,48,128]{3,2,1,0:T(8,128)} %refs_2_.6) | copy-start | bytes 1769476
  9.2 11.3 %copy-start.4 = (f32[1,24,48,128]{3,2,1,0:T(8,128)S(1)}, f32[1,24,48,128]{3,2,1,0:T(8,128)}, u32[]{:S(2)}) copy-start(f32[1,24,48,128]{3,2,1,0:T(8,128)} %refs_6_.1) | copy-start | bytes 1769476
  10.0 20.7 %copy-start.6 = (f32[1,24,48,128]{3,2,1,0:T(8,128)S(1)}, f32[1,24,48,128]{3,2,1,0:T(8,128)}, u32[]{:S(2)}) copy-start(f32[1,24,48,128]{3,2,1,0:T(8,128)} %refs_2_.6) | copy-start | bytes 1769476
  10.0 10.5 %collective-permute-start.4 = (f32[1,24,48,128]{3,2,1,0:T(8,128)S(1)}, f32[1,24,48,128]{3,2,1,0:T(8,128)S(1)}, u32[]{:S(2)}, u32[]{:S(2)}) collective-permute-start(f32[1,24,48,128]{3,2,1,0:T(8,128)S(1)} %get-tuple-element.29), channel_id=1, source_target_pairs={{0,1},{1,0},{2,3},{3,2},{4,5},{5,4},{6,7},{7,6},{8,9},{9,8},{10,11... | collective-permute-start | bytes 1769480 | tf_op jit(solution)/shard_map/ppermute | solution.py:21
  10.1 20.6 %collective-permute-start = (f32[1,24,48,128]{3,2,1,0:T(8,128)S(1)}, f32[1,24,48,128]{3,2,1,0:T(8,128)S(1)}, u32[]{:S(2)}, u32[]{:S(2)}) collective-permute-start(f32[1,24,48,128]{3,2,1,0:T(8,128)S(1)} %get-tuple-element.25), channel_id=1, source_target_pairs={{0,16},{16,0},{1,17},{17,1},{2,18},{18,2},{3,19},{19,3},{4,20},{20... | collective-permute-start | bytes 1769480 | tf_op jit(solution)/shard_map/ppermute | solution.py:21
  10.2 6.2 %collective-permute-start.1 = (f32[2,48,128]{2,1,0:T(8,128)S(1)}, f32[2,48,128]{2,1,0:T(8,128)S(1)}, u32[]{:S(2)}, u32[]{:S(2)}) collective-permute-start(f32[2,48,128]{2,1,0:T(8,128)S(1)} %get-tuple-element.26), channel_id=1, source_target_pairs={{0,4},{4,8},{8,12},{12,0},{1,5},{5,9},{9,13},{13,1},{2,6},{6,10},{... | collective-permute-start | bytes 147464 | tf_op jit(solution)/shard_map/ppermute | solution.py:23
  12.3 5.9 %collective-permute-start.2 = (f32[2,48,128]{2,1,0:T(8,128)S(1)}, f32[2,48,128]{2,1,0:T(8,128)S(1)}, u32[]{:S(2)}, u32[]{:S(2)}) collective-permute-start(f32[2,48,128]{2,1,0:T(8,128)S(1)} %get-tuple-element.27), channel_id=1, source_target_pairs={{0,12},{4,0},{8,4},{12,8},{1,13},{5,1},{9,5},{13,9},{2,14},{6,2},{... | collective-permute-start | bytes 147464 | tf_op jit(solution)/shard_map/ppermute | solution.py:23
  16.4 4.1 %collective-permute-start.3 = (f32[4,24,128]{2,1,0:T(8,128)S(1)}, f32[4,24,128]{2,1,0:T(8,128)S(1)}, u32[]{:S(2)}, u32[]{:S(2)}) collective-permute-start(f32[4,24,128]{2,1,0:T(8,128)S(1)} %get-tuple-element.28), channel_id=1, source_target_pairs={{0,2},{2,0},{1,3},{3,1},{4,6},{6,4},{5,7},{7,5},{8,10},{10,8},{9,1... | collective-permute-start | bytes 147464 | tf_op jit(solution)/shard_map/ppermute | solution.py:21
  21.4 23.5 %copy-start.2 = (s32[1,24,48,128]{3,2,1,0:T(8,128)S(1)}, s32[1,24,48,128]{3,2,1,0:T(8,128)}, u32[]{:S(2)}) copy-start(s32[1,24,48,128]{3,2,1,0:T(8,128)} %refs_2_.7) | copy-start | bytes 1769476
  21.4 23.5 %collective-permute-start.6 = (f32[1,24,48,128]{3,2,1,0:T(8,128)S(1)}, f32[1,24,48,128]{3,2,1,0:T(8,128)S(1)}, u32[]{:S(2)}, u32[]{:S(2)}) collective-permute-start(f32[1,24,48,128]{3,2,1,0:T(8,128)S(1)} %get-tuple-element.30.refs_9_.refs_12_), channel_id=1, source_target_pairs={{0,16},{16,0},{1,17},{17,1},{2,18},{18,2},{3,19},{19,3},{4,20},{20... | collective-permute-start | bytes 1769480 | tf_op jit(solution)/shard_map/ppermute | solution.py:21
  32.3 12.5 %collective-permute-start.10 = (f32[1,24,48,128]{3,2,1,0:T(8,128)S(1)}, f32[1,24,48,128]{3,2,1,0:T(8,128)S(1)}, u32[]{:S(2)}, u32[]{:S(2)}) collective-permute-start(f32[1,24,48,128]{3,2,1,0:T(8,128)S(1)} %get-tuple-element.36), channel_id=1, source_target_pairs={{0,1},{1,0},{2,3},{3,2},{4,5},{5,4},{6,7},{7,6},{8,9},{9,8},{10,11... | collective-permute-start | bytes 1769480 | tf_op jit(solution)/shard_map/ppermute | solution.py:21
  32.4 21.5 %collective-permute-start.11 = (f32[1,20,48,128]{3,2,1,0:T(8,128)S(1)}, f32[1,20,48,128]{3,2,1,0:T(8,128)S(1)}, u32[]{:S(2)}, u32[]{:S(2)}) collective-permute-start(f32[1,20,48,128]{3,2,1,0:T(8,128)S(1)} %get-tuple-element.40), channel_id=1, source_target_pairs={{0,16},{16,0},{1,17},{17,1},{2,18},{18,2},{3,19},{19,3},{4,20},{20... | collective-permute-start | bytes 1474568 | tf_op jit(solution)/shard_map/ppermute | solution.py:21
  34.5 6.0 %collective-permute-start.7 = (f32[2,48,128]{2,1,0:T(8,128)S(1)}, f32[2,48,128]{2,1,0:T(8,128)S(1)}, u32[]{:S(2)}, u32[]{:S(2)}) collective-permute-start(f32[2,48,128]{2,1,0:T(8,128)S(1)} %get-tuple-element.33), channel_id=1, source_target_pairs={{0,4},{4,8},{8,12},{12,0},{1,5},{5,9},{9,13},{13,1},{2,6},{6,10},{... | collective-permute-start | bytes 147464 | tf_op jit(solution)/shard_map/ppermute | solution.py:23
  36.1 4.7 %collective-permute-start.8 = (f32[2,48,128]{2,1,0:T(8,128)S(1)}, f32[2,48,128]{2,1,0:T(8,128)S(1)}, u32[]{:S(2)}, u32[]{:S(2)}) collective-permute-start(f32[2,48,128]{2,1,0:T(8,128)S(1)} %get-tuple-element.34), channel_id=1, source_target_pairs={{0,12},{4,0},{8,4},{12,8},{1,13},{5,1},{9,5},{13,9},{2,14},{6,2},{... | collective-permute-start | bytes 147464 | tf_op jit(solution)/shard_map/ppermute | solution.py:23
  40.5 14.6 %collective-permute-start.12 = (f32[1,4,48,128]{3,2,1,0:T(8,128)S(1)}, f32[1,4,48,128]{3,2,1,0:T(8,128)S(1)}, u32[]{:S(2)}, u32[]{:S(2)}) collective-permute-start(f32[1,4,48,128]{3,2,1,0:T(8,128)S(1)} %get-tuple-element.41), channel_id=1, source_target_pairs={{0,16},{16,0},{1,17},{17,1},{2,18},{18,2},{3,19},{19,3},{4,20},{20... | collective-permute-start | bytes 294920 | tf_op jit(solution)/shard_map/ppermute | solution.py:21
  40.7 4.1 %collective-permute-start.9 = (f32[4,24,128]{2,1,0:T(8,128)S(1)}, f32[4,24,128]{2,1,0:T(8,128)S(1)}, u32[]{:S(2)}, u32[]{:S(2)}) collective-permute-start(f32[4,24,128]{2,1,0:T(8,128)S(1)} %get-tuple-element.35), channel_id=1, source_target_pairs={{0,2},{2,0},{1,3},{3,1},{4,6},{6,4},{5,7},{7,5},{8,10},{10,8},{9,1... | collective-permute-start | bytes 147464 | tf_op jit(solution)/shard_map/ppermute | solution.py:21

commit v6 on v5

--- a/solution.py
+++ b/solution.py
@@ -21,6 +21,21 @@
         other = lax.ppermute(up, axis, ring(axis, 1))
         return other, other
     return lax.ppermute(up, axis, ring(axis, 1)), lax.ppermute(down, axis, ring(axis, -1))
+
+
+def row_swap(row):
+    ys, zs = lax.axis_size("gy"), lax.axis_size("gz")
+    axes = ("grp", "gy", "gz")
+
+    def at(g, y, z):
+        return (g * ys + y) * zs + z
+
+    straight = [(at(g, y, z), at(1 - g, y, z)) for g in range(2) for y in range(ys) for z in range(zs) if zs < 2 or y + z > 0]
+    parts = [lax.ppermute(row, axes, straight)]
+    if zs > 1:
+        row = lax.ppermute(row, axes, [(at(g, 0, 0), at(1 - g, 0, 1)) for g in range(2)])
+        parts.append(lax.ppermute(row, axes, [(at(g, 0, 1), at(g, 0, 0)) for g in range(2)]))
+    return parts
 
 
 def call(body, name, operands, shapes, flops):
@@ -51,8 +66,10 @@
 
 
 def rows(first, stop, step):
-    unroll = 4 if (stop - first) % 4 == 0 else 1
-    lax.fori_loop(first, stop, lambda b, _: step(b), None, unroll=unroll)
+    whole = first + (stop - first) // 4 * 4
+    lax.fori_loop(first, whole, lambda b, _: step(b), None, unroll=4)
+    for b in range(whole, stop):
+        step(b)
 
 
 def iotas(c, d):
@@ -112,7 +129,7 @@
     count, c, d = g_ref.shape[1:]
     row, lane = iotas(c, d)
 
-    def step(b):
+    def step(b, u, shift):
         r = [rates[j, 0, b] for j in range(8)]
         total = ((r[0] + r[1]) + (r[2] + r[3])) + ((r[4] + r[5]) + (r[6] + r[7]))
         f = jnp.where(labels[0, b] == 0, DAMP / total, 0.0)
@@ -120,7 +137,7 @@
         f_ref[0, b] = f
         g_ref[0, b] = g
         if pair:
-            u_refs[0][0, b] = (r[0] + r[1]) * g
+            u[0, b - shift] = (r[0] + r[1]) * g
         else:
             u_refs[0][0, b] = r[0] * g
             u_refs[1][0, b] = r[1] * g
@@ -130,7 +147,11 @@
         gz_ref[2, pl.ds(b, 1), :] = (r[4] * g)[c - 1 :]
         gz_ref[3, pl.ds(b, 1), :] = (r[5] * g)[:1]
 
-    rows(0, count, step)
+    if pair:
+        rows(0, count - 1, lambda b: step(b, u_refs[0], 0))
+        step(count - 1, u_refs[1], count - 1)
+    else:
+        rows(0, count, lambda b: step(b, None, 0))
     up_ref[0] = start[0, count - 1]
     up_ref[1] = rates[2, 0, count - 1] * g_ref[0, count - 1]
     down_ref[0] = start[0, 0]
@@ -171,7 +192,12 @@
     return out
 
 
-def back_body(pair, rates, f_ref, cot, g, u_before, u_after, up, down, gz_before, gz_after, wa_before, wa_after, first,
+def back_body(pair, parts, rates, f_ref, cot, g, u_before, u_after, *refs):
+    u_row, refs = refs[:parts], refs[parts:]
+    back_rows(pair, rates, f_ref, cot, g, u_before, u_after, u_row, *refs)
+
+
+def back_rows(pair, rates, f_ref, cot, g, u_before, u_after, u_row, up, down, gz_before, gz_after, wa_before, wa_after, first,
               back, h_ref, w_ref, up_ref, down_ref, gz_ref, *v_refs):
     count, c, d = g.shape[1:]
     row, lane = iotas(c, d)
@@ -179,9 +205,12 @@
     half = len(v_refs) // 2
     cut = v_refs[0].shape[1]
 
-    def step(b, v, shift):
+    def step(b, v, shift, came=None):
         out = spread(rates, f_ref, cot[0, b], g, up, down, gz_before, gz_after, wa_before, wa_after, 1, b, row, lane)
-        if pair:
+        if came:
+            for ref in came:
+                out = out + ref[0, 0]
+        elif pair:
             out = out + u_before[0, b]
         else:
             out = out + u_before[0, b] + u_after[0, b]
@@ -200,7 +229,10 @@
         gz_ref[3, pl.ds(b, 1), :] = (rates[5, 0, b] * h)[:1]
 
     rows(0, cut, lambda b: step(b, v_refs[:half], 0))
-    rows(cut, count, lambda b: step(b, v_refs[half:], cut))
+    stop = count - 1 if pair else count
+    rows(cut, stop, lambda b: step(b, v_refs[half:], cut))
+    if pair:
+        step(stop, v_refs[half:], cut, u_row)
     up_ref[0] = first[0, count - 1]
     up_ref[1] = rates[2, 0, count - 1] * h_ref[0, count - 1]
     down_ref[0] = first[0, 0]
@@ -266,9 +298,10 @@
 
     start_before, start_after = both_ways(start, start, "grp")
     f, g, w0, up, down, gz, *u = call(
-        functools.partial(prepare_body, pair), "prepare", [rates, labels, cotangent, start], [block] * 3 + faces + blocks, 20 * cells
-    )
-    u_before, u_after = both_ways(u[0], u[-1], "grp")
+        functools.partial(prepare_body, pair), "prepare", [rates, labels, cotangent, start], [block] * 3 + faces + ([(1, b - 1, c, d), (1, 1, c, d)] if pair else blocks), 20 * cells
+    )
+    u_before, u_after = both_ways(u[0], u[0] if pair else u[1], "grp")
+    u_row = row_swap(u[1]) if pair else []
     up0, down0 = both_ways(up, down, "gy")
     gz_before0, gz_after0 = both_ways(gz, gz, "gz")
     wa0 = both_ways(w0, w0, "wa")
@@ -283,9 +316,9 @@
     first_before, first_after = both_ways(first, first, "grp")
 
     back, h, w1, up, down, gz, *v = call(
-        functools.partial(back_body, pair),
+        functools.partial(back_body, pair, len(u_row)),
         "backward",
-        [rates, f, cotangent, g, u_before, u_after, up0, down0, gz_before0, gz_after0, *wa0, first],
+        [rates, f, cotangent, g, u_before, u_after, *u_row, up0, down0, gz_before0, gz_after0, *wa0, first],
         [block] * 3 + faces + [(1, b - tail, c, d)] * len(blocks) + [(1, tail, c, d)] * len(blocks),
         30 * cells,
     )

time: 56.1 us -> 55.6 us (level)
  waiting for transfers between devices: 20.6 us -> 15.1 us
  starting transfers between devices: 18.9 us -> 23.6 us
    ppermute x9, waiting for transfers between devices: 16.3 us -> 5.04 us  [both_ways(): other = lax.ppermute(up, axis, ring(axis, 1))]
    ppermute x0 -> x3, starting transfers between devices: none -> 6.28 us  [the longest x1 4.34 us: row_swap(): lax.ppermute(row, axes, [(at(g, 0, 0), at(1 - g, 0, 1)) for g in range(2)])]
    ppermute x0 -> x3, waiting for transfers between devices: none -> 6.26 us  [the longest x1 4.75 us: row_swap(): lax.ppermute(row, axes, [(at(g, 0, 1), at(g, 0, 0)) for g in range(2)])]
    ppermute x2, starting transfers between devices: 4.28 us -> 2.03 us  [both_ways(): lax.ppermute(down, axis, ring(axis, -1))]
    ppermute x2, waiting for transfers between devices: 4.3 us -> 2.13 us  [both_ways(): lax.ppermute(up, axis, ring(axis, 1))]
    ppermute x2, waiting for transfers between devices: 0.01 us -> 1.73 us  [both_ways(): lax.ppermute(down, axis, ring(axis, -1))]
  transfers between devices with their start and end apart: 13 -> 16, of which waited for: 7 -> 7; matrix products, arithmetic and copies ran while one was open for 0% -> 0% of each run, Pallas kernels for 17% -> 17%
where the time goes in v6:
time: 55.6 us; the launch traced here: 55.2 us
  starting transfers between devices  23.6 us (42%)
  waiting for transfers between devices  15.1 us (27%)
  Pallas kernels  9.56 us (17%)
  local copies, waits for them, and re-layouts  5.54 us (10%)
  between operations  0.76 us (1%)
  other arithmetic  0.65 us (1%)
    ppermute x9, starting transfers between devices, both_ways(): other = lax.ppermute(up, axis, ring(axis, 1))  11.1 us
    pallas_call x4, Pallas kernels, call(): pl.pallas_call(kernel, out_shape=[jax.ShapeDtypeStruct(s, jnp.float32) fo...  8.72 us
    unnamed x14, local copies, waits for them, and re-layouts  5.54 us
    ppermute x9, waiting for transfers between devices, both_ways(): other = lax.ppermute(up, axis, ring(axis, 1))  5.04 us
    ppermute x1, waiting for transfers between devices, row_swap(): lax.ppermute(row, axes, [(at(g, 0, 1), at(g, 0, 0)) for g in range(2)])  4.75 us
    ppermute x1, starting transfers between devices, row_swap(): lax.ppermute(row, axes, [(at(g, 0, 0), at(1 - g, 0, 1)) for g in range(2)])  4.34 us
    ppermute x2, starting transfers between devices, both_ways(): lax.ppermute(up, axis, ring(axis, 1))  4.19 us
    ppermute x2, waiting for transfers between devices, both_ways(): lax.ppermute(up, axis, ring(axis, 1))  2.13 us
  transfers between devices with their start and end apart: 16, of which 7 were waited for; matrix products, arithmetic and copies ran while one was open for 0% of the time, Pallas kernels for 17%

profile of v6, /device:TPU:0, one launch (start us, length us, event | category | flops | bytes accessed | tf_op | source)
XLA Modules:
  0.0 55.2 jit_solution(15033882147362061986)
XLA Ops:
  0.6 3.0 %collective-permute-start.8 = (f32[1,24,48,128]{3,2,1,0:T(8,128)}, f32[1,24,48,128]{3,2,1,0:T(8,128)S(1)}, u32[]{:S(2)}, u32[]{:S(2)}) collective-permute-start(f32[1,24,48,128]{3,2,1,0:T(8,128)} %refs_6_.1), channel_id=1, source_target_pairs={{0,16},{16,0},{1,17},{17,1},{2,18},{18,2},{3,19},{19,3},{4,20},{20... | collective-permute-start | bytes 1769480 | tf_op jit(solution)/shard_map/ppermute | solution.py:21
  3.7 0.0 copy-start
  3.7 2.3 %copy-done = f32[8,1,24,48,128]{4,3,2,1,0:T(8,128)S(1)} copy-done((f32[8,1,24,48,128]{4,3,2,1,0:T(8,128)S(1)}, f32[8,1,24,48,128]{4,3,2,1,0:T(8,128)}, u32[]{:S(2)}) %copy-start) | copy-done | bytes 4718616
  6.0 0.0 copy-start.1
  6.0 1.1 %copy-done.1 = s32[1,24,48,128]{3,2,1,0:T(8,128)S(1)} copy-done((s32[1,24,48,128]{3,2,1,0:T(8,128)S(1)}, s32[1,24,48,128]{3,2,1,0:T(8,128)}, u32[]{:S(2)}) %copy-start.1) | copy-done | bytes 589848
  7.1 0.0 copy-start.3
  7.1 1.1 %copy-done.3 = f32[1,24,48,128]{3,2,1,0:T(8,128)S(1)} copy-done((f32[1,24,48,128]{3,2,1,0:T(8,128)S(1)}, f32[1,24,48,128]{3,2,1,0:T(8,128)}, u32[]{:S(2)}) %copy-start.3) | copy-done | bytes 589848
  8.1 0.0 copy-start.5
  8.1 1.1 %copy-done.5 = f32[1,24,48,128]{3,2,1,0:T(8,128)S(1)} copy-done((f32[1,24,48,128]{3,2,1,0:T(8,128)S(1)}, f32[1,24,48,128]{3,2,1,0:T(8,128)}, u32[]{:S(2)}) %copy-start.5) | copy-done | bytes 589848
  9.2 0.0 copy-start.4
  9.2 0.8 %prepare.1 = (f32[1,24,48,128]{3,2,1,0:T(8,128)S(1)}, f32[1,24,48,128]{3,2,1,0:T(8,128)S(1)}, f32[1,24,48,128]{3,2,1,0:T(8,128)S(1)}, f32[2,48,128]{2,1,0:T(8,12...) custom-call(f32[8,1,24,48,128]{4,3,2,1,0:T(8,128)S(1)} %copy-done, ...), custom_call_target="tpu_custom_call" | custom-call | flops 2949120 | bytes 8994816 | tf_op jit(solution)/shard_map/prepare/pallas_call | solution.py:57
  10.0 0.0 copy-start.6
  10.0 0.1 collective-permute-start.7
  10.1 0.1 collective-permute-start
  10.2 2.1 %collective-permute-start.4 = (f32[2,48,128]{2,1,0:T(8,128)S(1)}, f32[2,48,128]{2,1,0:T(8,128)S(1)}, u32[]{:S(2)}, u32[]{:S(2)}) collective-permute-start(f32[2,48,128]{2,1,0:T(8,128)S(1)} %get-tuple-element.28), channel_id=1, source_target_pairs={{0,4},{4,8},{8,12},{12,0},{1,5},{5,9},{9,13},{13,1},{2,6},{6,10},{... | collective-permute-start | bytes 147464 | tf_op jit(solution)/shard_map/ppermute | solution.py:23
  12.2 4.3 %collective-permute-start.2 = (f32[1,1,48,128]{3,2,1,0:T(8,128)S(1)}, f32[1,1,48,128]{3,2,1,0:T(8,128)S(1)}, u32[]{:S(2)}, u32[]{:S(2)}) collective-permute-start(f32[1,1,48,128]{3,2,1,0:T(8,128)S(1)} %get-tuple-element.27), channel_id=1, source_target_pairs={{0,18},{16,2},{1,19},{17,3}} | collective-permute-start | bytes 73736 | tf_op jit(solution)/shard_map/ppermute | solution.py:36
  16.6 1.5 %collective-permute-done.2 = f32[1,1,48,128]{3,2,1,0:T(8,128)S(1)} collective-permute-done((f32[1,1,48,128]{3,2,1,0:T(8,128)S(1)}, f32[1,1,48,128]{3,2,1,0:T(8,128)S(1)}, u32[]{:S(2)}, u32[]{:S(2)}) %collective-permute-start.2) | collective-permute-done | bytes 24608 | tf_op jit(solution)/shard_map/ppermute | solution.py:36
  18.1 0.0 collective-permute-start.5
  18.1 0.0 collective-permute-done.4.refs_5_.refs_7_.refs_8_
  18.1 2.4 %collective-permute-start.6 = (f32[4,24,128]{2,1,0:T(8,128)S(1)}, f32[4,24,128]{2,1,0:T(8,128)S(1)}, u32[]{:S(2)}, u32[]{:S(2)}) collective-permute-start(f32[4,24,128]{2,1,0:T(8,128)S(1)} %get-tuple-element.30), channel_id=1, source_target_pairs={{0,2},{2,0},{1,3},{3,1},{4,6},{6,4},{5,7},{7,5},{8,10},{10,8},{9,1... | collective-permute-start | bytes 147464 | tf_op jit(solution)/shard_map/ppermute | solution.py:21
  20.5 1.7 %collective-permute-done.5.refs_6_.refs_8_.refs_9_ = f32[2,48,128]{2,1,0:T(8,128)S(1)} collective-permute-done((f32[2,48,128]{2,1,0:T(8,128)S(1)}, f32[2,48,128]{2,1,0:T(8,128)S(1)}, u32[]{:S(2)}, u32[]{:S(2)}) %collective-permute-start.5) | collective-permute-done | bytes 49184 | tf_op jit(solution)/shard_map/ppermute | solution.py:23
  22.2 0.7 %collective-permute-start.1 = (f32[1,1,48,128]{3,2,1,0:T(8,128)S(1)}, f32[1,1,48,128]{3,2,1,0:T(8,128)S(1)}, u32[]{:S(2)}, u32[]{:S(2)}) collective-permute-start(f32[1,1,48,128]{3,2,1,0:T(8,128)S(1)} %get-tuple-element.27), channel_id=1, source_target_pairs={{2,18},{4,20},{6,22},{8,24},{10,26},{12,28},{14,30},{18,2},{20,4},... | collective-permute-start | bytes 73736 | tf_op jit(solution)/shard_map/ppermute | solution.py:34
  22.8 0.0 collective-permute-done.6.refs_7_.refs_9_.refs_10_
  22.9 1.3 %collective-permute-start.3 = (f32[1,1,48,128]{3,2,1,0:T(8,128)S(1)}, f32[1,1,48,128]{3,2,1,0:T(8,128)S(1)}, u32[]{:S(2)}, u32[]{:S(2)}) collective-permute-start(f32[1,1,48,128]{3,2,1,0:T(8,128)S(1)} %collective-permute-done.2), channel_id=1, source_target_pairs={{2,0},{18,16},{3,1},{19,17}} | collective-permute-start | bytes 73736 | tf_op jit(solution)/shard_map/ppermute | solution.py:37
  24.1 0.0 collective-permute-done.8.refs_4_.refs_7_
  24.2 0.0 collective-permute-done.7.refs_8_.refs_10_.refs_11_
  24.2 0.0 copy-done.4
  24.2 0.9 %forward.1 = (f32[1,24,48,128]{3,2,1,0:T(8,128)S(1)}, f32[1,24,48,128]{3,2,1,0:T(8,128)S(1)}) custom-call(f32[8,1,24,48,128]{4,3,2,1,0:T(8,128)S(1)} %copy-done, f32[1,24,48,128]{3,2,1,0:T(8,128)S(1)} %get-tuple-element.24.refs_1_, s32[1,24,48,128]{3,2,1,0:T(8,128)S(1)} %copy-done.1, f32[1,24,48,128]{3,2,1,0:T(8,128)S(1)} %copy-done.4, ...), custom_call_target="tpu_custom_call" | custom-call | flops 4423680 | bytes 8994816 | tf_op jit(solution)/shard_map/forward/pallas_call | solution.py:57
  25.0 0.0 copy-start.2
  25.1 1.2 %collective-permute-start.9 = (f32[1,24,48,128]{3,2,1,0:T(8,128)S(1)}, f32[1,24,48,128]{3,2,1,0:T(8,128)S(1)}, u32[]{:S(2)}, u32[]{:S(2)}) collective-permute-start(f32[1,24,48,128]{3,2,1,0:T(8,128)S(1)} %get-tuple-element.32.refs_11_.refs_12_), channel_id=1, source_target_pairs={{0,16},{16,0},{1,17},{17,1},{2,18},{18,2},{3,19},{19,3},{4,20},{20... | collective-permute-start | bytes 1769480 | tf_op jit(solution)/shard_map/ppermute | solution.py:21
  26.3 0.0 collective-permute-done.1.refs_5_
  26.3 4.8 %collective-permute-done.3.refs_6_ = f32[1,1,48,128]{3,2,1,0:T(8,128)S(1)} collective-permute-done((f32[1,1,48,128]{3,2,1,0:T(8,128)S(1)}, f32[1,1,48,128]{3,2,1,0:T(8,128)S(1)}, u32[]{:S(2)}, u32[]{:S(2)}) %collective-permute-start.3) | collective-permute-done | bytes 24608 | tf_op jit(solution)/shard_map/ppermute | solution.py:37
  31.1 0.0 collective-permute-done.refs_4_
  31.1 0.0 copy-done.6
  31.1 1.7 %backward.1 = (f32[1,24,48,128]{3,2,1,0:T(8,128)S(1)}, f32[1,24,48,128]{3,2,1,0:T(8,128)S(1)}, f32[1,24,48,128]{3,2,1,0:T(8,128)S(1)}, f32[2,48,128]{2,1,0:T(8,1...) custom-call(f32[8,1,24,48,128]{4,3,2,1,0:T(8,128)S(1)} %copy-done, ...), custom_call_target="tpu_custom_call" | custom-call | flops 4423680 | bytes 10936320 | tf_op jit(solution)/shard_map/backward/pallas_call | solution.py:57
  32.8 0.1 collective-permute-start.13
  32.8 1.2 %collective-permute-start.14 = (f32[1,20,48,128]{3,2,1,0:T(8,128)S(1)}, f32[1,20,48,128]{3,2,1,0:T(8,128)S(1)}, u32[]{:S(2)}, u32[]{:S(2)}) collective-permute-start(f32[1,20,48,128]{3,2,1,0:T(8,128)S(1)} %get-tuple-element.42), channel_id=1, source_target_pairs={{0,16},{16,0},{1,17},{17,1},{2,18},{18,2},{3,19},{19,3},{4,20},{20... | collective-permute-start | bytes 1474568 | tf_op jit(solution)/shard_map/ppermute | solution.py:21
  34.0 2.1 %collective-permute-start.10 = (f32[2,48,128]{2,1,0:T(8,128)S(1)}, f32[2,48,128]{2,1,0:T(8,128)S(1)}, u32[]{:S(2)}, u32[]{:S(2)}) collective-permute-start(f32[2,48,128]{2,1,0:T(8,128)S(1)} %get-tuple-element.35), channel_id=1, source_target_pairs={{0,4},{4,8},{8,12},{12,0},{1,5},{5,9},{9,13},{13,1},{2,6},{6,10},{... | collective-permute-start | bytes 147464 | tf_op jit(solution)/shard_map/ppermute | solution.py:23
  36.2 2.0 %collective-permute-start.11 = (f32[2,48,128]{2,1,0:T(8,128)S(1)}, f32[2,48,128]{2,1,0:T(8,128)S(1)}, u32[]{:S(2)}, u32[]{:S(2)}) collective-permute-start(f32[2,48,128]{2,1,0:T(8,128)S(1)} %get-tuple-element.36), channel_id=1, source_target_pairs={{0,12},{4,0},{8,4},{12,8},{1,13},{5,1},{9,5},{13,9},{2,14},{6,2},{... | collective-permute-start | bytes 147464 | tf_op jit(solution)/shard_map/ppermute | solution.py:23
  38.2 2.1 %collective-permute-done.10.refs_14_ = f32[2,48,128]{2,1,0:T(8,128)S(1)} collective-permute-done((f32[2,48,128]{2,1,0:T(8,128)S(1)}, f32[2,48,128]{2,1,0:T(8,128)S(1)}, u32[]{:S(2)}, u32[]{:S(2)}) %collective-permute-start.10) | collective-permute-done | bytes 49184 | tf_op jit(solution)/shard_map/ppermute | solution.py:23
  40.3 0.6 %collective-permute-start.15 = (f32[1,4,48,128]{3,2,1,0:T(8,128)S(1)}, f32[1,4,48,128]{3,2,1,0:T(8,128)S(1)}, u32[]{:S(2)}, u32[]{:S(2)}) collective-permute-start(f32[1,4,48,128]{3,2,1,0:T(8,128)S(1)} %get-tuple-element.43), channel_id=1, source_target_pairs={{0,16},{16,0},{1,17},{17,1},{2,18},{18,2},{3,19},{19,3},{4,20},{20... | collective-permute-start | bytes 294920 | tf_op jit(solution)/shard_map/ppermute | solution.py:21
  40.9 0.0 collective-permute-done.11.refs_15_
  40.9 2.4 %collective-permute-start.12 = (f32[4,24,128]{2,1,0:T(8,128)S(1)}, f32[4,24,128]{2,1,0:T(8,128)S(1)}, u32[]{:S(2)}, u32[]{:S(2)}) collective-permute-start(f32[4,24,128]{2,1,0:T(8,128)S(1)} %get-tuple-element.37), channel_id=1, source_target_pairs={{0,2},{2,0},{1,3},{3,1},{4,6},{6,4},{5,7},{7,5},{8,10},{10,8},{9,1... | collective-permute-start | bytes 147464 | tf_op jit(solution)/shard_map/ppermute | solution.py:21
  43.3 2.1 %collective-permute-done.12.refs_16_ = f32[4,24,128]{2,1,0:T(8,128)S(1)} collective-permute-done((f32[4,24,128]{2,1,0:T(8,128)S(1)}, f32[4,24,128]{2,1,0:T(8,128)S(1)}, u32[]{:S(2)}, u32[]{:S(2)}) %collective-permute-start.12) | collective-permute-done | bytes 49184 | tf_op jit(solution)/shard_map/ppermute | solution.py:21
  45.4 0.0 collective-permute-done.9.refs_13_
  45.4 0.0 collective-permute-done.13.refs_17_
  45.4 0.0 copy-done.2
  45.4 5.4 %last.1 = (f32[1,24,48,128]{3,2,1,0:T(8,128)}, f32[8,1,24,48,128]{4,3,2,1,0:T(8,128)}, f32[1,24,48,128]{3,2,1,0:T(8,128)S(1)}) custom-call(f32[8,1,24,48,128]{4,3,2,1,0:T(8,128)S(1)} %copy-done, f32[1,24,48,128]{3,2,1,0:T(8,128)S(1)} %get-tuple-element.24.refs_1_, s32[1,24,48,128]{3,2,1,0:T(8,128)S(1)} %copy-done.2, ...), custom_call_target="tpu_custom_call" | custom-call | flops 17694720 | bytes 17989632 | tf_op jit(solution)/shard_map/last/pallas_call | solution.py:57
  50.8 2.5 %collective-permute-done.14.refs_1_ = f32[1,20,48,128]{3,2,1,0:T(8,128)S(1)} collective-permute-done((f32[1,20,48,128]{3,2,1,0:T(8,128)S(1)}, f32[1,20,48,128]{3,2,1,0:T(8,128)S(1)}, u32[]{:S(2)}, u32[]{:S(2)}) %collective-permute-start.14) | collective-permute-done | bytes 491552 | tf_op jit(solution)/shard_map/ppermute | solution.py:21
  53.3 0.8 %finish.1 = f32[1,24,48,128]{3,2,1,0:T(8,128)} custom-call(f32[1,24,48,128]{3,2,1,0:T(8,128)S(1)} %get-tuple-element.41.refs_0_, f32[1,20,48,128]{3,2,1,0:T(8,128)S(1)} %collective-permute-done.14.refs_1_), custom_call_target="tpu_custom_call" | custom-call | tf_op jit(solution)/shard_map/finish/pallas_call | solution.py:279
  54.2 0.4 collective-permute-done.15
  54.6 0.7 %add_dynamic-update-slice_fusion = f32[1,24,48,128]{3,2,1,0:T(8,128)} fusion(f32[1,24,48,128]{3,2,1,0:T(8,128)} %finish.1, f32[1,4,48,128]{3,2,1,0:T(8,128)S(1)} %collective-permute-done.15, f32[1,24,48,128]{3,2,1,0:T(8,128)S(1)} %get-tuple-element.41.refs_0_), kind=kLoop, calls=%fused_computation | loop fusion | flops 24576 | bytes 294912 | tf_op jit(solution)/shard_map/dynamic_update_slice | solution.py:342
Async XLA Ops:
  0.6 23.5 %collective-permute-start.8 = (f32[1,24,48,128]{3,2,1,0:T(8,128)}, f32[1,24,48,128]{3,2,1,0:T(8,128)S(1)}, u32[]{:S(2)}, u32[]{:S(2)}) collective-permute-start(f32[1,24,48,128]{3,2,1,0:T(8,128)} %refs_6_.1), channel_id=1, source_target_pairs={{0,16},{16,0},{1,17},{17,1},{2,18},{18,2},{3,19},{19,3},{4,20},{20... | collective-permute-start | bytes 1769480 | tf_op jit(solution)/shard_map/ppermute | solution.py:21
  3.7 2.3 %copy-start = (f32[8,1,24,48,128]{4,3,2,1,0:T(8,128)S(1)}, f32[8,1,24,48,128]{4,3,2,1,0:T(8,128)}, u32[]{:S(2)}) copy-start(f32[8,1,24,48,128]{4,3,2,1,0:T(8,128)} %refs_0_.7) | copy-start | bytes 14155780
  6.0 1.1 %copy-start.1 = (s32[1,24,48,128]{3,2,1,0:T(8,128)S(1)}, s32[1,24,48,128]{3,2,1,0:T(8,128)}, u32[]{:S(2)}) copy-start(s32[1,24,48,128]{3,2,1,0:T(8,128)} %refs_2_.7) | copy-start | bytes 1769476
  7.1 1.1 %copy-start.3 = (f32[1,24,48,128]{3,2,1,0:T(8,128)S(1)}, f32[1,24,48,128]{3,2,1,0:T(8,128)}, u32[]{:S(2)}) copy-start(f32[1,24,48,128]{3,2,1,0:T(8,128)} %refs_6_.1) | copy-start | bytes 1769476
  8.1 1.1 %copy-start.5 = (f32[1,24,48,128]{3,2,1,0:T(8,128)S(1)}, f32[1,24,48,128]{3,2,1,0:T(8,128)}, u32[]{:S(2)}) copy-start(f32[1,24,48,128]{3,2,1,0:T(8,128)} %refs_2_.6) | copy-start | bytes 1769476
  9.2 15.0 %copy-start.4 = (f32[1,24,48,128]{3,2,1,0:T(8,128)S(1)}, f32[1,24,48,128]{3,2,1,0:T(8,128)}, u32[]{:S(2)}) copy-start(f32[1,24,48,128]{3,2,1,0:T(8,128)} %refs_6_.1) | copy-start | bytes 1769476
  10.0 21.1 %copy-start.6 = (f32[1,24,48,128]{3,2,1,0:T(8,128)S(1)}, f32[1,24,48,128]{3,2,1,0:T(8,128)}, u32[]{:S(2)}) copy-start(f32[1,24,48,128]{3,2,1,0:T(8,128)} %refs_2_.6) | copy-start | bytes 1769476
  10.0 14.2 %collective-permute-start.7 = (f32[1,24,48,128]{3,2,1,0:T(8,128)S(1)}, f32[1,24,48,128]{3,2,1,0:T(8,128)S(1)}, u32[]{:S(2)}, u32[]{:S(2)}) collective-permute-start(f32[1,24,48,128]{3,2,1,0:T(8,128)S(1)} %get-tuple-element.31), channel_id=1, source_target_pairs={{0,1},{1,0},{2,3},{3,2},{4,5},{5,4},{6,7},{7,6},{8,9},{9,8},{10,11... | collective-permute-start | bytes 1769480 | tf_op jit(solution)/shard_map/ppermute | solution.py:21
  10.1 21.0 %collective-permute-start = (f32[1,23,48,128]{3,2,1,0:T(8,128)S(1)}, f32[1,23,48,128]{3,2,1,0:T(8,128)S(1)}, u32[]{:S(2)}, u32[]{:S(2)}) collective-permute-start(f32[1,23,48,128]{3,2,1,0:T(8,128)S(1)} %get-tuple-element.26), channel_id=1, source_target_pairs={{0,16},{16,0},{1,17},{17,1},{2,18},{18,2},{3,19},{19,3},{4,20},{20... | collective-permute-start | bytes 1695752 | tf_op jit(solution)/shard_map/ppermute | solution.py:21
  10.2 7.9 %collective-permute-start.4 = (f32[2,48,128]{2,1,0:T(8,128)S(1)}, f32[2,48,128]{2,1,0:T(8,128)S(1)}, u32[]{:S(2)}, u32[]{:S(2)}) collective-permute-start(f32[2,48,128]{2,1,0:T(8,128)S(1)} %get-tuple-element.28), channel_id=1, source_target_pairs={{0,4},{4,8},{8,12},{12,0},{1,5},{5,9},{9,13},{13,1},{2,6},{6,10},{... | collective-permute-start | bytes 147464 | tf_op jit(solution)/shard_map/ppermute | solution.py:23
  12.2 5.8 %collective-permute-start.2 = (f32[1,1,48,128]{3,2,1,0:T(8,128)S(1)}, f32[1,1,48,128]{3,2,1,0:T(8,128)S(1)}, u32[]{:S(2)}, u32[]{:S(2)}) collective-permute-start(f32[1,1,48,128]{3,2,1,0:T(8,128)S(1)} %get-tuple-element.27), channel_id=1, source_target_pairs={{0,18},{16,2},{1,19},{17,3}} | collective-permute-start | bytes 73736 | tf_op jit(solution)/shard_map/ppermute | solution.py:36
  18.1 4.1 %collective-permute-start.5 = (f32[2,48,128]{2,1,0:T(8,128)S(1)}, f32[2,48,128]{2,1,0:T(8,128)S(1)}, u32[]{:S(2)}, u32[]{:S(2)}) collective-permute-start(f32[2,48,128]{2,1,0:T(8,128)S(1)} %get-tuple-element.29), channel_id=1, source_target_pairs={{0,12},{4,0},{8,4},{12,8},{1,13},{5,1},{9,5},{13,9},{2,14},{6,2},{... | collective-permute-start | bytes 147464 | tf_op jit(solution)/shard_map/ppermute | solution.py:23
  18.1 4.7 %collective-permute-start.6 = (f32[4,24,128]{2,1,0:T(8,128)S(1)}, f32[4,24,128]{2,1,0:T(8,128)S(1)}, u32[]{:S(2)}, u32[]{:S(2)}) collective-permute-start(f32[4,24,128]{2,1,0:T(8,128)S(1)} %get-tuple-element.30), channel_id=1, source_target_pairs={{0,2},{2,0},{1,3},{3,1},{4,6},{6,4},{5,7},{7,5},{8,10},{10,8},{9,1... | collective-permute-start | bytes 147464 | tf_op jit(solution)/shard_map/ppermute | solution.py:21
  22.2 4.1 %collective-permute-start.1 = (f32[1,1,48,128]{3,2,1,0:T(8,128)S(1)}, f32[1,1,48,128]{3,2,1,0:T(8,128)S(1)}, u32[]{:S(2)}, u32[]{:S(2)}) collective-permute-start(f32[1,1,48,128]{3,2,1,0:T(8,128)S(1)} %get-tuple-element.27), channel_id=1, source_target_pairs={{2,18},{4,20},{6,22},{8,24},{10,26},{12,28},{14,30},{18,2},{20,4},... | collective-permute-start | bytes 73736 | tf_op jit(solution)/shard_map/ppermute | solution.py:34
  22.9 8.2 %collective-permute-start.3 = (f32[1,1,48,128]{3,2,1,0:T(8,128)S(1)}, f32[1,1,48,128]{3,2,1,0:T(8,128)S(1)}, u32[]{:S(2)}, u32[]{:S(2)}) collective-permute-start(f32[1,1,48,128]{3,2,1,0:T(8,128)S(1)} %collective-permute-done.2), channel_id=1, source_target_pairs={{2,0},{18,16},{3,1},{19,17}} | collective-permute-start | bytes 73736 | tf_op jit(solution)/shard_map/ppermute | solution.py:37
  25.0 20.4 %copy-start.2 = (s32[1,24,48,128]{3,2,1,0:T(8,128)S(1)}, s32[1,24,48,128]{3,2,1,0:T(8,128)}, u32[]{:S(2)}) copy-start(s32[1,24,48,128]{3,2,1,0:T(8,128)} %refs_2_.7) | copy-start | bytes 1769476
  25.1 20.4 %collective-permute-start.9 = (f32[1,24,48,128]{3,2,1,0:T(8,128)S(1)}, f32[1,24,48,128]{3,2,1,0:T(8,128)S(1)}, u32[]{:S(2)}, u32[]{:S(2)}) collective-permute-start(f32[1,24,48,128]{3,2,1,0:T(8,128)S(1)} %get-tuple-element.32.refs_11_.refs_12_), channel_id=1, source_target_pairs={{0,16},{16,0},{1,17},{17,1},{2,18},{18,2},{3,19},{19,3},{4,20},{20... | collective-permute-start | bytes 1769480 | tf_op jit(solution)/shard_map/ppermute | solution.py:21
  32.8 12.7 %collective-permute-start.13 = (f32[1,24,48,128]{3,2,1,0:T(8,128)S(1)}, f32[1,24,48,128]{3,2,1,0:T(8,128)S(1)}, u32[]{:S(2)}, u32[]{:S(2)}) collective-permute-start(f32[1,24,48,128]{3,2,1,0:T(8,128)S(1)} %get-tuple-element.38), channel_id=1, source_target_pairs={{0,1},{1,0},{2,3},{3,2},{4,5},{5,4},{6,7},{7,6},{8,9},{9,8},{10,11... | collective-permute-start | bytes 1769480 | tf_op jit(solution)/shard_map/ppermute | solution.py:21
  32.8 20.5 %collective-permute-start.14 = (f32[1,20,48,128]{3,2,1,0:T(8,128)S(1)}, f32[1,20,48,128]{3,2,1,0:T(8,128)S(1)}, u32[]{:S(2)}, u32[]{:S(2)}) collective-permute-start(f32[1,20,48,128]{3,2,1,0:T(8,128)S(1)} %get-tuple-element.42), channel_id=1, source_target_pairs={{0,16},{16,0},{1,17},{17,1},{2,18},{18,2},{3,19},{19,3},{4,20},{20... | collective-permute-start | bytes 1474568 | tf_op jit(solution)/shard_map/ppermute | solution.py:21
  34.0 6.3 %collective-permute-start.10 = (f32[2,48,128]{2,1,0:T(8,128)S(1)}, f32[2,48,128]{2,1,0:T(8,128)S(1)}, u32[]{:S(2)}, u32[]{:S(2)}) collective-permute-start(f32[2,48,128]{2,1,0:T(8,128)S(1)} %get-tuple-element.35), channel_id=1, source_target_pairs={{0,4},{4,8},{8,12},{12,0},{1,5},{5,9},{9,13},{13,1},{2,6},{6,10},{... | collective-permute-start | bytes 147464 | tf_op jit(solution)/shard_map/ppermute | solution.py:23
  36.2 4.8 %collective-permute-start.11 = (f32[2,48,128]{2,1,0:T(8,128)S(1)}, f32[2,48,128]{2,1,0:T(8,128)S(1)}, u32[]{:S(2)}, u32[]{:S(2)}) collective-permute-start(f32[2,48,128]{2,1,0:T(8,128)S(1)} %get-tuple-element.36), channel_id=1, source_target_pairs={{0,12},{4,0},{8,4},{12,8},{1,13},{5,1},{9,5},{13,9},{2,14},{6,2},{... | collective-permute-start | bytes 147464 | tf_op jit(solution)/shard_map/ppermute | solution.py:23
  40.3 14.3 %collective-permute-start.15 = (f32[1,4,48,128]{3,2,1,0:T(8,128)S(1)}, f32[1,4,48,128]{3,2,1,0:T(8,128)S(1)}, u32[]{:S(2)}, u32[]{:S(2)}) collective-permute-start(f32[1,4,48,128]{3,2,1,0:T(8,128)S(1)} %get-tuple-element.43), channel_id=1, source_target_pairs={{0,16},{16,0},{1,17},{17,1},{2,18},{18,2},{3,19},{19,3},{4,20},{20... | collective-permute-start | bytes 294920 | tf_op jit(solution)/shard_map/ppermute | solution.py:21
  40.9 4.5 %collective-permute-start.12 = (f32[4,24,128]{2,1,0:T(8,128)S(1)}, f32[4,24,128]{2,1,0:T(8,128)S(1)}, u32[]{:S(2)}, u32[]{:S(2)}) collective-permute-start(f32[4,24,128]{2,1,0:T(8,128)S(1)} %get-tuple-element.37), channel_id=1, source_target_pairs={{0,2},{2,0},{1,3},{3,1},{4,6},{6,4},{5,7},{7,5},{8,10},{10,8},{9,1... | collective-permute-start | bytes 147464 | tf_op jit(solution)/shard_map/ppermute | solution.py:21

commit v7 on v6

--- a/solution.py
+++ b/solution.py
@@ -23,19 +23,28 @@
     return lax.ppermute(up, axis, ring(axis, 1)), lax.ppermute(down, axis, ring(axis, -1))
 
 
-def row_swap(row):
-    ys, zs = lax.axis_size("gy"), lax.axis_size("gz")
-    axes = ("grp", "gy", "gz")
-
-    def at(g, y, z):
-        return (g * ys + y) * zs + z
-
-    straight = [(at(g, y, z), at(1 - g, y, z)) for g in range(2) for y in range(ys) for z in range(zs) if zs < 2 or y + z > 0]
-    parts = [lax.ppermute(row, axes, straight)]
+def part_swap(part):
+    ys, zs, ws = lax.axis_size("gy"), lax.axis_size("gz"), lax.axis_size("wa")
+    axes = ("grp", "gy", "gz", "wa")
+
+    def at(g, y, z, w):
+        return ((g * ys + y) * zs + z) * ws + w
+
+    def middle(g, w):
+        return at(1 - g, 0, 1, w) if w == 0 or ys == 1 else at(1 - g, 1, 0, w)
+
+    cells = [(g, y, z, w) for g in range(2) for y in range(ys) for z in range(zs) for w in range(ws)]
+    straight = [(at(g, y, z, w), at(1 - g, y, z, w)) for g, y, z, w in cells if zs < 2 or y + z > 0]
+    parts = [lax.ppermute(part, axes, straight)]
     if zs > 1:
-        row = lax.ppermute(row, axes, [(at(g, 0, 0), at(1 - g, 0, 1)) for g in range(2)])
-        parts.append(lax.ppermute(row, axes, [(at(g, 0, 1), at(g, 0, 0)) for g in range(2)]))
+        ends = [(g, w) for g in range(2) for w in range(ws)]
+        part = lax.ppermute(part, axes, [(at(g, 0, 0, w), middle(g, w)) for g, w in ends])
+        parts.append(lax.ppermute(part, axes, [(middle(g, w), at(1 - g, 0, 0, w)) for g, w in ends]))
     return parts
+
+
+def part_lines(c):
+    return c + c // 3 // 8 * 8
 
 
 def call(body, name, operands, shapes, flops):
@@ -129,7 +138,7 @@
     count, c, d = g_ref.shape[1:]
     row, lane = iotas(c, d)
 
-    def step(b, u, shift):
+    def step(b, places):
         r = [rates[j, 0, b] for j in range(8)]
         total = ((r[0] + r[1]) + (r[2] + r[3])) + ((r[4] + r[5]) + (r[6] + r[7]))
         f = jnp.where(labels[0, b] == 0, DAMP / total, 0.0)
@@ -137,7 +146,8 @@
         f_ref[0, b] = f
         g_ref[0, b] = g
         if pair:
-            u[0, b - shift] = (r[0] + r[1]) * g
+            for ref, to, lines in places:
+                ref[0, to, :] = ((r[0] + r[1]) * g)[lines]
         else:
             u_refs[0][0, b] = r[0] * g
             u_refs[1][0, b] = r[1] * g
@@ -148,10 +158,14 @@
         gz_ref[3, pl.ds(b, 1), :] = (r[5] * g)[:1]
 
     if pair:
-        rows(0, count - 1, lambda b: step(b, u_refs[0], 0))
-        step(count - 1, u_refs[1], count - 1)
+        most, part = u_refs
+        over = part.shape[1] - c
+        rows(0, count - 2, lambda b: step(b, [(most, pl.ds(pl.multiple_of(b * c, 8), c), slice(None))]))
+        mixed = [(most, pl.ds((count - 2) * c, c - over), slice(0, c - over))]
+        step(count - 2, mixed + ([(part, pl.ds(0, over), slice(c - over, c))] if over else []))
+        step(count - 1, [(part, pl.ds(over, c), slice(None))])
     else:
-        rows(0, count, lambda b: step(b, None, 0))
+        rows(0, count, lambda b: step(b, []))
     up_ref[0] = start[0, count - 1]
     up_ref[1] = rates[2, 0, count - 1] * g_ref[0, count - 1]
     down_ref[0] = start[0, 0]
@@ -208,10 +222,7 @@
     def step(b, v, shift, came=None):
         out = spread(rates, f_ref, cot[0, b], g, up, down, gz_before, gz_after, wa_before, wa_after, 1, b, row, lane)
         if came:
-            for ref in came:
-                out = out + ref[0, 0]
-        elif pair:
-            out = out + u_before[0, b]
+            out = out + came(b)
         else:
             out = out + u_before[0, b] + u_after[0, b]
         h = f_ref[0, b] * out
@@ -228,11 +239,25 @@
         gz_ref[2, pl.ds(b, 1), :] = (rates[4, 0, b] * h)[c - 1 :]
         gz_ref[3, pl.ds(b, 1), :] = (rates[5, 0, b] * h)[:1]
 
-    rows(0, cut, lambda b: step(b, v_refs[:half], 0))
-    stop = count - 1 if pair else count
-    rows(cut, stop, lambda b: step(b, v_refs[half:], cut))
-    if pair:
-        step(stop, v_refs[half:], cut, u_row)
+    if not pair:
+        rows(0, cut, lambda b: step(b, v_refs[:half], 0))
+        rows(cut, count, lambda b: step(b, v_refs[half:], cut))
+    else:
+        over = u_row[0].shape[1] - c
+
+        def part(first, lines):
+            return sum(ref[0, first : first + lines] for ref in u_row)
+
+        def most(b):
+            return u_before[0, pl.ds(pl.multiple_of(b * c, 8), c), :]
+
+        def mixed(b):
+            return jnp.concatenate([u_before[0, pl.ds(b * c, c - over), :], part(0, over)], axis=0)
+
+        rows(0, cut, lambda b: step(b, v_refs[:half], 0, most))
+        rows(cut, count - 2, lambda b: step(b, v_refs[half:], cut, most))
+        step(count - 2, v_refs[half:], cut, mixed if over else most)
+        step(count - 1, v_refs[half:], cut, lambda b: part(over, c))
     up_ref[0] = first[0, count - 1]
     up_ref[1] = rates[2, 0, count - 1] * h_ref[0, count - 1]
     down_ref[0] = first[0, 0]
@@ -298,10 +323,10 @@
 
     start_before, start_after = both_ways(start, start, "grp")
     f, g, w0, up, down, gz, *u = call(
-        functools.partial(prepare_body, pair), "prepare", [rates, labels, cotangent, start], [block] * 3 + faces + ([(1, b - 1, c, d), (1, 1, c, d)] if pair else blocks), 20 * cells
+        functools.partial(prepare_body, pair), "prepare", [rates, labels, cotangent, start], [block] * 3 + faces + ([(1, b * c - part_lines(c), d), (1, part_lines(c), d)] if pair else blocks), 20 * cells
     )
     u_before, u_after = both_ways(u[0], u[0] if pair else u[1], "grp")
-    u_row = row_swap(u[1]) if pair else []
+    u_row = part_swap(u[1]) if pair else []
     up0, down0 = both_ways(up, down, "gy")
     gz_before0, gz_after0 = both_ways(gz, gz, "gz")
     wa0 = both_ways(w0, w0, "wa")

time: 55.6 us -> 55.4 us (level)
  starting transfers between devices: 23.6 us -> 22.8 us
  waiting for transfers between devices: 15.1 us -> 15.9 us
    ppermute x9, starting transfers between devices: 11.1 us -> 10.1 us  [both_ways(): other = lax.ppermute(up, axis, ring(axis, 1))]
where the time goes in v7:
time: 55.4 us; the launch traced here: 55.1 us
  starting transfers between devices  22.8 us (41%)
  waiting for transfers between devices  15.9 us (29%)
  Pallas kernels  9.36 us (17%)
  local copies, waits for them, and re-layouts  5.54 us (10%)
  between operations  0.76 us (1%)
  other arithmetic  0.65 us (1%)
    ppermute x9, starting transfers between devices, both_ways(): other = lax.ppermute(up, axis, ring(axis, 1))  10.1 us
    pallas_call x4, Pallas kernels, call(): pl.pallas_call(kernel, out_shape=[jax.ShapeDtypeStruct(s, jnp.float32) fo...  8.52 us
    unnamed x14, local copies, waits for them, and re-layouts  5.54 us
    ppermute x9, waiting for transfers between devices, both_ways(): other = lax.ppermute(up, axis, ring(axis, 1))  5.32 us
    ppermute x1, waiting for transfers between devices, part_swap(): lax.ppermute(part, axes, [(middle(g, w), at(1 - g, 0, 0, w)) for g, w in...  4.84 us
    ppermute x2, starting transfers between devices, both_ways(): lax.ppermute(up, axis, ring(axis, 1))  4.72 us
    ppermute x1, starting transfers between devices, part_swap(): lax.ppermute(part, axes, [(at(g, 0, 0, w), middle(g, w)) for g, w in ends])  4.34 us
    ppermute x2, waiting for transfers between devices, both_ways(): lax.ppermute(up, axis, ring(axis, 1))  2.19 us
  transfers between devices with their start and end apart: 16, of which 7 were waited for; matrix products, arithmetic and copies ran while one was open for 0% of the time, Pallas kernels for 17%

profile of v7, /device:TPU:0, one launch (start us, length us, event | category | flops | bytes accessed | tf_op | source)
XLA Modules:
  0.0 55.1 jit_solution(8233515391730503397)
XLA Ops:
  0.6 3.0 %collective-permute-start.8 = (f32[1,24,48,128]{3,2,1,0:T(8,128)}, f32[1,24,48,128]{3,2,1,0:T(8,128)S(1)}, u32[]{:S(2)}, u32[]{:S(2)}) collective-permute-start(f32[1,24,48,128]{3,2,1,0:T(8,128)} %refs_6_.1), channel_id=1, source_target_pairs={{0,16},{16,0},{1,17},{17,1},{2,18},{18,2},{3,19},{19,3},{4,20},{20... | collective-permute-start | bytes 1769480 | tf_op jit(solution)/shard_map/ppermute | solution.py:21
  3.7 0.0 copy-start
  3.7 2.3 %copy-done = f32[8,1,24,48,128]{4,3,2,1,0:T(8,128)S(1)} copy-done((f32[8,1,24,48,128]{4,3,2,1,0:T(8,128)S(1)}, f32[8,1,24,48,128]{4,3,2,1,0:T(8,128)}, u32[]{:S(2)}) %copy-start) | copy-done | bytes 4718616
  6.0 0.0 copy-start.1
  6.0 1.1 %copy-done.1 = s32[1,24,48,128]{3,2,1,0:T(8,128)S(1)} copy-done((s32[1,24,48,128]{3,2,1,0:T(8,128)S(1)}, s32[1,24,48,128]{3,2,1,0:T(8,128)}, u32[]{:S(2)}) %copy-start.1) | copy-done | bytes 589848
  7.1 0.0 copy-start.3
  7.1 1.1 %copy-done.3 = f32[1,24,48,128]{3,2,1,0:T(8,128)S(1)} copy-done((f32[1,24,48,128]{3,2,1,0:T(8,128)S(1)}, f32[1,24,48,128]{3,2,1,0:T(8,128)}, u32[]{:S(2)}) %copy-start.3) | copy-done | bytes 589848
  8.1 0.0 copy-start.5
  8.1 1.1 %copy-done.5 = f32[1,24,48,128]{3,2,1,0:T(8,128)S(1)} copy-done((f32[1,24,48,128]{3,2,1,0:T(8,128)S(1)}, f32[1,24,48,128]{3,2,1,0:T(8,128)}, u32[]{:S(2)}) %copy-start.5) | copy-done | bytes 589848
  9.2 0.0 copy-start.4
  9.2 0.8 %prepare.1 = (f32[1,24,48,128]{3,2,1,0:T(8,128)S(1)}, f32[1,24,48,128]{3,2,1,0:T(8,128)S(1)}, f32[1,24,48,128]{3,2,1,0:T(8,128)S(1)}, f32[2,48,128]{2,1,0:T(8,12...) custom-call(f32[8,1,24,48,128]{4,3,2,1,0:T(8,128)S(1)} %copy-done, ...), custom_call_target="tpu_custom_call" | custom-call | flops 2949120 | bytes 8994816 | tf_op jit(solution)/shard_map/prepare/pallas_call | solution.py:66
  10.0 0.0 copy-start.6
  10.0 0.1 collective-permute-start.7
  10.1 0.1 collective-permute-start
  10.2 2.1 %collective-permute-start.4 = (f32[2,48,128]{2,1,0:T(8,128)S(1)}, f32[2,48,128]{2,1,0:T(8,128)S(1)}, u32[]{:S(2)}, u32[]{:S(2)}) collective-permute-start(f32[2,48,128]{2,1,0:T(8,128)S(1)} %get-tuple-element.28), channel_id=1, source_target_pairs={{0,4},{4,8},{8,12},{12,0},{1,5},{5,9},{9,13},{13,1},{2,6},{6,10},{... | collective-permute-start | bytes 147464 | tf_op jit(solution)/shard_map/ppermute | solution.py:23
  12.2 4.3 %collective-permute-start.2 = (f32[1,64,128]{2,1,0:T(8,128)S(1)}, f32[1,64,128]{2,1,0:T(8,128)S(1)}, u32[]{:S(2)}, u32[]{:S(2)}) collective-permute-start(f32[1,64,128]{2,1,0:T(8,128)S(1)} %get-tuple-element.27), channel_id=1, source_target_pairs={{0,18},{1,21},{16,2},{17,5}} | collective-permute-start | bytes 98312 | tf_op jit(solution)/shard_map/ppermute | solution.py:41
  16.6 1.7 %collective-permute-done.2 = f32[1,64,128]{2,1,0:T(8,128)S(1)} collective-permute-done((f32[1,64,128]{2,1,0:T(8,128)S(1)}, f32[1,64,128]{2,1,0:T(8,128)S(1)}, u32[]{:S(2)}, u32[]{:S(2)}) %collective-permute-start.2) | collective-permute-done | bytes 32800 | tf_op jit(solution)/shard_map/ppermute | solution.py:41
  18.3 0.0 collective-permute-start.5
  18.3 0.0 collective-permute-done.4.refs_5_.refs_7_.refs_8_
  18.3 2.2 %collective-permute-start.6 = (f32[4,24,128]{2,1,0:T(8,128)S(1)}, f32[4,24,128]{2,1,0:T(8,128)S(1)}, u32[]{:S(2)}, u32[]{:S(2)}) collective-permute-start(f32[4,24,128]{2,1,0:T(8,128)S(1)} %get-tuple-element.30), channel_id=1, source_target_pairs={{0,2},{2,0},{1,3},{3,1},{4,6},{6,4},{5,7},{7,5},{8,10},{10,8},{9,1... | collective-permute-start | bytes 147464 | tf_op jit(solution)/shard_map/ppermute | solution.py:21
  20.5 1.9 %collective-permute-done.5.refs_6_.refs_8_.refs_9_ = f32[2,48,128]{2,1,0:T(8,128)S(1)} collective-permute-done((f32[2,48,128]{2,1,0:T(8,128)S(1)}, f32[2,48,128]{2,1,0:T(8,128)S(1)}, u32[]{:S(2)}, u32[]{:S(2)}) %collective-permute-start.5) | collective-permute-done | bytes 49184 | tf_op jit(solution)/shard_map/ppermute | solution.py:23
  22.4 0.7 %collective-permute-start.1 = (f32[1,64,128]{2,1,0:T(8,128)S(1)}, f32[1,64,128]{2,1,0:T(8,128)S(1)}, u32[]{:S(2)}, u32[]{:S(2)}) collective-permute-start(f32[1,64,128]{2,1,0:T(8,128)S(1)} %get-tuple-element.27), channel_id=1, source_target_pairs={{2,18},{3,19},{4,20},{5,21},{6,22},{7,23},{8,24},{9,25},{10,26},{1... | collective-permute-start | bytes 98312 | tf_op jit(solution)/shard_map/ppermute | solution.py:38
  23.1 0.0 collective-permute-done.6.refs_7_.refs_9_.refs_10_
  23.1 1.3 %collective-permute-start.3 = (f32[1,64,128]{2,1,0:T(8,128)S(1)}, f32[1,64,128]{2,1,0:T(8,128)S(1)}, u32[]{:S(2)}, u32[]{:S(2)}) collective-permute-start(f32[1,64,128]{2,1,0:T(8,128)S(1)} %collective-permute-done.2), channel_id=1, source_target_pairs={{18,16},{21,17},{2,0},{5,1}} | collective-permute-start | bytes 98312 | tf_op jit(solution)/shard_map/ppermute | solution.py:42
  24.4 0.0 collective-permute-done.8.refs_4_.refs_7_
  24.4 0.0 collective-permute-done.7.refs_8_.refs_10_.refs_11_
  24.4 0.0 copy-done.4
  24.4 0.9 %forward.1 = (f32[1,24,48,128]{3,2,1,0:T(8,128)S(1)}, f32[1,24,48,128]{3,2,1,0:T(8,128)S(1)}) custom-call(f32[8,1,24,48,128]{4,3,2,1,0:T(8,128)S(1)} %copy-done, f32[1,24,48,128]{3,2,1,0:T(8,128)S(1)} %get-tuple-element.24.refs_1_, s32[1,24,48,128]{3,2,1,0:T(8,128)S(1)} %copy-done.1, f32[1,24,48,128]{3,2,1,0:T(8,128)S(1)} %copy-done.4, ...), custom_call_target="tpu_custom_call" | custom-call | flops 4423680 | bytes 8994816 | tf_op jit(solution)/shard_map/forward/pallas_call | solution.py:66
  25.3 0.0 copy-start.2
  25.3 1.3 %collective-permute-start.9 = (f32[1,24,48,128]{3,2,1,0:T(8,128)S(1)}, f32[1,24,48,128]{3,2,1,0:T(8,128)S(1)}, u32[]{:S(2)}, u32[]{:S(2)}) collective-permute-start(f32[1,24,48,128]{3,2,1,0:T(8,128)S(1)} %get-tuple-element.32.refs_11_.refs_12_), channel_id=1, source_target_pairs={{0,16},{16,0},{1,17},{17,1},{2,18},{18,2},{3,19},{19,3},{4,20},{20... | collective-permute-start | bytes 1769480 | tf_op jit(solution)/shard_map/ppermute | solution.py:21
  26.6 0.0 collective-permute-done.1.refs_5_
  26.6 4.8 %collective-permute-done.3.refs_6_ = f32[1,64,128]{2,1,0:T(8,128)S(1)} collective-permute-done((f32[1,64,128]{2,1,0:T(8,128)S(1)}, f32[1,64,128]{2,1,0:T(8,128)S(1)}, u32[]{:S(2)}, u32[]{:S(2)}) %collective-permute-start.3) | collective-permute-done | bytes 32800 | tf_op jit(solution)/shard_map/ppermute | solution.py:42
  31.4 0.0 collective-permute-done.refs_4_
  31.4 0.0 copy-done.6
  31.4 1.6 %backward.1 = (f32[1,24,48,128]{3,2,1,0:T(8,128)S(1)}, f32[1,24,48,128]{3,2,1,0:T(8,128)S(1)}, f32[1,24,48,128]{3,2,1,0:T(8,128)S(1)}, f32[2,48,128]{2,1,0:T(8,1...) custom-call(f32[8,1,24,48,128]{4,3,2,1,0:T(8,128)S(1)} %copy-done, ...), custom_call_target="tpu_custom_call" | custom-call | flops 4423680 | bytes 10944512 | tf_op jit(solution)/shard_map/backward/pallas_call | solution.py:66
  33.1 0.1 collective-permute-start.13
  33.1 0.6 %collective-permute-start.14 = (f32[1,20,48,128]{3,2,1,0:T(8,128)S(1)}, f32[1,20,48,128]{3,2,1,0:T(8,128)S(1)}, u32[]{:S(2)}, u32[]{:S(2)}) collective-permute-start(f32[1,20,48,128]{3,2,1,0:T(8,128)S(1)} %get-tuple-element.42), channel_id=1, source_target_pairs={{0,16},{16,0},{1,17},{17,1},{2,18},{18,2},{3,19},{19,3},{4,20},{20... | collective-permute-start | bytes 1474568 | tf_op jit(solution)/shard_map/ppermute | solution.py:21
  33.8 2.6 %collective-permute-start.10 = (f32[2,48,128]{2,1,0:T(8,128)S(1)}, f32[2,48,128]{2,1,0:T(8,128)S(1)}, u32[]{:S(2)}, u32[]{:S(2)}) collective-permute-start(f32[2,48,128]{2,1,0:T(8,128)S(1)} %get-tuple-element.35), channel_id=1, source_target_pairs={{0,4},{4,8},{8,12},{12,0},{1,5},{5,9},{9,13},{13,1},{2,6},{6,10},{... | collective-permute-start | bytes 147464 | tf_op jit(solution)/shard_map/ppermute | solution.py:23
  36.4 1.7 %collective-permute-start.11 = (f32[2,48,128]{2,1,0:T(8,128)S(1)}, f32[2,48,128]{2,1,0:T(8,128)S(1)}, u32[]{:S(2)}, u32[]{:S(2)}) collective-permute-start(f32[2,48,128]{2,1,0:T(8,128)S(1)} %get-tuple-element.36), channel_id=1, source_target_pairs={{0,12},{4,0},{8,4},{12,8},{1,13},{5,1},{9,5},{13,9},{2,14},{6,2},{... | collective-permute-start | bytes 147464 | tf_op jit(solution)/shard_map/ppermute | solution.py:23
  38.1 2.2 %collective-permute-done.10.refs_14_ = f32[2,48,128]{2,1,0:T(8,128)S(1)} collective-permute-done((f32[2,48,128]{2,1,0:T(8,128)S(1)}, f32[2,48,128]{2,1,0:T(8,128)S(1)}, u32[]{:S(2)}, u32[]{:S(2)}) %collective-permute-start.10) | collective-permute-done | bytes 49184 | tf_op jit(solution)/shard_map/ppermute | solution.py:23
  40.3 0.9 %collective-permute-start.15 = (f32[1,4,48,128]{3,2,1,0:T(8,128)S(1)}, f32[1,4,48,128]{3,2,1,0:T(8,128)S(1)}, u32[]{:S(2)}, u32[]{:S(2)}) collective-permute-start(f32[1,4,48,128]{3,2,1,0:T(8,128)S(1)} %get-tuple-element.43), channel_id=1, source_target_pairs={{0,16},{16,0},{1,17},{17,1},{2,18},{18,2},{3,19},{19,3},{4,20},{20... | collective-permute-start | bytes 294920 | tf_op jit(solution)/shard_map/ppermute | solution.py:21
  41.2 0.0 collective-permute-done.11.refs_15_
  41.2 1.8 %collective-permute-start.12 = (f32[4,24,128]{2,1,0:T(8,128)S(1)}, f32[4,24,128]{2,1,0:T(8,128)S(1)}, u32[]{:S(2)}, u32[]{:S(2)}) collective-permute-start(f32[4,24,128]{2,1,0:T(8,128)S(1)} %get-tuple-element.37), channel_id=1, source_target_pairs={{0,2},{2,0},{1,3},{3,1},{4,6},{6,4},{5,7},{7,5},{8,10},{10,8},{9,1... | collective-permute-start | bytes 147464 | tf_op jit(solution)/shard_map/ppermute | solution.py:21
  43.0 2.3 %collective-permute-done.12.refs_16_ = f32[4,24,128]{2,1,0:T(8,128)S(1)} collective-permute-done((f32[4,24,128]{2,1,0:T(8,128)S(1)}, f32[4,24,128]{2,1,0:T(8,128)S(1)}, u32[]{:S(2)}, u32[]{:S(2)}) %collective-permute-start.12) | collective-permute-done | bytes 49184 | tf_op jit(solution)/shard_map/ppermute | solution.py:21
  45.3 0.0 collective-permute-done.9.refs_13_
  45.3 0.0 collective-permute-done.13.refs_17_
  45.3 0.0 copy-done.2
  45.3 5.3 %last.1 = (f32[1,24,48,128]{3,2,1,0:T(8,128)}, f32[8,1,24,48,128]{4,3,2,1,0:T(8,128)}, f32[1,24,48,128]{3,2,1,0:T(8,128)S(1)}) custom-call(f32[8,1,24,48,128]{4,3,2,1,0:T(8,128)S(1)} %copy-done, f32[1,24,48,128]{3,2,1,0:T(8,128)S(1)} %get-tuple-element.24.refs_1_, s32[1,24,48,128]{3,2,1,0:T(8,128)S(1)} %copy-done.2, ...), custom_call_target="tpu_custom_call" | custom-call | flops 17694720 | bytes 17989632 | tf_op jit(solution)/shard_map/last/pallas_call | solution.py:66
  50.6 2.6 %collective-permute-done.14.refs_1_ = f32[1,20,48,128]{3,2,1,0:T(8,128)S(1)} collective-permute-done((f32[1,20,48,128]{3,2,1,0:T(8,128)S(1)}, f32[1,20,48,128]{3,2,1,0:T(8,128)S(1)}, u32[]{:S(2)}, u32[]{:S(2)}) %collective-permute-start.14) | collective-permute-done | bytes 491552 | tf_op jit(solution)/shard_map/ppermute | solution.py:21
  53.1 0.8 %finish.1 = f32[1,24,48,128]{3,2,1,0:T(8,128)} custom-call(f32[1,24,48,128]{3,2,1,0:T(8,128)S(1)} %get-tuple-element.41.refs_0_, f32[1,20,48,128]{3,2,1,0:T(8,128)S(1)} %collective-permute-done.14.refs_1_), custom_call_target="tpu_custom_call" | custom-call | tf_op jit(solution)/shard_map/finish/pallas_call | solution.py:304
  54.0 0.4 collective-permute-done.15
  54.4 0.7 %add_dynamic-update-slice_fusion = f32[1,24,48,128]{3,2,1,0:T(8,128)} fusion(f32[1,24,48,128]{3,2,1,0:T(8,128)} %finish.1, f32[1,4,48,128]{3,2,1,0:T(8,128)S(1)} %collective-permute-done.15, f32[1,24,48,128]{3,2,1,0:T(8,128)S(1)} %get-tuple-element.41.refs_0_), kind=kLoop, calls=%fused_computation | loop fusion | flops 24576 | bytes 294912 | tf_op jit(solution)/shard_map/dynamic_update_slice | solution.py:367
Async XLA Ops:
  0.6 23.7 %collective-permute-start.8 = (f32[1,24,48,128]{3,2,1,0:T(8,128)}, f32[1,24,48,128]{3,2,1,0:T(8,128)S(1)}, u32[]{:S(2)}, u32[]{:S(2)}) collective-permute-start(f32[1,24,48,128]{3,2,1,0:T(8,128)} %refs_6_.1), channel_id=1, source_target_pairs={{0,16},{16,0},{1,17},{17,1},{2,18},{18,2},{3,19},{19,3},{4,20},{20... | collective-permute-start | bytes 1769480 | tf_op jit(solution)/shard_map/ppermute | solution.py:21
  3.7 2.3 %copy-start = (f32[8,1,24,48,128]{4,3,2,1,0:T(8,128)S(1)}, f32[8,1,24,48,128]{4,3,2,1,0:T(8,128)}, u32[]{:S(2)}) copy-start(f32[8,1,24,48,128]{4,3,2,1,0:T(8,128)} %refs_0_.7) | copy-start | bytes 14155780
  6.0 1.1 %copy-start.1 = (s32[1,24,48,128]{3,2,1,0:T(8,128)S(1)}, s32[1,24,48,128]{3,2,1,0:T(8,128)}, u32[]{:S(2)}) copy-start(s32[1,24,48,128]{3,2,1,0:T(8,128)} %refs_2_.7) | copy-start | bytes 1769476
  7.1 1.1 %copy-start.3 = (f32[1,24,48,128]{3,2,1,0:T(8,128)S(1)}, f32[1,24,48,128]{3,2,1,0:T(8,128)}, u32[]{:S(2)}) copy-start(f32[1,24,48,128]{3,2,1,0:T(8,128)} %refs_6_.1) | copy-start | bytes 1769476
  8.1 1.1 %copy-start.5 = (f32[1,24,48,128]{3,2,1,0:T(8,128)S(1)}, f32[1,24,48,128]{3,2,1,0:T(8,128)}, u32[]{:S(2)}) copy-start(f32[1,24,48,128]{3,2,1,0:T(8,128)} %refs_2_.6) | copy-start | bytes 1769476
  9.2 15.2 %copy-start.4 = (f32[1,24,48,128]{3,2,1,0:T(8,128)S(1)}, f32[1,24,48,128]{3,2,1,0:T(8,128)}, u32[]{:S(2)}) copy-start(f32[1,24,48,128]{3,2,1,0:T(8,128)} %refs_6_.1) | copy-start | bytes 1769476
  10.0 21.4 %copy-start.6 = (f32[1,24,48,128]{3,2,1,0:T(8,128)S(1)}, f32[1,24,48,128]{3,2,1,0:T(8,128)}, u32[]{:S(2)}) copy-start(f32[1,24,48,128]{3,2,1,0:T(8,128)} %refs_2_.6) | copy-start | bytes 1769476
  10.0 14.4 %collective-permute-start.7 = (f32[1,24,48,128]{3,2,1,0:T(8,128)S(1)}, f32[1,24,48,128]{3,2,1,0:T(8,128)S(1)}, u32[]{:S(2)}, u32[]{:S(2)}) collective-permute-start(f32[1,24,48,128]{3,2,1,0:T(8,128)S(1)} %get-tuple-element.31), channel_id=1, source_target_pairs={{0,1},{1,0},{2,3},{3,2},{4,5},{5,4},{6,7},{7,6},{8,9},{9,8},{10,11... | collective-permute-start | bytes 1769480 | tf_op jit(solution)/shard_map/ppermute | solution.py:21
  10.1 21.4 %collective-permute-start = (f32[1,1088,128]{2,1,0:T(8,128)S(1)}, f32[1,1088,128]{2,1,0:T(8,128)S(1)}, u32[]{:S(2)}, u32[]{:S(2)}) collective-permute-start(f32[1,1088,128]{2,1,0:T(8,128)S(1)} %get-tuple-element.26), channel_id=1, source_target_pairs={{0,16},{16,0},{1,17},{17,1},{2,18},{18,2},{3,19},{19,3},{4,20},{20... | collective-permute-start | bytes 1671176 | tf_op jit(solution)/shard_map/ppermute | solution.py:21
  10.2 8.2 %collective-permute-start.4 = (f32[2,48,128]{2,1,0:T(8,128)S(1)}, f32[2,48,128]{2,1,0:T(8,128)S(1)}, u32[]{:S(2)}, u32[]{:S(2)}) collective-permute-start(f32[2,48,128]{2,1,0:T(8,128)S(1)} %get-tuple-element.28), channel_id=1, source_target_pairs={{0,4},{4,8},{8,12},{12,0},{1,5},{5,9},{9,13},{13,1},{2,6},{6,10},{... | collective-permute-start | bytes 147464 | tf_op jit(solution)/shard_map/ppermute | solution.py:23
  12.2 6.1 %collective-permute-start.2 = (f32[1,64,128]{2,1,0:T(8,128)S(1)}, f32[1,64,128]{2,1,0:T(8,128)S(1)}, u32[]{:S(2)}, u32[]{:S(2)}) collective-permute-start(f32[1,64,128]{2,1,0:T(8,128)S(1)} %get-tuple-element.27), channel_id=1, source_target_pairs={{0,18},{1,21},{16,2},{17,5}} | collective-permute-start | bytes 98312 | tf_op jit(solution)/shard_map/ppermute | solution.py:41
  18.3 4.1 %collective-permute-start.5 = (f32[2,48,128]{2,1,0:T(8,128)S(1)}, f32[2,48,128]{2,1,0:T(8,128)S(1)}, u32[]{:S(2)}, u32[]{:S(2)}) collective-permute-start(f32[2,48,128]{2,1,0:T(8,128)S(1)} %get-tuple-element.29), channel_id=1, source_target_pairs={{0,12},{4,0},{8,4},{12,8},{1,13},{5,1},{9,5},{13,9},{2,14},{6,2},{... | collective-permute-start | bytes 147464 | tf_op jit(solution)/shard_map/ppermute | solution.py:23
  18.3 4.7 %collective-permute-start.6 = (f32[4,24,128]{2,1,0:T(8,128)S(1)}, f32[4,24,128]{2,1,0:T(8,128)S(1)}, u32[]{:S(2)}, u32[]{:S(2)}) collective-permute-start(f32[4,24,128]{2,1,0:T(8,128)S(1)} %get-tuple-element.30), channel_id=1, source_target_pairs={{0,2},{2,0},{1,3},{3,1},{4,6},{6,4},{5,7},{7,5},{8,10},{10,8},{9,1... | collective-permute-start | bytes 147464 | tf_op jit(solution)/shard_map/ppermute | solution.py:21
  22.4 4.2 %collective-permute-start.1 = (f32[1,64,128]{2,1,0:T(8,128)S(1)}, f32[1,64,128]{2,1,0:T(8,128)S(1)}, u32[]{:S(2)}, u32[]{:S(2)}) collective-permute-start(f32[1,64,128]{2,1,0:T(8,128)S(1)} %get-tuple-element.27), channel_id=1, source_target_pairs={{2,18},{3,19},{4,20},{5,21},{6,22},{7,23},{8,24},{9,25},{10,26},{1... | collective-permute-start | bytes 98312 | tf_op jit(solution)/shard_map/ppermute | solution.py:38
  23.1 8.4 %collective-permute-start.3 = (f32[1,64,128]{2,1,0:T(8,128)S(1)}, f32[1,64,128]{2,1,0:T(8,128)S(1)}, u32[]{:S(2)}, u32[]{:S(2)}) collective-permute-start(f32[1,64,128]{2,1,0:T(8,128)S(1)} %collective-permute-done.2), channel_id=1, source_target_pairs={{18,16},{21,17},{2,0},{5,1}} | collective-permute-start | bytes 98312 | tf_op jit(solution)/shard_map/ppermute | solution.py:42
  25.3 20.1 %copy-start.2 = (s32[1,24,48,128]{3,2,1,0:T(8,128)S(1)}, s32[1,24,48,128]{3,2,1,0:T(8,128)}, u32[]{:S(2)}) copy-start(s32[1,24,48,128]{3,2,1,0:T(8,128)} %refs_2_.7) | copy-start | bytes 1769476
  25.3 20.0 %collective-permute-start.9 = (f32[1,24,48,128]{3,2,1,0:T(8,128)S(1)}, f32[1,24,48,128]{3,2,1,0:T(8,128)S(1)}, u32[]{:S(2)}, u32[]{:S(2)}) collective-permute-start(f32[1,24,48,128]{3,2,1,0:T(8,128)S(1)} %get-tuple-element.32.refs_11_.refs_12_), channel_id=1, source_target_pairs={{0,16},{16,0},{1,17},{17,1},{2,18},{18,2},{3,19},{19,3},{4,20},{20... | collective-permute-start | bytes 1769480 | tf_op jit(solution)/shard_map/ppermute | solution.py:21
  33.1 12.3 %collective-permute-start.13 = (f32[1,24,48,128]{3,2,1,0:T(8,128)S(1)}, f32[1,24,48,128]{3,2,1,0:T(8,128)S(1)}, u32[]{:S(2)}, u32[]{:S(2)}) collective-permute-start(f32[1,24,48,128]{3,2,1,0:T(8,128)S(1)} %get-tuple-element.38), channel_id=1, source_target_pairs={{0,1},{1,0},{2,3},{3,2},{4,5},{5,4},{6,7},{7,6},{8,9},{9,8},{10,11... | collective-permute-start | bytes 1769480 | tf_op jit(solution)/shard_map/ppermute | solution.py:21
  33.1 20.0 %collective-permute-start.14 = (f32[1,20,48,128]{3,2,1,0:T(8,128)S(1)}, f32[1,20,48,128]{3,2,1,0:T(8,128)S(1)}, u32[]{:S(2)}, u32[]{:S(2)}) collective-permute-start(f32[1,20,48,128]{3,2,1,0:T(8,128)S(1)} %get-tuple-element.42), channel_id=1, source_target_pairs={{0,16},{16,0},{1,17},{17,1},{2,18},{18,2},{3,19},{19,3},{4,20},{20... | collective-permute-start | bytes 1474568 | tf_op jit(solution)/shard_map/ppermute | solution.py:21
  33.8 6.5 %collective-permute-start.10 = (f32[2,48,128]{2,1,0:T(8,128)S(1)}, f32[2,48,128]{2,1,0:T(8,128)S(1)}, u32[]{:S(2)}, u32[]{:S(2)}) collective-permute-start(f32[2,48,128]{2,1,0:T(8,128)S(1)} %get-tuple-element.35), channel_id=1, source_target_pairs={{0,4},{4,8},{8,12},{12,0},{1,5},{5,9},{9,13},{13,1},{2,6},{6,10},{... | collective-permute-start | bytes 147464 | tf_op jit(solution)/shard_map/ppermute | solution.py:23
  36.4 4.8 %collective-permute-start.11 = (f32[2,48,128]{2,1,0:T(8,128)S(1)}, f32[2,48,128]{2,1,0:T(8,128)S(1)}, u32[]{:S(2)}, u32[]{:S(2)}) collective-permute-start(f32[2,48,128]{2,1,0:T(8,128)S(1)} %get-tuple-element.36), channel_id=1, source_target_pairs={{0,12},{4,0},{8,4},{12,8},{1,13},{5,1},{9,5},{13,9},{2,14},{6,2},{... | collective-permute-start | bytes 147464 | tf_op jit(solution)/shard_map/ppermute | solution.py:23
  40.3 14.1 %collective-permute-start.15 = (f32[1,4,48,128]{3,2,1,0:T(8,128)S(1)}, f32[1,4,48,128]{3,2,1,0:T(8,128)S(1)}, u32[]{:S(2)}, u32[]{:S(2)}) collective-permute-start(f32[1,4,48,128]{3,2,1,0:T(8,128)S(1)} %get-tuple-element.43), channel_id=1, source_target_pairs={{0,16},{16,0},{1,17},{17,1},{2,18},{18,2},{3,19},{19,3},{4,20},{20... | collective-permute-start | bytes 294920 | tf_op jit(solution)/shard_map/ppermute | solution.py:21
  41.2 4.1 %collective-permute-start.12 = (f32[4,24,128]{2,1,0:T(8,128)S(1)}, f32[4,24,128]{2,1,0:T(8,128)S(1)}, u32[]{:S(2)}, u32[]{:S(2)}) collective-permute-start(f32[4,24,128]{2,1,0:T(8,128)S(1)} %get-tuple-element.37), channel_id=1, source_target_pairs={{0,2},{2,0},{1,3},{3,1},{4,6},{6,4},{5,7},{7,5},{8,10},{10,8},{9,1... | collective-permute-start | bytes 147464 | tf_op jit(solution)/shard_map/ppermute | solution.py:21

commit v8 on v7

--- a/solution.py
+++ b/solution.py
@@ -44,7 +44,7 @@
 
 
 def part_lines(c):
-    return c + c // 3 // 8 * 8
+    return c + c // 2 // 8 * 8
 
 
 def call(body, name, operands, shapes, flops):
@@ -318,7 +318,7 @@
     cells = b * c * d
     pair = lax.axis_size("grp") == 2
     blocks = [block] * (1 if pair else 2)
-    tail = max(1, b // 6)
+    tail = max(2, b // 6)
     faces = [(2, c, d), (2, c, d), (4, b, d)]
 
     start_before, start_after = both_ways(start, start, "grp")

time: 55.4 us -> 55.3 us (level)
  no operation moved by 1% of the time
where the time goes in v8:
time: 55.3 us; the launch traced here: 55 us
  starting transfers between devices  22.7 us (41%)
  waiting for transfers between devices  15.8 us (29%)
  Pallas kernels  9.55 us (17%)
  local copies, waits for them, and re-layouts  5.54 us (10%)
  between operations  0.76 us (1%)
  other arithmetic  0.65 us (1%)
    ppermute x9, starting transfers between devices, both_ways(): other = lax.ppermute(up, axis, ring(axis, 1))  9.94 us
    pallas_call x4, Pallas kernels, call(): pl.pallas_call(kernel, out_shape=[jax.ShapeDtypeStruct(s, jnp.float32) fo...  8.71 us
    unnamed x14, local copies, waits for them, and re-layouts  5.54 us
    ppermute x9, waiting for transfers between devices, both_ways(): other = lax.ppermute(up, axis, ring(axis, 1))  5.05 us
    ppermute x1, waiting for transfers between devices, part_swap(): lax.ppermute(part, axes, [(middle(g, w), at(1 - g, 0, 0, w)) for g, w in...  4.88 us
    ppermute x2, starting transfers between devices, both_ways(): lax.ppermute(up, axis, ring(axis, 1))  4.85 us
    ppermute x1, starting transfers between devices, part_swap(): lax.ppermute(part, axes, [(at(g, 0, 0, w), middle(g, w)) for g, w in ends])  4.34 us
    ppermute x2, waiting for transfers between devices, both_ways(): lax.ppermute(up, axis, ring(axis, 1))  2.19 us
  transfers between devices with their start and end apart: 16, of which 7 were waited for; matrix products, arithmetic and copies ran while one was open for 0% of the time, Pallas kernels for 17%

profile of v8, /device:TPU:0, one launch (start us, length us, event | category | flops | bytes accessed | tf_op | source)
XLA Modules:
  0.0 55.0 jit_solution(13450718708113132291)
XLA Ops:
  0.6 3.0 %collective-permute-start.8 = (f32[1,24,48,128]{3,2,1,0:T(8,128)}, f32[1,24,48,128]{3,2,1,0:T(8,128)S(1)}, u32[]{:S(2)}, u32[]{:S(2)}) collective-permute-start(f32[1,24,48,128]{3,2,1,0:T(8,128)} %refs_6_.1), channel_id=1, source_target_pairs={{0,16},{16,0},{1,17},{17,1},{2,18},{18,2},{3,19},{19,3},{4,20},{20... | collective-permute-start | bytes 1769480 | tf_op jit(solution)/shard_map/ppermute | solution.py:21
  3.7 0.0 copy-start
  3.7 2.3 %copy-done = f32[8,1,24,48,128]{4,3,2,1,0:T(8,128)S(1)} copy-done((f32[8,1,24,48,128]{4,3,2,1,0:T(8,128)S(1)}, f32[8,1,24,48,128]{4,3,2,1,0:T(8,128)}, u32[]{:S(2)}) %copy-start) | copy-done | bytes 4718616
  6.0 0.0 copy-start.1
  6.0 1.1 %copy-done.1 = s32[1,24,48,128]{3,2,1,0:T(8,128)S(1)} copy-done((s32[1,24,48,128]{3,2,1,0:T(8,128)S(1)}, s32[1,24,48,128]{3,2,1,0:T(8,128)}, u32[]{:S(2)}) %copy-start.1) | copy-done | bytes 589848
  7.1 0.0 copy-start.3
  7.1 1.1 %copy-done.3 = f32[1,24,48,128]{3,2,1,0:T(8,128)S(1)} copy-done((f32[1,24,48,128]{3,2,1,0:T(8,128)S(1)}, f32[1,24,48,128]{3,2,1,0:T(8,128)}, u32[]{:S(2)}) %copy-start.3) | copy-done | bytes 589848
  8.1 0.0 copy-start.5
  8.1 1.1 %copy-done.5 = f32[1,24,48,128]{3,2,1,0:T(8,128)S(1)} copy-done((f32[1,24,48,128]{3,2,1,0:T(8,128)S(1)}, f32[1,24,48,128]{3,2,1,0:T(8,128)}, u32[]{:S(2)}) %copy-start.5) | copy-done | bytes 589848
  9.2 0.0 copy-start.4
  9.2 0.8 %prepare.1 = (f32[1,24,48,128]{3,2,1,0:T(8,128)S(1)}, f32[1,24,48,128]{3,2,1,0:T(8,128)S(1)}, f32[1,24,48,128]{3,2,1,0:T(8,128)S(1)}, f32[2,48,128]{2,1,0:T(8,12...) custom-call(f32[8,1,24,48,128]{4,3,2,1,0:T(8,128)S(1)} %copy-done, ...), custom_call_target="tpu_custom_call" | custom-call | flops 2949120 | bytes 8994816 | tf_op jit(solution)/shard_map/prepare/pallas_call | solution.py:66
  10.0 0.0 copy-start.6
  10.0 0.1 collective-permute-start.7
  10.1 0.1 collective-permute-start
  10.2 2.1 %collective-permute-start.4 = (f32[2,48,128]{2,1,0:T(8,128)S(1)}, f32[2,48,128]{2,1,0:T(8,128)S(1)}, u32[]{:S(2)}, u32[]{:S(2)}) collective-permute-start(f32[2,48,128]{2,1,0:T(8,128)S(1)} %get-tuple-element.28), channel_id=1, source_target_pairs={{0,4},{4,8},{8,12},{12,0},{1,5},{5,9},{9,13},{13,1},{2,6},{6,10},{... | collective-permute-start | bytes 147464 | tf_op jit(solution)/shard_map/ppermute | solution.py:23
  12.2 4.3 %collective-permute-start.2 = (f32[1,72,128]{2,1,0:T(8,128)S(1)}, f32[1,72,128]{2,1,0:T(8,128)S(1)}, u32[]{:S(2)}, u32[]{:S(2)}) collective-permute-start(f32[1,72,128]{2,1,0:T(8,128)S(1)} %get-tuple-element.27), channel_id=1, source_target_pairs={{0,18},{1,21},{16,2},{17,5}} | collective-permute-start | bytes 110600 | tf_op jit(solution)/shard_map/ppermute | solution.py:41
  16.6 1.8 %collective-permute-done.2 = f32[1,72,128]{2,1,0:T(8,128)S(1)} collective-permute-done((f32[1,72,128]{2,1,0:T(8,128)S(1)}, f32[1,72,128]{2,1,0:T(8,128)S(1)}, u32[]{:S(2)}, u32[]{:S(2)}) %collective-permute-start.2) | collective-permute-done | bytes 36896 | tf_op jit(solution)/shard_map/ppermute | solution.py:41
  18.4 0.0 collective-permute-start.5
  18.4 0.0 collective-permute-done.4.refs_5_.refs_7_.refs_8_
  18.4 2.2 %collective-permute-start.6 = (f32[4,24,128]{2,1,0:T(8,128)S(1)}, f32[4,24,128]{2,1,0:T(8,128)S(1)}, u32[]{:S(2)}, u32[]{:S(2)}) collective-permute-start(f32[4,24,128]{2,1,0:T(8,128)S(1)} %get-tuple-element.30), channel_id=1, source_target_pairs={{0,2},{2,0},{1,3},{3,1},{4,6},{6,4},{5,7},{7,5},{8,10},{10,8},{9,1... | collective-permute-start | bytes 147464 | tf_op jit(solution)/shard_map/ppermute | solution.py:21
  20.6 1.9 %collective-permute-done.5.refs_6_.refs_8_.refs_9_ = f32[2,48,128]{2,1,0:T(8,128)S(1)} collective-permute-done((f32[2,48,128]{2,1,0:T(8,128)S(1)}, f32[2,48,128]{2,1,0:T(8,128)S(1)}, u32[]{:S(2)}, u32[]{:S(2)}) %collective-permute-start.5) | collective-permute-done | bytes 49184 | tf_op jit(solution)/shard_map/ppermute | solution.py:23
  22.5 0.7 %collective-permute-start.1 = (f32[1,72,128]{2,1,0:T(8,128)S(1)}, f32[1,72,128]{2,1,0:T(8,128)S(1)}, u32[]{:S(2)}, u32[]{:S(2)}) collective-permute-start(f32[1,72,128]{2,1,0:T(8,128)S(1)} %get-tuple-element.27), channel_id=1, source_target_pairs={{2,18},{3,19},{4,20},{5,21},{6,22},{7,23},{8,24},{9,25},{10,26},{1... | collective-permute-start | bytes 110600 | tf_op jit(solution)/shard_map/ppermute | solution.py:38
  23.1 0.0 collective-permute-done.6.refs_7_.refs_9_.refs_10_
  23.1 1.3 %collective-permute-start.3 = (f32[1,72,128]{2,1,0:T(8,128)S(1)}, f32[1,72,128]{2,1,0:T(8,128)S(1)}, u32[]{:S(2)}, u32[]{:S(2)}) collective-permute-start(f32[1,72,128]{2,1,0:T(8,128)S(1)} %collective-permute-done.2), channel_id=1, source_target_pairs={{18,16},{21,17},{2,0},{5,1}} | collective-permute-start | bytes 110600 | tf_op jit(solution)/shard_map/ppermute | solution.py:42
  24.4 0.0 collective-permute-done.8.refs_4_.refs_7_
  24.4 0.0 collective-permute-done.7.refs_8_.refs_10_.refs_11_
  24.4 0.0 copy-done.4
  24.5 0.9 %forward.1 = (f32[1,24,48,128]{3,2,1,0:T(8,128)S(1)}, f32[1,24,48,128]{3,2,1,0:T(8,128)S(1)}) custom-call(f32[8,1,24,48,128]{4,3,2,1,0:T(8,128)S(1)} %copy-done, f32[1,24,48,128]{3,2,1,0:T(8,128)S(1)} %get-tuple-element.24.refs_1_, s32[1,24,48,128]{3,2,1,0:T(8,128)S(1)} %copy-done.1, f32[1,24,48,128]{3,2,1,0:T(8,128)S(1)} %copy-done.4, ...), custom_call_target="tpu_custom_call" | custom-call | flops 4423680 | bytes 8994816 | tf_op jit(solution)/shard_map/forward/pallas_call | solution.py:66
  25.3 0.0 copy-start.2
  25.3 1.3 %collective-permute-start.9 = (f32[1,24,48,128]{3,2,1,0:T(8,128)S(1)}, f32[1,24,48,128]{3,2,1,0:T(8,128)S(1)}, u32[]{:S(2)}, u32[]{:S(2)}) collective-permute-start(f32[1,24,48,128]{3,2,1,0:T(8,128)S(1)} %get-tuple-element.32.refs_11_.refs_12_), channel_id=1, source_target_pairs={{0,16},{16,0},{1,17},{17,1},{2,18},{18,2},{3,19},{19,3},{4,20},{20... | collective-permute-start | bytes 1769480 | tf_op jit(solution)/shard_map/ppermute | solution.py:21
  26.6 0.0 collective-permute-done.1.refs_5_
  26.6 4.9 %collective-permute-done.3.refs_6_ = f32[1,72,128]{2,1,0:T(8,128)S(1)} collective-permute-done((f32[1,72,128]{2,1,0:T(8,128)S(1)}, f32[1,72,128]{2,1,0:T(8,128)S(1)}, u32[]{:S(2)}, u32[]{:S(2)}) %collective-permute-start.3) | collective-permute-done | bytes 36896 | tf_op jit(solution)/shard_map/ppermute | solution.py:42
  31.5 0.0 collective-permute-done.refs_4_
  31.5 0.0 copy-done.6
  31.5 1.7 %backward.1 = (f32[1,24,48,128]{3,2,1,0:T(8,128)S(1)}, f32[1,24,48,128]{3,2,1,0:T(8,128)S(1)}, f32[1,24,48,128]{3,2,1,0:T(8,128)S(1)}, f32[2,48,128]{2,1,0:T(8,1...) custom-call(f32[8,1,24,48,128]{4,3,2,1,0:T(8,128)S(1)} %copy-done, ...), custom_call_target="tpu_custom_call" | custom-call | flops 4423680 | bytes 10948608 | tf_op jit(solution)/shard_map/backward/pallas_call | solution.py:66
  33.2 0.1 collective-permute-start.13
  33.3 0.5 collective-permute-start.14
  33.8 2.8 %collective-permute-start.10 = (f32[2,48,128]{2,1,0:T(8,128)S(1)}, f32[2,48,128]{2,1,0:T(8,128)S(1)}, u32[]{:S(2)}, u32[]{:S(2)}) collective-permute-start(f32[2,48,128]{2,1,0:T(8,128)S(1)} %get-tuple-element.35), channel_id=1, source_target_pairs={{0,4},{4,8},{8,12},{12,0},{1,5},{5,9},{9,13},{13,1},{2,6},{6,10},{... | collective-permute-start | bytes 147464 | tf_op jit(solution)/shard_map/ppermute | solution.py:23
  36.6 1.6 %collective-permute-start.11 = (f32[2,48,128]{2,1,0:T(8,128)S(1)}, f32[2,48,128]{2,1,0:T(8,128)S(1)}, u32[]{:S(2)}, u32[]{:S(2)}) collective-permute-start(f32[2,48,128]{2,1,0:T(8,128)S(1)} %get-tuple-element.36), channel_id=1, source_target_pairs={{0,12},{4,0},{8,4},{12,8},{1,13},{5,1},{9,5},{13,9},{2,14},{6,2},{... | collective-permute-start | bytes 147464 | tf_op jit(solution)/shard_map/ppermute | solution.py:23
  38.2 2.2 %collective-permute-done.10.refs_14_ = f32[2,48,128]{2,1,0:T(8,128)S(1)} collective-permute-done((f32[2,48,128]{2,1,0:T(8,128)S(1)}, f32[2,48,128]{2,1,0:T(8,128)S(1)}, u32[]{:S(2)}, u32[]{:S(2)}) %collective-permute-start.10) | collective-permute-done | bytes 49184 | tf_op jit(solution)/shard_map/ppermute | solution.py:23
  40.4 1.1 %collective-permute-start.15 = (f32[1,4,48,128]{3,2,1,0:T(8,128)S(1)}, f32[1,4,48,128]{3,2,1,0:T(8,128)S(1)}, u32[]{:S(2)}, u32[]{:S(2)}) collective-permute-start(f32[1,4,48,128]{3,2,1,0:T(8,128)S(1)} %get-tuple-element.43), channel_id=1, source_target_pairs={{0,16},{16,0},{1,17},{17,1},{2,18},{18,2},{3,19},{19,3},{4,20},{20... | collective-permute-start | bytes 294920 | tf_op jit(solution)/shard_map/ppermute | solution.py:21
  41.5 0.0 collective-permute-done.11.refs_15_
  41.5 1.6 %collective-permute-start.12 = (f32[4,24,128]{2,1,0:T(8,128)S(1)}, f32[4,24,128]{2,1,0:T(8,128)S(1)}, u32[]{:S(2)}, u32[]{:S(2)}) collective-permute-start(f32[4,24,128]{2,1,0:T(8,128)S(1)} %get-tuple-element.37), channel_id=1, source_target_pairs={{0,2},{2,0},{1,3},{3,1},{4,6},{6,4},{5,7},{7,5},{8,10},{10,8},{9,1... | collective-permute-start | bytes 147464 | tf_op jit(solution)/shard_map/ppermute | solution.py:21
  43.1 2.5 %collective-permute-done.12.refs_16_ = f32[4,24,128]{2,1,0:T(8,128)S(1)} collective-permute-done((f32[4,24,128]{2,1,0:T(8,128)S(1)}, f32[4,24,128]{2,1,0:T(8,128)S(1)}, u32[]{:S(2)}, u32[]{:S(2)}) %collective-permute-start.12) | collective-permute-done | bytes 49184 | tf_op jit(solution)/shard_map/ppermute | solution.py:21
  45.6 0.0 collective-permute-done.9.refs_13_
  45.6 0.0 collective-permute-done.13.refs_17_
  45.6 0.0 copy-done.2
  45.6 5.4 %last.1 = (f32[1,24,48,128]{3,2,1,0:T(8,128)}, f32[8,1,24,48,128]{4,3,2,1,0:T(8,128)}, f32[1,24,48,128]{3,2,1,0:T(8,128)S(1)}) custom-call(f32[8,1,24,48,128]{4,3,2,1,0:T(8,128)S(1)} %copy-done, f32[1,24,48,128]{3,2,1,0:T(8,128)S(1)} %get-tuple-element.24.refs_1_, s32[1,24,48,128]{3,2,1,0:T(8,128)S(1)} %copy-done.2, ...), custom_call_target="tpu_custom_call" | custom-call | flops 17694720 | bytes 17989632 | tf_op jit(solution)/shard_map/last/pallas_call | solution.py:66
  51.0 2.1 %collective-permute-done.14.refs_1_ = f32[1,20,48,128]{3,2,1,0:T(8,128)S(1)} collective-permute-done((f32[1,20,48,128]{3,2,1,0:T(8,128)S(1)}, f32[1,20,48,128]{3,2,1,0:T(8,128)S(1)}, u32[]{:S(2)}, u32[]{:S(2)}) %collective-permute-start.14) | collective-permute-done | bytes 491552 | tf_op jit(solution)/shard_map/ppermute | solution.py:21
  53.1 0.8 %finish.1 = f32[1,24,48,128]{3,2,1,0:T(8,128)} custom-call(f32[1,24,48,128]{3,2,1,0:T(8,128)S(1)} %get-tuple-element.41.refs_0_, f32[1,20,48,128]{3,2,1,0:T(8,128)S(1)} %collective-permute-done.14.refs_1_), custom_call_target="tpu_custom_call" | custom-call | tf_op jit(solution)/shard_map/finish/pallas_call | solution.py:304
  53.9 0.4 collective-permute-done.15
  54.3 0.7 %add_dynamic-update-slice_fusion = f32[1,24,48,128]{3,2,1,0:T(8,128)} fusion(f32[1,24,48,128]{3,2,1,0:T(8,128)} %finish.1, f32[1,4,48,128]{3,2,1,0:T(8,128)S(1)} %collective-permute-done.15, f32[1,24,48,128]{3,2,1,0:T(8,128)S(1)} %get-tuple-element.41.refs_0_), kind=kLoop, calls=%fused_computation | loop fusion | flops 24576 | bytes 294912 | tf_op jit(solution)/shard_map/dynamic_update_slice | solution.py:367
Async XLA Ops:
  0.6 23.8 %collective-permute-start.8 = (f32[1,24,48,128]{3,2,1,0:T(8,128)}, f32[1,24,48,128]{3,2,1,0:T(8,128)S(1)}, u32[]{:S(2)}, u32[]{:S(2)}) collective-permute-start(f32[1,24,48,128]{3,2,1,0:T(8,128)} %refs_6_.1), channel_id=1, source_target_pairs={{0,16},{16,0},{1,17},{17,1},{2,18},{18,2},{3,19},{19,3},{4,20},{20... | collective-permute-start | bytes 1769480 | tf_op jit(solution)/shard_map/ppermute | solution.py:21
  3.7 2.3 %copy-start = (f32[8,1,24,48,128]{4,3,2,1,0:T(8,128)S(1)}, f32[8,1,24,48,128]{4,3,2,1,0:T(8,128)}, u32[]{:S(2)}) copy-start(f32[8,1,24,48,128]{4,3,2,1,0:T(8,128)} %refs_0_.7) | copy-start | bytes 14155780
  6.0 1.1 %copy-start.1 = (s32[1,24,48,128]{3,2,1,0:T(8,128)S(1)}, s32[1,24,48,128]{3,2,1,0:T(8,128)}, u32[]{:S(2)}) copy-start(s32[1,24,48,128]{3,2,1,0:T(8,128)} %refs_2_.7) | copy-start | bytes 1769476
  7.1 1.1 %copy-start.3 = (f32[1,24,48,128]{3,2,1,0:T(8,128)S(1)}, f32[1,24,48,128]{3,2,1,0:T(8,128)}, u32[]{:S(2)}) copy-start(f32[1,24,48,128]{3,2,1,0:T(8,128)} %refs_6_.1) | copy-start | bytes 1769476
  8.1 1.1 %copy-start.5 = (f32[1,24,48,128]{3,2,1,0:T(8,128)S(1)}, f32[1,24,48,128]{3,2,1,0:T(8,128)}, u32[]{:S(2)}) copy-start(f32[1,24,48,128]{3,2,1,0:T(8,128)} %refs_2_.6) | copy-start | bytes 1769476
  9.2 15.3 %copy-start.4 = (f32[1,24,48,128]{3,2,1,0:T(8,128)S(1)}, f32[1,24,48,128]{3,2,1,0:T(8,128)}, u32[]{:S(2)}) copy-start(f32[1,24,48,128]{3,2,1,0:T(8,128)} %refs_6_.1) | copy-start | bytes 1769476
  10.0 21.5 %copy-start.6 = (f32[1,24,48,128]{3,2,1,0:T(8,128)S(1)}, f32[1,24,48,128]{3,2,1,0:T(8,128)}, u32[]{:S(2)}) copy-start(f32[1,24,48,128]{3,2,1,0:T(8,128)} %refs_2_.6) | copy-start | bytes 1769476
  10.0 14.4 %collective-permute-start.7 = (f32[1,24,48,128]{3,2,1,0:T(8,128)S(1)}, f32[1,24,48,128]{3,2,1,0:T(8,128)S(1)}, u32[]{:S(2)}, u32[]{:S(2)}) collective-permute-start(f32[1,24,48,128]{3,2,1,0:T(8,128)S(1)} %get-tuple-element.31), channel_id=1, source_target_pairs={{0,1},{1,0},{2,3},{3,2},{4,5},{5,4},{6,7},{7,6},{8,9},{9,8},{10,11... | collective-permute-start | bytes 1769480 | tf_op jit(solution)/shard_map/ppermute | solution.py:21
  10.1 21.4 %collective-permute-start = (f32[1,1080,128]{2,1,0:T(8,128)S(1)}, f32[1,1080,128]{2,1,0:T(8,128)S(1)}, u32[]{:S(2)}, u32[]{:S(2)}) collective-permute-start(f32[1,1080,128]{2,1,0:T(8,128)S(1)} %get-tuple-element.26), channel_id=1, source_target_pairs={{0,16},{16,0},{1,17},{17,1},{2,18},{18,2},{3,19},{19,3},{4,20},{20... | collective-permute-start | bytes 1658888 | tf_op jit(solution)/shard_map/ppermute | solution.py:21
  10.2 8.2 %collective-permute-start.4 = (f32[2,48,128]{2,1,0:T(8,128)S(1)}, f32[2,48,128]{2,1,0:T(8,128)S(1)}, u32[]{:S(2)}, u32[]{:S(2)}) collective-permute-start(f32[2,48,128]{2,1,0:T(8,128)S(1)} %get-tuple-element.28), channel_id=1, source_target_pairs={{0,4},{4,8},{8,12},{12,0},{1,5},{5,9},{9,13},{13,1},{2,6},{6,10},{... | collective-permute-start | bytes 147464 | tf_op jit(solution)/shard_map/ppermute | solution.py:23
  12.2 6.1 %collective-permute-start.2 = (f32[1,72,128]{2,1,0:T(8,128)S(1)}, f32[1,72,128]{2,1,0:T(8,128)S(1)}, u32[]{:S(2)}, u32[]{:S(2)}) collective-permute-start(f32[1,72,128]{2,1,0:T(8,128)S(1)} %get-tuple-element.27), channel_id=1, source_target_pairs={{0,18},{1,21},{16,2},{17,5}} | collective-permute-start | bytes 110600 | tf_op jit(solution)/shard_map/ppermute | solution.py:41
  18.4 4.1 %collective-permute-start.5 = (f32[2,48,128]{2,1,0:T(8,128)S(1)}, f32[2,48,128]{2,1,0:T(8,128)S(1)}, u32[]{:S(2)}, u32[]{:S(2)}) collective-permute-start(f32[2,48,128]{2,1,0:T(8,128)S(1)} %get-tuple-element.29), channel_id=1, source_target_pairs={{0,12},{4,0},{8,4},{12,8},{1,13},{5,1},{9,5},{13,9},{2,14},{6,2},{... | collective-permute-start | bytes 147464 | tf_op jit(solution)/shard_map/ppermute | solution.py:23
  18.4 4.7 %collective-permute-start.6 = (f32[4,24,128]{2,1,0:T(8,128)S(1)}, f32[4,24,128]{2,1,0:T(8,128)S(1)}, u32[]{:S(2)}, u32[]{:S(2)}) collective-permute-start(f32[4,24,128]{2,1,0:T(8,128)S(1)} %get-tuple-element.30), channel_id=1, source_target_pairs={{0,2},{2,0},{1,3},{3,1},{4,6},{6,4},{5,7},{7,5},{8,10},{10,8},{9,1... | collective-permute-start | bytes 147464 | tf_op jit(solution)/shard_map/ppermute | solution.py:21
  22.5 4.2 %collective-permute-start.1 = (f32[1,72,128]{2,1,0:T(8,128)S(1)}, f32[1,72,128]{2,1,0:T(8,128)S(1)}, u32[]{:S(2)}, u32[]{:S(2)}) collective-permute-start(f32[1,72,128]{2,1,0:T(8,128)S(1)} %get-tuple-element.27), channel_id=1, source_target_pairs={{2,18},{3,19},{4,20},{5,21},{6,22},{7,23},{8,24},{9,25},{10,26},{1... | collective-permute-start | bytes 110600 | tf_op jit(solution)/shard_map/ppermute | solution.py:38
  23.1 8.4 %collective-permute-start.3 = (f32[1,72,128]{2,1,0:T(8,128)S(1)}, f32[1,72,128]{2,1,0:T(8,128)S(1)}, u32[]{:S(2)}, u32[]{:S(2)}) collective-permute-start(f32[1,72,128]{2,1,0:T(8,128)S(1)} %collective-permute-done.2), channel_id=1, source_target_pairs={{18,16},{21,17},{2,0},{5,1}} | collective-permute-start | bytes 110600 | tf_op jit(solution)/shard_map/ppermute | solution.py:42
  25.3 20.3 %copy-start.2 = (s32[1,24,48,128]{3,2,1,0:T(8,128)S(1)}, s32[1,24,48,128]{3,2,1,0:T(8,128)}, u32[]{:S(2)}) copy-start(s32[1,24,48,128]{3,2,1,0:T(8,128)} %refs_2_.7) | copy-start | bytes 1769476
  25.3 20.3 %collective-permute-start.9 = (f32[1,24,48,128]{3,2,1,0:T(8,128)S(1)}, f32[1,24,48,128]{3,2,1,0:T(8,128)S(1)}, u32[]{:S(2)}, u32[]{:S(2)}) collective-permute-start(f32[1,24,48,128]{3,2,1,0:T(8,128)S(1)} %get-tuple-element.32.refs_11_.refs_12_), channel_id=1, source_target_pairs={{0,16},{16,0},{1,17},{17,1},{2,18},{18,2},{3,19},{19,3},{4,20},{20... | collective-permute-start | bytes 1769480 | tf_op jit(solution)/shard_map/ppermute | solution.py:21
  33.2 12.4 %collective-permute-start.13 = (f32[1,24,48,128]{3,2,1,0:T(8,128)S(1)}, f32[1,24,48,128]{3,2,1,0:T(8,128)S(1)}, u32[]{:S(2)}, u32[]{:S(2)}) collective-permute-start(f32[1,24,48,128]{3,2,1,0:T(8,128)S(1)} %get-tuple-element.38), channel_id=1, source_target_pairs={{0,1},{1,0},{2,3},{3,2},{4,5},{5,4},{6,7},{7,6},{8,9},{9,8},{10,11... | collective-permute-start | bytes 1769480 | tf_op jit(solution)/shard_map/ppermute | solution.py:21
  33.3 19.7 %collective-permute-start.14 = (f32[1,20,48,128]{3,2,1,0:T(8,128)S(1)}, f32[1,20,48,128]{3,2,1,0:T(8,128)S(1)}, u32[]{:S(2)}, u32[]{:S(2)}) collective-permute-start(f32[1,20,48,128]{3,2,1,0:T(8,128)S(1)} %get-tuple-element.42), channel_id=1, source_target_pairs={{0,16},{16,0},{1,17},{17,1},{2,18},{18,2},{3,19},{19,3},{4,20},{20... | collective-permute-start | bytes 1474568 | tf_op jit(solution)/shard_map/ppermute | solution.py:21
  33.8 6.6 %collective-permute-start.10 = (f32[2,48,128]{2,1,0:T(8,128)S(1)}, f32[2,48,128]{2,1,0:T(8,128)S(1)}, u32[]{:S(2)}, u32[]{:S(2)}) collective-permute-start(f32[2,48,128]{2,1,0:T(8,128)S(1)} %get-tuple-element.35), channel_id=1, source_target_pairs={{0,4},{4,8},{8,12},{12,0},{1,5},{5,9},{9,13},{13,1},{2,6},{6,10},{... | collective-permute-start | bytes 147464 | tf_op jit(solution)/shard_map/ppermute | solution.py:23
  36.6 4.9 %collective-permute-start.11 = (f32[2,48,128]{2,1,0:T(8,128)S(1)}, f32[2,48,128]{2,1,0:T(8,128)S(1)}, u32[]{:S(2)}, u32[]{:S(2)}) collective-permute-start(f32[2,48,128]{2,1,0:T(8,128)S(1)} %get-tuple-element.36), channel_id=1, source_target_pairs={{0,12},{4,0},{8,4},{12,8},{1,13},{5,1},{9,5},{13,9},{2,14},{6,2},{... | collective-permute-start | bytes 147464 | tf_op jit(solution)/shard_map/ppermute | solution.py:23
  40.4 14.0 %collective-permute-start.15 = (f32[1,4,48,128]{3,2,1,0:T(8,128)S(1)}, f32[1,4,48,128]{3,2,1,0:T(8,128)S(1)}, u32[]{:S(2)}, u32[]{:S(2)}) collective-permute-start(f32[1,4,48,128]{3,2,1,0:T(8,128)S(1)} %get-tuple-element.43), channel_id=1, source_target_pairs={{0,16},{16,0},{1,17},{17,1},{2,18},{18,2},{3,19},{19,3},{4,20},{20... | collective-permute-start | bytes 294920 | tf_op jit(solution)/shard_map/ppermute | solution.py:21
  41.5 4.1 %collective-permute-start.12 = (f32[4,24,128]{2,1,0:T(8,128)S(1)}, f32[4,24,128]{2,1,0:T(8,128)S(1)}, u32[]{:S(2)}, u32[]{:S(2)}) collective-permute-start(f32[4,24,128]{2,1,0:T(8,128)S(1)} %get-tuple-element.37), channel_id=1, source_target_pairs={{0,2},{2,0},{1,3},{3,1},{4,6},{6,4},{5,7},{7,5},{8,10},{10,8},{9,1... | collective-permute-start | bytes 147464 | tf_op jit(solution)/shard_map/ppermute | solution.py:21

commit v9 on v7

--- a/solution.py
+++ b/solution.py
@@ -318,7 +318,7 @@
     cells = b * c * d
     pair = lax.axis_size("grp") == 2
     blocks = [block] * (1 if pair else 2)
-    tail = max(1, b // 6)
+    tail = max(2, b // 4)
     faces = [(2, c, d), (2, c, d), (4, b, d)]
 
     start_before, start_after = both_ways(start, start, "grp")

time: 55.4 us -> 55.4 us (level)
    ppermute x9, waiting for transfers between devices: 5.32 us -> 2.14 us  [both_ways(): other = lax.ppermute(up, axis, ring(axis, 1))]
    ppermute x2, waiting for transfers between devices: 1.86 us -> 3.93 us  [both_ways(): lax.ppermute(down, axis, ring(axis, -1))]
    ppermute x2, waiting for transfers between devices: 2.19 us -> 3.24 us  [both_ways(): lax.ppermute(up, axis, ring(axis, 1))]
where the time goes in v9:
time: 55.4 us; the launch traced here: 55.1 us
  starting transfers between devices  23 us (42%)
  waiting for transfers between devices  15.9 us (29%)
  Pallas kernels  9.21 us (17%)
  local copies, waits for them, and re-layouts  5.54 us (10%)
  between operations  0.76 us (1%)
  other arithmetic  0.68 us (1%)
    ppermute x9, starting transfers between devices, both_ways(): other = lax.ppermute(up, axis, ring(axis, 1))  10 us
    pallas_call x4, Pallas kernels, call(): pl.pallas_call(kernel, out_shape=[jax.ShapeDtypeStruct(s, jnp.float32) fo...  8.4 us
    unnamed x14, local copies, waits for them, and re-layouts  5.54 us
    ppermute x1, waiting for transfers between devices, part_swap(): lax.ppermute(part, axes, [(middle(g, w), at(1 - g, 0, 0, w)) for g, w in...  4.84 us
    ppermute x2, starting transfers between devices, both_ways(): lax.ppermute(up, axis, ring(axis, 1))  4.72 us
    ppermute x1, starting transfers between devices, part_swap(): lax.ppermute(part, axes, [(at(g, 0, 0, w), middle(g, w)) for g, w in ends])  4.34 us
    ppermute x2, waiting for transfers between devices, both_ways(): lax.ppermute(down, axis, ring(axis, -1))  3.93 us
    ppermute x2, waiting for transfers between devices, both_ways(): lax.ppermute(up, axis, ring(axis, 1))  3.24 us
  transfers between devices with their start and end apart: 16, of which 7 were waited for; matrix products, arithmetic and copies ran while one was open for 0% of the time, Pallas kernels for 17%

profile of v9, /device:TPU:0, one launch (start us, length us, event | category | flops | bytes accessed | tf_op | source)
XLA Modules:
  0.0 55.1 jit_solution(3946638059827208777)
XLA Ops:
  0.6 3.0 %collective-permute-start.8 = (f32[1,24,48,128]{3,2,1,0:T(8,128)}, f32[1,24,48,128]{3,2,1,0:T(8,128)S(1)}, u32[]{:S(2)}, u32[]{:S(2)}) collective-permute-start(f32[1,24,48,128]{3,2,1,0:T(8,128)} %refs_6_.1), channel_id=1, source_target_pairs={{0,16},{16,0},{1,17},{17,1},{2,18},{18,2},{3,19},{19,3},{4,20},{20... | collective-permute-start | bytes 1769480 | tf_op jit(solution)/shard_map/ppermute | solution.py:21
  3.7 0.0 copy-start
  3.7 2.3 %copy-done = f32[8,1,24,48,128]{4,3,2,1,0:T(8,128)S(1)} copy-done((f32[8,1,24,48,128]{4,3,2,1,0:T(8,128)S(1)}, f32[8,1,24,48,128]{4,3,2,1,0:T(8,128)}, u32[]{:S(2)}) %copy-start) | copy-done | bytes 4718616
  6.0 0.0 copy-start.1
  6.0 1.1 %copy-done.1 = s32[1,24,48,128]{3,2,1,0:T(8,128)S(1)} copy-done((s32[1,24,48,128]{3,2,1,0:T(8,128)S(1)}, s32[1,24,48,128]{3,2,1,0:T(8,128)}, u32[]{:S(2)}) %copy-start.1) | copy-done | bytes 589848
  7.1 0.0 copy-start.3
  7.1 1.1 %copy-done.3 = f32[1,24,48,128]{3,2,1,0:T(8,128)S(1)} copy-done((f32[1,24,48,128]{3,2,1,0:T(8,128)S(1)}, f32[1,24,48,128]{3,2,1,0:T(8,128)}, u32[]{:S(2)}) %copy-start.3) | copy-done | bytes 589848
  8.1 0.0 copy-start.5
  8.1 1.1 %copy-done.5 = f32[1,24,48,128]{3,2,1,0:T(8,128)S(1)} copy-done((f32[1,24,48,128]{3,2,1,0:T(8,128)S(1)}, f32[1,24,48,128]{3,2,1,0:T(8,128)}, u32[]{:S(2)}) %copy-start.5) | copy-done | bytes 589848
  9.2 0.0 copy-start.4
  9.2 0.8 %prepare.1 = (f32[1,24,48,128]{3,2,1,0:T(8,128)S(1)}, f32[1,24,48,128]{3,2,1,0:T(8,128)S(1)}, f32[1,24,48,128]{3,2,1,0:T(8,128)S(1)}, f32[2,48,128]{2,1,0:T(8,12...) custom-call(f32[8,1,24,48,128]{4,3,2,1,0:T(8,128)S(1)} %copy-done, ...), custom_call_target="tpu_custom_call" | custom-call | flops 2949120 | bytes 8994816 | tf_op jit(solution)/shard_map/prepare/pallas_call | solution.py:66
  10.0 0.0 copy-start.6
  10.0 0.1 collective-permute-start.7
  10.1 0.1 collective-permute-start
  10.2 2.1 %collective-permute-start.4 = (f32[2,48,128]{2,1,0:T(8,128)S(1)}, f32[2,48,128]{2,1,0:T(8,128)S(1)}, u32[]{:S(2)}, u32[]{:S(2)}) collective-permute-start(f32[2,48,128]{2,1,0:T(8,128)S(1)} %get-tuple-element.28), channel_id=1, source_target_pairs={{0,4},{4,8},{8,12},{12,0},{1,5},{5,9},{9,13},{13,1},{2,6},{6,10},{... | collective-permute-start | bytes 147464 | tf_op jit(solution)/shard_map/ppermute | solution.py:23
  12.2 4.3 %collective-permute-start.2 = (f32[1,64,128]{2,1,0:T(8,128)S(1)}, f32[1,64,128]{2,1,0:T(8,128)S(1)}, u32[]{:S(2)}, u32[]{:S(2)}) collective-permute-start(f32[1,64,128]{2,1,0:T(8,128)S(1)} %get-tuple-element.27), channel_id=1, source_target_pairs={{0,18},{1,21},{16,2},{17,5}} | collective-permute-start | bytes 98312 | tf_op jit(solution)/shard_map/ppermute | solution.py:41
  16.6 1.7 %collective-permute-done.2 = f32[1,64,128]{2,1,0:T(8,128)S(1)} collective-permute-done((f32[1,64,128]{2,1,0:T(8,128)S(1)}, f32[1,64,128]{2,1,0:T(8,128)S(1)}, u32[]{:S(2)}, u32[]{:S(2)}) %collective-permute-start.2) | collective-permute-done | bytes 32800 | tf_op jit(solution)/shard_map/ppermute | solution.py:41
  18.3 0.0 collective-permute-start.5
  18.3 0.0 collective-permute-done.4.refs_5_.refs_7_.refs_8_
  18.3 2.2 %collective-permute-start.6 = (f32[4,24,128]{2,1,0:T(8,128)S(1)}, f32[4,24,128]{2,1,0:T(8,128)S(1)}, u32[]{:S(2)}, u32[]{:S(2)}) collective-permute-start(f32[4,24,128]{2,1,0:T(8,128)S(1)} %get-tuple-element.30), channel_id=1, source_target_pairs={{0,2},{2,0},{1,3},{3,1},{4,6},{6,4},{5,7},{7,5},{8,10},{10,8},{9,1... | collective-permute-start | bytes 147464 | tf_op jit(solution)/shard_map/ppermute | solution.py:21
  20.5 1.9 %collective-permute-done.5.refs_6_.refs_8_.refs_9_ = f32[2,48,128]{2,1,0:T(8,128)S(1)} collective-permute-done((f32[2,48,128]{2,1,0:T(8,128)S(1)}, f32[2,48,128]{2,1,0:T(8,128)S(1)}, u32[]{:S(2)}, u32[]{:S(2)}) %collective-permute-start.5) | collective-permute-done | bytes 49184 | tf_op jit(solution)/shard_map/ppermute | solution.py:23
  22.4 0.7 %collective-permute-start.1 = (f32[1,64,128]{2,1,0:T(8,128)S(1)}, f32[1,64,128]{2,1,0:T(8,128)S(1)}, u32[]{:S(2)}, u32[]{:S(2)}) collective-permute-start(f32[1,64,128]{2,1,0:T(8,128)S(1)} %get-tuple-element.27), channel_id=1, source_target_pairs={{2,18},{3,19},{4,20},{5,21},{6,22},{7,23},{8,24},{9,25},{10,26},{1... | collective-permute-start | bytes 98312 | tf_op jit(solution)/shard_map/ppermute | solution.py:38
  23.1 0.0 collective-permute-done.6.refs_7_.refs_9_.refs_10_
  23.1 1.3 %collective-permute-start.3 = (f32[1,64,128]{2,1,0:T(8,128)S(1)}, f32[1,64,128]{2,1,0:T(8,128)S(1)}, u32[]{:S(2)}, u32[]{:S(2)}) collective-permute-start(f32[1,64,128]{2,1,0:T(8,128)S(1)} %collective-permute-done.2), channel_id=1, source_target_pairs={{18,16},{21,17},{2,0},{5,1}} | collective-permute-start | bytes 98312 | tf_op jit(solution)/shard_map/ppermute | solution.py:42
  24.4 0.0 collective-permute-done.8.refs_4_.refs_7_
  24.4 0.0 collective-permute-done.7.refs_8_.refs_10_.refs_11_
  24.4 0.0 copy-done.4
  24.4 0.9 %forward.1 = (f32[1,24,48,128]{3,2,1,0:T(8,128)S(1)}, f32[1,24,48,128]{3,2,1,0:T(8,128)S(1)}) custom-call(f32[8,1,24,48,128]{4,3,2,1,0:T(8,128)S(1)} %copy-done, f32[1,24,48,128]{3,2,1,0:T(8,128)S(1)} %get-tuple-element.24.refs_1_, s32[1,24,48,128]{3,2,1,0:T(8,128)S(1)} %copy-done.1, f32[1,24,48,128]{3,2,1,0:T(8,128)S(1)} %copy-done.4, ...), custom_call_target="tpu_custom_call" | custom-call | flops 4423680 | bytes 8994816 | tf_op jit(solution)/shard_map/forward/pallas_call | solution.py:66
  25.3 0.0 copy-start.2
  25.3 1.3 %collective-permute-start.9 = (f32[1,24,48,128]{3,2,1,0:T(8,128)S(1)}, f32[1,24,48,128]{3,2,1,0:T(8,128)S(1)}, u32[]{:S(2)}, u32[]{:S(2)}) collective-permute-start(f32[1,24,48,128]{3,2,1,0:T(8,128)S(1)} %get-tuple-element.32.refs_11_.refs_12_), channel_id=1, source_target_pairs={{0,16},{16,0},{1,17},{17,1},{2,18},{18,2},{3,19},{19,3},{4,20},{20... | collective-permute-start | bytes 1769480 | tf_op jit(solution)/shard_map/ppermute | solution.py:21
  26.6 0.0 collective-permute-done.1.refs_5_
  26.6 4.8 %collective-permute-done.3.refs_6_ = f32[1,64,128]{2,1,0:T(8,128)S(1)} collective-permute-done((f32[1,64,128]{2,1,0:T(8,128)S(1)}, f32[1,64,128]{2,1,0:T(8,128)S(1)}, u32[]{:S(2)}, u32[]{:S(2)}) %collective-permute-start.3) | collective-permute-done | bytes 32800 | tf_op jit(solution)/shard_map/ppermute | solution.py:42
  31.4 0.0 collective-permute-done.refs_4_
  31.4 0.0 copy-done.6
  31.4 1.5 %backward.1 = (f32[1,24,48,128]{3,2,1,0:T(8,128)S(1)}, f32[1,24,48,128]{3,2,1,0:T(8,128)S(1)}, f32[1,24,48,128]{3,2,1,0:T(8,128)S(1)}, f32[2,48,128]{2,1,0:T(8,1...) custom-call(f32[8,1,24,48,128]{4,3,2,1,0:T(8,128)S(1)} %copy-done, ...), custom_call_target="tpu_custom_call" | custom-call | flops 4423680 | bytes 10944512 | tf_op jit(solution)/shard_map/backward/pallas_call | solution.py:66
  32.9 0.1 collective-permute-start.13
  33.0 0.6 %collective-permute-start.14 = (f32[1,18,48,128]{3,2,1,0:T(8,128)S(1)}, f32[1,18,48,128]{3,2,1,0:T(8,128)S(1)}, u32[]{:S(2)}, u32[]{:S(2)}) collective-permute-start(f32[1,18,48,128]{3,2,1,0:T(8,128)S(1)} %get-tuple-element.42), channel_id=1, source_target_pairs={{0,16},{16,0},{1,17},{17,1},{2,18},{18,2},{3,19},{19,3},{4,20},{20... | collective-permute-start | bytes 1327112 | tf_op jit(solution)/shard_map/ppermute | solution.py:21
  33.7 2.6 %collective-permute-start.10 = (f32[2,48,128]{2,1,0:T(8,128)S(1)}, f32[2,48,128]{2,1,0:T(8,128)S(1)}, u32[]{:S(2)}, u32[]{:S(2)}) collective-permute-start(f32[2,48,128]{2,1,0:T(8,128)S(1)} %get-tuple-element.35), channel_id=1, source_target_pairs={{0,4},{4,8},{8,12},{12,0},{1,5},{5,9},{9,13},{13,1},{2,6},{6,10},{... | collective-permute-start | bytes 147464 | tf_op jit(solution)/shard_map/ppermute | solution.py:23
  36.3 0.5 collective-permute-start.15
  36.8 3.2 %collective-permute-done.10.refs_14_ = f32[2,48,128]{2,1,0:T(8,128)S(1)} collective-permute-done((f32[2,48,128]{2,1,0:T(8,128)S(1)}, f32[2,48,128]{2,1,0:T(8,128)S(1)}, u32[]{:S(2)}, u32[]{:S(2)}) %collective-permute-start.10) | collective-permute-done | bytes 49184 | tf_op jit(solution)/shard_map/ppermute | solution.py:23
  40.0 2.0 %collective-permute-start.11 = (f32[2,48,128]{2,1,0:T(8,128)S(1)}, f32[2,48,128]{2,1,0:T(8,128)S(1)}, u32[]{:S(2)}, u32[]{:S(2)}) collective-permute-start(f32[2,48,128]{2,1,0:T(8,128)S(1)} %get-tuple-element.36), channel_id=1, source_target_pairs={{0,12},{4,0},{8,4},{12,8},{1,13},{5,1},{9,5},{13,9},{2,14},{6,2},{... | collective-permute-start | bytes 147464 | tf_op jit(solution)/shard_map/ppermute | solution.py:23
  42.1 2.1 %collective-permute-done.11.refs_15_ = f32[2,48,128]{2,1,0:T(8,128)S(1)} collective-permute-done((f32[2,48,128]{2,1,0:T(8,128)S(1)}, f32[2,48,128]{2,1,0:T(8,128)S(1)}, u32[]{:S(2)}, u32[]{:S(2)}) %collective-permute-start.11) | collective-permute-done | bytes 49184 | tf_op jit(solution)/shard_map/ppermute | solution.py:23
  44.1 2.1 %collective-permute-start.12 = (f32[4,24,128]{2,1,0:T(8,128)S(1)}, f32[4,24,128]{2,1,0:T(8,128)S(1)}, u32[]{:S(2)}, u32[]{:S(2)}) collective-permute-start(f32[4,24,128]{2,1,0:T(8,128)S(1)} %get-tuple-element.37), channel_id=1, source_target_pairs={{0,2},{2,0},{1,3},{3,1},{4,6},{6,4},{5,7},{7,5},{8,10},{10,8},{9,1... | collective-permute-start | bytes 147464 | tf_op jit(solution)/shard_map/ppermute | solution.py:21
  46.2 2.1 %collective-permute-done.12.refs_16_ = f32[4,24,128]{2,1,0:T(8,128)S(1)} collective-permute-done((f32[4,24,128]{2,1,0:T(8,128)S(1)}, f32[4,24,128]{2,1,0:T(8,128)S(1)}, u32[]{:S(2)}, u32[]{:S(2)}) %collective-permute-start.12) | collective-permute-done | bytes 49184 | tf_op jit(solution)/shard_map/ppermute | solution.py:21
  48.3 0.0 collective-permute-done.9.refs_13_
  48.3 0.0 collective-permute-done.13.refs_17_
  48.3 0.0 copy-done.2
  48.3 5.3 %last.1 = (f32[1,24,48,128]{3,2,1,0:T(8,128)}, f32[8,1,24,48,128]{4,3,2,1,0:T(8,128)}, f32[1,24,48,128]{3,2,1,0:T(8,128)S(1)}) custom-call(f32[8,1,24,48,128]{4,3,2,1,0:T(8,128)S(1)} %copy-done, f32[1,24,48,128]{3,2,1,0:T(8,128)S(1)} %get-tuple-element.24.refs_1_, s32[1,24,48,128]{3,2,1,0:T(8,128)S(1)} %copy-done.2, ...), custom_call_target="tpu_custom_call" | custom-call | flops 17694720 | bytes 17989632 | tf_op jit(solution)/shard_map/last/pallas_call | solution.py:66
  53.5 0.0 collective-permute-done.14.refs_1_
  53.5 0.8 %finish.1 = f32[1,24,48,128]{3,2,1,0:T(8,128)} custom-call(f32[1,24,48,128]{3,2,1,0:T(8,128)S(1)} %get-tuple-element.41.refs_0_, f32[1,18,48,128]{3,2,1,0:T(8,128)S(1)} %collective-permute-done.14.refs_1_), custom_call_target="tpu_custom_call" | custom-call | tf_op jit(solution)/shard_map/finish/pallas_call | solution.py:304
  54.4 0.1 collective-permute-done.15
  54.4 0.7 %add_dynamic-update-slice_fusion = f32[1,24,48,128]{3,2,1,0:T(8,128)} fusion(f32[1,24,48,128]{3,2,1,0:T(8,128)} %finish.1, f32[1,6,48,128]{3,2,1,0:T(8,128)S(1)} %collective-permute-done.15, f32[1,24,48,128]{3,2,1,0:T(8,128)S(1)} %get-tuple-element.41.refs_0_), kind=kLoop, calls=%fused_computation | loop fusion | flops 36864 | bytes 442368 | tf_op jit(solution)/shard_map/dynamic_update_slice | solution.py:367
Async XLA Ops:
  0.6 23.7 %collective-permute-start.8 = (f32[1,24,48,128]{3,2,1,0:T(8,128)}, f32[1,24,48,128]{3,2,1,0:T(8,128)S(1)}, u32[]{:S(2)}, u32[]{:S(2)}) collective-permute-start(f32[1,24,48,128]{3,2,1,0:T(8,128)} %refs_6_.1), channel_id=1, source_target_pairs={{0,16},{16,0},{1,17},{17,1},{2,18},{18,2},{3,19},{19,3},{4,20},{20... | collective-permute-start | bytes 1769480 | tf_op jit(solution)/shard_map/ppermute | solution.py:21
  3.7 2.3 %copy-start = (f32[8,1,24,48,128]{4,3,2,1,0:T(8,128)S(1)}, f32[8,1,24,48,128]{4,3,2,1,0:T(8,128)}, u32[]{:S(2)}) copy-start(f32[8,1,24,48,128]{4,3,2,1,0:T(8,128)} %refs_0_.7) | copy-start | bytes 14155780
  6.0 1.1 %copy-start.1 = (s32[1,24,48,128]{3,2,1,0:T(8,128)S(1)}, s32[1,24,48,128]{3,2,1,0:T(8,128)}, u32[]{:S(2)}) copy-start(s32[1,24,48,128]{3,2,1,0:T(8,128)} %refs_2_.7) | copy-start | bytes 1769476
  7.1 1.1 %copy-start.3 = (f32[1,24,48,128]{3,2,1,0:T(8,128)S(1)}, f32[1,24,48,128]{3,2,1,0:T(8,128)}, u32[]{:S(2)}) copy-start(f32[1,24,48,128]{3,2,1,0:T(8,128)} %refs_6_.1) | copy-start | bytes 1769476
  8.1 1.1 %copy-start.5 = (f32[1,24,48,128]{3,2,1,0:T(8,128)S(1)}, f32[1,24,48,128]{3,2,1,0:T(8,128)}, u32[]{:S(2)}) copy-start(f32[1,24,48,128]{3,2,1,0:T(8,128)} %refs_2_.6) | copy-start | bytes 1769476
  9.2 15.2 %copy-start.4 = (f32[1,24,48,128]{3,2,1,0:T(8,128)S(1)}, f32[1,24,48,128]{3,2,1,0:T(8,128)}, u32[]{:S(2)}) copy-start(f32[1,24,48,128]{3,2,1,0:T(8,128)} %refs_6_.1) | copy-start | bytes 1769476
  10.0 21.4 %copy-start.6 = (f32[1,24,48,128]{3,2,1,0:T(8,128)S(1)}, f32[1,24,48,128]{3,2,1,0:T(8,128)}, u32[]{:S(2)}) copy-start(f32[1,24,48,128]{3,2,1,0:T(8,128)} %refs_2_.6) | copy-start | bytes 1769476
  10.0 14.4 %collective-permute-start.7 = (f32[1,24,48,128]{3,2,1,0:T(8,128)S(1)}, f32[1,24,48,128]{3,2,1,0:T(8,128)S(1)}, u32[]{:S(2)}, u32[]{:S(2)}) collective-permute-start(f32[1,24,48,128]{3,2,1,0:T(8,128)S(1)} %get-tuple-element.31), channel_id=1, source_target_pairs={{0,1},{1,0},{2,3},{3,2},{4,5},{5,4},{6,7},{7,6},{8,9},{9,8},{10,11... | collective-permute-start | bytes 1769480 | tf_op jit(solution)/shard_map/ppermute | solution.py:21
  10.1 21.4 %collective-permute-start = (f32[1,1088,128]{2,1,0:T(8,128)S(1)}, f32[1,1088,128]{2,1,0:T(8,128)S(1)}, u32[]{:S(2)}, u32[]{:S(2)}) collective-permute-start(f32[1,1088,128]{2,1,0:T(8,128)S(1)} %get-tuple-element.26), channel_id=1, source_target_pairs={{0,16},{16,0},{1,17},{17,1},{2,18},{18,2},{3,19},{19,3},{4,20},{20... | collective-permute-start | bytes 1671176 | tf_op jit(solution)/shard_map/ppermute | solution.py:21
  10.2 8.2 %collective-permute-start.4 = (f32[2,48,128]{2,1,0:T(8,128)S(1)}, f32[2,48,128]{2,1,0:T(8,128)S(1)}, u32[]{:S(2)}, u32[]{:S(2)}) collective-permute-start(f32[2,48,128]{2,1,0:T(8,128)S(1)} %get-tuple-element.28), channel_id=1, source_target_pairs={{0,4},{4,8},{8,12},{12,0},{1,5},{5,9},{9,13},{13,1},{2,6},{6,10},{... | collective-permute-start | bytes 147464 | tf_op jit(solution)/shard_map/ppermute | solution.py:23
  12.2 6.1 %collective-permute-start.2 = (f32[1,64,128]{2,1,0:T(8,128)S(1)}, f32[1,64,128]{2,1,0:T(8,128)S(1)}, u32[]{:S(2)}, u32[]{:S(2)}) collective-permute-start(f32[1,64,128]{2,1,0:T(8,128)S(1)} %get-tuple-element.27), channel_id=1, source_target_pairs={{0,18},{1,21},{16,2},{17,5}} | collective-permute-start | bytes 98312 | tf_op jit(solution)/shard_map/ppermute | solution.py:41
  18.3 4.1 %collective-permute-start.5 = (f32[2,48,128]{2,1,0:T(8,128)S(1)}, f32[2,48,128]{2,1,0:T(8,128)S(1)}, u32[]{:S(2)}, u32[]{:S(2)}) collective-permute-start(f32[2,48,128]{2,1,0:T(8,128)S(1)} %get-tuple-element.29), channel_id=1, source_target_pairs={{0,12},{4,0},{8,4},{12,8},{1,13},{5,1},{9,5},{13,9},{2,14},{6,2},{... | collective-permute-start | bytes 147464 | tf_op jit(solution)/shard_map/ppermute | solution.py:23
  18.3 4.7 %collective-permute-start.6 = (f32[4,24,128]{2,1,0:T(8,128)S(1)}, f32[4,24,128]{2,1,0:T(8,128)S(1)}, u32[]{:S(2)}, u32[]{:S(2)}) collective-permute-start(f32[4,24,128]{2,1,0:T(8,128)S(1)} %get-tuple-element.30), channel_id=1, source_target_pairs={{0,2},{2,0},{1,3},{3,1},{4,6},{6,4},{5,7},{7,5},{8,10},{10,8},{9,1... | collective-permute-start | bytes 147464 | tf_op jit(solution)/shard_map/ppermute | solution.py:21
  22.4 4.2 %collective-permute-start.1 = (f32[1,64,128]{2,1,0:T(8,128)S(1)}, f32[1,64,128]{2,1,0:T(8,128)S(1)}, u32[]{:S(2)}, u32[]{:S(2)}) collective-permute-start(f32[1,64,128]{2,1,0:T(8,128)S(1)} %get-tuple-element.27), channel_id=1, source_target_pairs={{2,18},{3,19},{4,20},{5,21},{6,22},{7,23},{8,24},{9,25},{10,26},{1... | collective-permute-start | bytes 98312 | tf_op jit(solution)/shard_map/ppermute | solution.py:38
  23.1 8.4 %collective-permute-start.3 = (f32[1,64,128]{2,1,0:T(8,128)S(1)}, f32[1,64,128]{2,1,0:T(8,128)S(1)}, u32[]{:S(2)}, u32[]{:S(2)}) collective-permute-start(f32[1,64,128]{2,1,0:T(8,128)S(1)} %collective-permute-done.2), channel_id=1, source_target_pairs={{18,16},{21,17},{2,0},{5,1}} | collective-permute-start | bytes 98312 | tf_op jit(solution)/shard_map/ppermute | solution.py:42
  25.3 23.0 %copy-start.2 = (s32[1,24,48,128]{3,2,1,0:T(8,128)S(1)}, s32[1,24,48,128]{3,2,1,0:T(8,128)}, u32[]{:S(2)}) copy-start(s32[1,24,48,128]{3,2,1,0:T(8,128)} %refs_2_.7) | copy-start | bytes 1769476
  25.3 23.0 %collective-permute-start.9 = (f32[1,24,48,128]{3,2,1,0:T(8,128)S(1)}, f32[1,24,48,128]{3,2,1,0:T(8,128)S(1)}, u32[]{:S(2)}, u32[]{:S(2)}) collective-permute-start(f32[1,24,48,128]{3,2,1,0:T(8,128)S(1)} %get-tuple-element.32.refs_11_.refs_12_), channel_id=1, source_target_pairs={{0,16},{16,0},{1,17},{17,1},{2,18},{18,2},{3,19},{19,3},{4,20},{20... | collective-permute-start | bytes 1769480 | tf_op jit(solution)/shard_map/ppermute | solution.py:21
  32.9 15.3 %collective-permute-start.13 = (f32[1,24,48,128]{3,2,1,0:T(8,128)S(1)}, f32[1,24,48,128]{3,2,1,0:T(8,128)S(1)}, u32[]{:S(2)}, u32[]{:S(2)}) collective-permute-start(f32[1,24,48,128]{3,2,1,0:T(8,128)S(1)} %get-tuple-element.38), channel_id=1, source_target_pairs={{0,1},{1,0},{2,3},{3,2},{4,5},{5,4},{6,7},{7,6},{8,9},{9,8},{10,11... | collective-permute-start | bytes 1769480 | tf_op jit(solution)/shard_map/ppermute | solution.py:21
  33.0 20.5 %collective-permute-start.14 = (f32[1,18,48,128]{3,2,1,0:T(8,128)S(1)}, f32[1,18,48,128]{3,2,1,0:T(8,128)S(1)}, u32[]{:S(2)}, u32[]{:S(2)}) collective-permute-start(f32[1,18,48,128]{3,2,1,0:T(8,128)S(1)} %get-tuple-element.42), channel_id=1, source_target_pairs={{0,16},{16,0},{1,17},{17,1},{2,18},{18,2},{3,19},{19,3},{4,20},{20... | collective-permute-start | bytes 1327112 | tf_op jit(solution)/shard_map/ppermute | solution.py:21
  33.7 6.4 %collective-permute-start.10 = (f32[2,48,128]{2,1,0:T(8,128)S(1)}, f32[2,48,128]{2,1,0:T(8,128)S(1)}, u32[]{:S(2)}, u32[]{:S(2)}) collective-permute-start(f32[2,48,128]{2,1,0:T(8,128)S(1)} %get-tuple-element.35), channel_id=1, source_target_pairs={{0,4},{4,8},{8,12},{12,0},{1,5},{5,9},{9,13},{13,1},{2,6},{6,10},{... | collective-permute-start | bytes 147464 | tf_op jit(solution)/shard_map/ppermute | solution.py:23
  36.3 18.1 %collective-permute-start.15 = (f32[1,6,48,128]{3,2,1,0:T(8,128)S(1)}, f32[1,6,48,128]{3,2,1,0:T(8,128)S(1)}, u32[]{:S(2)}, u32[]{:S(2)}) collective-permute-start(f32[1,6,48,128]{3,2,1,0:T(8,128)S(1)} %get-tuple-element.43), channel_id=1, source_target_pairs={{0,16},{16,0},{1,17},{17,1},{2,18},{18,2},{3,19},{19,3},{4,20},{20... | collective-permute-start | bytes 442376 | tf_op jit(solution)/shard_map/ppermute | solution.py:21
  40.0 4.1 %collective-permute-start.11 = (f32[2,48,128]{2,1,0:T(8,128)S(1)}, f32[2,48,128]{2,1,0:T(8,128)S(1)}, u32[]{:S(2)}, u32[]{:S(2)}) collective-permute-start(f32[2,48,128]{2,1,0:T(8,128)S(1)} %get-tuple-element.36), channel_id=1, source_target_pairs={{0,12},{4,0},{8,4},{12,8},{1,13},{5,1},{9,5},{13,9},{2,14},{6,2},{... | collective-permute-start | bytes 147464 | tf_op jit(solution)/shard_map/ppermute | solution.py:23
  44.1 4.1 %collective-permute-start.12 = (f32[4,24,128]{2,1,0:T(8,128)S(1)}, f32[4,24,128]{2,1,0:T(8,128)S(1)}, u32[]{:S(2)}, u32[]{:S(2)}) collective-permute-start(f32[4,24,128]{2,1,0:T(8,128)S(1)} %get-tuple-element.37), channel_id=1, source_target_pairs={{0,2},{2,0},{1,3},{3,1},{4,6},{6,4},{5,7},{7,5},{8,10},{10,8},{9,1... | collective-permute-start | bytes 147464 | tf_op jit(solution)/shard_map/ppermute | solution.py:21
